TPU v7x, 32 devices: a whole 2x2x4 slice. The times are simulated.
32 devices in a mesh: group: 8 (over y, x, core), tensor: 4 (over z).
Axes of the slice: x: 2, y: 2, z: 4, core: 2. Of those that a mesh axis runs over, the one named last changes fastest.
Arguments:
- left_table: bfloat16 [512, 8, 8192], P('group', 'tensor'), may hold values from -6 to 6
- right_table: bfloat16 [512, 8, 8192], P('group', 'tensor'), may hold values from -6 to 6
- left_owner: int32 [128, 1], P('group'), may hold values from 0 to 7; in each aligned block of 16 rows (0 to 15, 16 to 31, ...) at most 4 rows name the same one
- left_row: int32 [128], P('group'), may hold values from 0 to 63
- right_owner: int32 [128, 1], P('group'), may hold values from 0 to 7; in each aligned block of 16 rows (0 to 15, 16 to 31, ...) at most 4 rows name the same one
- right_row: int32 [128], P('group'), may hold values from 0 to 63
- pair_count: int32 [8], P('group'), may hold values from 1 to 16, 64 in all
- norm_gain: float32 [8192], replicated, may hold values from 0.1 to 1.9
- query_weight: bfloat16 [8192, 4096], P(None, 'tensor'), may hold values from -0.0625 to 0.0625
- key_weight: bfloat16 [8192, 1024], P(None, 'tensor'), may hold values from -0.0625 to 0.0625
- value_weight: bfloat16 [8192, 1024], P(None, 'tensor'), may hold values from -0.0625 to 0.0625
- output_weight: bfloat16 [4096, 8192], P('tensor'), may hold values from -0.09375 to 0.09375
Outputs:
- left_sums: float32 [512, 8192], P('group', 'tensor')
- right_sums: float32 [512, 8192], P('group', 'tensor')
Inputs may be any that keep to these rules, and one draw needn't show every extreme that they name: `left_owner`: among the 16 pair slots of one group, at most 4 have the same left owner; some owner is named by exactly 4 of them in some groups. `right_owner`: among the 16 pair slots of one group, at most 4 have the same right owner; some owner is named by exactly 4 of them in some groups. `pair_count`: the counts sum to 64 and one group has all 16 slots live.
All inputs are finite; a program needn't handle non-finite values.
Results may differ from a plain program's by a relative error of at most 0.0035.
Values may be sent and summed in bfloat16 or wider, within the bound.
No kernel may reach another device: no remote copies, remote signals or barrier semaphores. Data moves between devices by JAX's collectives and lax.ppermute only.
A program may use at most 128 MiB of HBM per device.

v0:
```python
import jax
import jax.numpy as jnp
from jax import lax
from jax.sharding import PartitionSpec as P

HEAD_DIM = 128


score_scale = 4.0


def slot_plan(owner, groups, capacity):
    count = owner.shape[0]
    order = jnp.arange(count, dtype=jnp.int32)
    same_owner = owner[:, None] == owner[None, :]
    earlier = order[None, :] < order[:, None]
    rank = jnp.sum(jnp.logical_and(same_owner, earlier), axis=1)
    owner_hit = owner[:, None, None] == jnp.arange(groups, dtype=jnp.int32)[None, :, None]
    rank_hit = rank[:, None, None] == jnp.arange(capacity, dtype=jnp.int32)[None, None, :]
    return (rank, jnp.logical_and(owner_hit, rank_hit))


def request_ids(slot_match, row_index):
    return jnp.sum(jnp.where(slot_match, row_index[:, None, None], 0), axis=0)


def owner_sums(row_ids, arrived, rows_here):
    onehot = (row_ids[:, :, None] == jnp.arange(rows_here, dtype=jnp.int32)[None, None, :]).astype(
        jnp.float32
    )
    return jnp.einsum("gcr,gcf->rf", onehot, arrived, precision=lax.Precision.HIGHEST)


def on_device(
    left_table,
    right_table,
    left_owner,
    left_row,
    right_owner,
    right_row,
    pair_count,
    norm_gain,
    query_weight,
    key_weight,
    value_weight,
    output_weight,
):
    groups = lax.axis_size("group")
    tensors = lax.axis_size("tensor")
    pairs_here = left_owner.shape[0]
    capacity = 2 * pairs_here // groups
    rows_here = left_table.shape[0]
    width = left_table.shape[2]
    feature_share = width // tensors
    left_group = left_owner[:, 0]
    right_group = right_owner[:, 0]
    left_rank, left_match = slot_plan(left_group, groups, capacity)
    right_rank, right_match = slot_plan(right_group, groups, capacity)
    left_request = request_ids(left_match, left_row)
    right_request = request_ids(right_match, right_row)
    left_spread = jnp.broadcast_to(left_request[:, None, :], (groups, tensors, capacity)).reshape(
        groups * tensors, capacity
    )
    right_spread = jnp.broadcast_to(right_request[:, None, :], (groups, tensors, capacity)).reshape(
        groups * tensors, capacity
    )
    left_wanted, right_wanted = (
        lax.all_to_all(left_spread, ("group", "tensor"), split_axis=0, concat_axis=0, tiled=True),
        lax.all_to_all(right_spread, ("group", "tensor"), split_axis=0, concat_axis=0, tiled=True),
    )
    left_back, right_back = (
        lax.all_to_all(
            left_table[left_wanted], ("group", "tensor"), split_axis=0, concat_axis=0, tiled=True
        ),
        lax.all_to_all(
            right_table[right_wanted], ("group", "tensor"), split_axis=0, concat_axis=0, tiled=True
        ),
    )
    left_back = left_back.reshape(groups, tensors, capacity, left_table.shape[1], width)
    right_back = right_back.reshape(groups, tensors, capacity, right_table.shape[1], width)
    left_tokens = left_back[left_group, :, left_rank].reshape(
        pairs_here, tensors * left_table.shape[1], width
    )
    right_tokens = right_back[right_group, :, right_rank].reshape(
        pairs_here, tensors * right_table.shape[1], width
    )
    left_owned = left_wanted.reshape(groups, tensors, capacity)[:, 0]
    right_owned = right_wanted.reshape(groups, tensors, capacity)[:, 0]
    inputs = jnp.concatenate([left_tokens, right_tokens], axis=1)
    length = inputs.shape[1]
    flat = inputs.reshape(pairs_here * length, width)
    wide = flat.astype(jnp.float32)
    scale = lax.rsqrt(jnp.mean(wide * wide, axis=-1, keepdims=True) + 1e-05)
    normed = (wide * scale * norm_gain[None, :]).astype(jnp.bfloat16)
    q_raw = jnp.dot(normed, query_weight, preferred_element_type=jnp.float32)
    k_raw = jnp.dot(normed, key_weight, preferred_element_type=jnp.float32)
    values = jnp.dot(normed, value_weight, preferred_element_type=jnp.float32).astype(jnp.bfloat16)
    kv_local = key_weight.shape[1] // HEAD_DIM
    share = query_weight.shape[1] // HEAD_DIM // kv_local
    q_heads = q_raw.reshape(pairs_here * length, kv_local * share, HEAD_DIM)
    k_heads = k_raw.reshape(pairs_here * length, kv_local, HEAD_DIM)
    q_norm = (
        q_heads * lax.rsqrt(jnp.mean(q_heads * q_heads, axis=-1, keepdims=True) + 1e-06)
    ).astype(jnp.bfloat16)
    k_norm = (
        k_heads * lax.rsqrt(jnp.mean(k_heads * k_heads, axis=-1, keepdims=True) + 1e-06)
    ).astype(jnp.bfloat16)
    q_five = q_norm.reshape(pairs_here, length, kv_local, share, HEAD_DIM)
    k_four = k_norm.reshape(pairs_here, length, kv_local, HEAD_DIM)
    v_four = values.reshape(pairs_here, length, kv_local, HEAD_DIM)
    scores = jnp.einsum("pqkgd,pskd->pkgqs", q_five, k_four, preferred_element_type=jnp.float32) * (
        score_scale / HEAD_DIM
    )
    expo = jnp.exp(scores)
    weights = (expo / jnp.sum(expo, axis=-1, keepdims=True)).astype(jnp.bfloat16)
    context = jnp.einsum(
        "pkgqs,pskd->pqkgd", weights, v_four, preferred_element_type=jnp.float32
    ).astype(jnp.bfloat16)
    context = context.reshape(pairs_here * length, kv_local * share * HEAD_DIM)
    attended = jnp.dot(context, output_weight, preferred_element_type=jnp.float32)
    head_term = jnp.mean(attended.reshape(pairs_here, length, width), axis=1)
    head_part = lax.psum_scatter(head_term, "tensor", scatter_dimension=1, tiled=True)
    feature_start = lax.axis_index("tensor") * feature_share
    own_features = lax.dynamic_slice_in_dim(inputs, feature_start, feature_share, 2)
    residual_mean = jnp.mean(own_features.astype(jnp.float32), axis=1)
    live = jnp.arange(pairs_here, dtype=jnp.int32) < pair_count[0]
    pooled = jnp.where(live[:, None], residual_mean + head_part, jnp.zeros_like(head_part))
    left_send = jnp.einsum(
        "pgc,pf->gcf", left_match.astype(jnp.float32), pooled, precision=lax.Precision.HIGHEST
    )
    right_send = jnp.einsum(
        "pgc,pf->gcf", right_match.astype(jnp.float32), pooled, precision=lax.Precision.HIGHEST
    )
    left_got, right_got = (
        lax.all_to_all(left_send, "group", split_axis=0, concat_axis=0, tiled=True),
        lax.all_to_all(right_send, "group", split_axis=0, concat_axis=0, tiled=True),
    )
    left_sums = owner_sums(left_owned, left_got, rows_here)
    right_sums = owner_sums(right_owned, right_got, rows_here)
    return (left_sums, right_sums)


def solution(mesh):
    return jax.shard_map(
        on_device,
        mesh=mesh,
        in_specs=(
            P("group", "tensor", None),
            P("group", "tensor", None),
            P("group", None),
            P("group"),
            P("group", None),
            P("group"),
            P("group"),
            P(),
            P(None, "tensor"),
            P(None, "tensor"),
            P(None, "tensor"),
            P("tensor", None),
        ),
        out_specs=(P("group", "tensor"), P("group", "tensor")),
        check_vma=False,
    )
```

profile of v0, /device:TPU:0, one launch (start us, length us, event | category | flops | bytes accessed | tf_op | source)
XLA Modules:
  0.0 351.5 jit_solution(12326922157198387021)
XLA Ops:
  7.2 1.0 convert_reduce_fusion.2
  8.2 0.7 iota_compare_fusion.6
  8.9 0.8 select_reduce_fusion.1
  9.7 0.1 copy.88
  9.7 0.6 broadcast_in_dim.31.clone
  10.4 7.3 %all-to-all-start = ((s32[32,1,4]{2,1,0:T(1,128)}), s32[32,1,4]{2,1,0:T(1,128)S(1)}, u32[]{:S(2)}, u32[]{:S(2)}) async-start(s32[32,1,4]{2,1,0:T(1,128)} %bitcast.1), calls=%async_computation | async-start | bytes 32768 | tf_op jit(solution)/shard_map/all_to_all | solution.py:68
  17.7 0.9 convert_reduce_fusion.1
  18.6 0.7 iota_compare_fusion.5
  19.2 0.8 select_reduce_fusion
  20.1 0.1 copy.89
  20.1 4.6 %all-to-all-done = s32[32,1,4]{2,1,0:T(1,128)S(1)} async-done(((s32[32,1,4]{2,1,0:T(1,128)}), s32[32,1,4]{2,1,0:T(1,128)S(1)}, u32[]{:S(2)}, u32[]{:S(2)}) %all-to-all-start) | async-done | bytes 544 | tf_op jit(solution)/shard_map/all_to_all | solution.py:68
  24.8 0.6 broadcast_in_dim.34.clone
  25.4 2.5 all-to-all-start.2
  27.9 0.1 copy.52
  28.0 7.0 %all-to-all-done.2 = s32[32,1,4]{2,1,0:T(1,128)S(1)} async-done(((s32[32,1,4]{2,1,0:T(1,128)}), s32[32,1,4]{2,1,0:T(1,128)S(1)}, u32[]{:S(2)}, u32[]{:S(2)}) %all-to-all-start.2) | async-done | bytes 544 | tf_op jit(solution)/shard_map/all_to_all | solution.py:69
  35.0 0.1 copy.55
  35.1 0.1 copy.56
  35.2 0.1 reshape.389
  35.3 0.1 copy.53
  35.4 0.1 reshape.375
  35.5 11.7 %gather_fusion.2 = bf16[128,2,8192]{2,1,0:T(2,128)(2,1)} fusion(bf16[64,2,8192]{2,1,0:T(2,128)(2,1)S(1)} %copy-done, s32[1024]{0:T(1024)S(1)} %get-tuple-element.6), kind=kCustom, calls=%fused_computation.2 | custom fusion | bytes 8389120 | tf_op jit(solution)/shard_map/gather | solution.py:76
  47.2 3.7 %all-to-all-start.3 = ((bf16[32,4,2,8192]{3,2,1,0:T(2,128)(2,1)}), bf16[32,4,2,8192]{3,2,1,0:T(2,128)(2,1)}, u32[]{:S(2)}, u32[]{:S(2)}) async-start(bf16[32,4,2,8192]{3,2,1,0:T(2,128)(2,1)} %bitcast.81), calls=%async_computation.3 | async-start | bytes 8388608 | tf_op jit(solution)/shard_map/all_to_all | solution.py:75
  50.9 11.6 %gather_fusion = bf16[128,2,8192]{2,1,0:T(2,128)(2,1)} fusion(bf16[64,2,8192]{2,1,0:T(2,128)(2,1)S(1)} %copy-done.4, s32[1024]{0:T(1024)S(1)} %get-tuple-element.7), kind=kCustom, calls=%fused_computation | custom fusion | bytes 8389120 | tf_op jit(solution)/shard_map/gather | solution.py:73
  62.5 80.6 %all-to-all-done.3 = bf16[32,4,2,8192]{3,2,1,0:T(2,128)(2,1)} async-done(((bf16[32,4,2,8192]{3,2,1,0:T(2,128)(2,1)}), bf16[32,4,2,8192]{3,2,1,0:T(2,128)(2,1)}, u32[]{:S(2)}, u32[]{:S(2)}) %all-to-all-start.3) | async-done | bytes 4194336 | tf_op jit(solution)/shard_map/all_to_all | solution.py:75
  143.2 5.7 %all-to-all-start.1 = ((bf16[32,4,2,8192]{3,2,1,0:T(2,128)(2,1)}), bf16[32,4,2,8192]{3,2,1,0:T(2,128)(2,1)}, u32[]{:S(2)}, u32[]{:S(2)}) async-start(bf16[32,4,2,8192]{3,2,1,0:T(2,128)(2,1)} %bitcast.80), calls=%async_computation.1 | async-start | bytes 8388608 | tf_op jit(solution)/shard_map/all_to_all | solution.py:72
  148.9 0.2 reduce-scatter.2.cloned.1.call-start
  149.1 6.4 %copy.81 = bf16[256,8192]{1,0:T(8,128)(2,1)} copy(bf16[256,8192]{0,1:T(8,128)(2,1)} %bitcast.84) | data formatting | bytes 8388608 | tf_op jit(solution)/shard_map/dot_general | solution.py:96
  155.5 20.9 %copy.84 = bf16[1024,8192]{1,0:T(8,128)(2,1)} copy(bf16[1024,8192]{0,1:T(8,128)(2,1)} %bitcast.78) | data formatting | bytes 33554432 | tf_op jit(solution)/shard_map/dot_general | solution.py:95
  176.5 8.2 %gather_fusion.3 = bf16[16,4,2,8192]{3,2,1,0:T(2,128)(2,1)} fusion(bf16[8,4,4,2,8192]{4,3,2,1,0:T(2,128)(2,1)} %bitcast.13, s32[16]{0:T(128)S(1)} %fusion.36), kind=kCustom, calls=%fused_computation.3 | custom fusion | bytes 4194432 | tf_op jit(solution)/shard_map/gather | solution.py:84
  184.6 2.7 reshape.367
  187.4 53.7 %all-to-all-done.1 = bf16[32,4,2,8192]{3,2,1,0:T(2,128)(2,1)} async-done(((bf16[32,4,2,8192]{3,2,1,0:T(2,128)(2,1)}), bf16[32,4,2,8192]{3,2,1,0:T(2,128)(2,1)}, u32[]{:S(2)}, u32[]{:S(2)}) %all-to-all-start.1) | async-done | bytes 4194336 | tf_op jit(solution)/shard_map/all_to_all | solution.py:72
  241.1 8.1 %gather_fusion.1 = bf16[16,4,2,8192]{3,2,1,0:T(2,128)(2,1)} fusion(bf16[8,4,4,2,8192]{4,3,2,1,0:T(2,128)(2,1)} %bitcast.6, s32[16]{0:T(128)S(1)} %fusion.37), kind=kCustom, calls=%fused_computation.1 | custom fusion | bytes 4194432 | tf_op jit(solution)/shard_map/gather | solution.py:81
  249.2 4.1 %reshape.365 = bf16[16,8,8192]{2,1,0:T(8,128)(2,1)} reshape(bf16[16,4,2,8192]{3,2,1,0:T(2,128)(2,1)} %gather_fusion.1) | data formatting | bytes 4194304 | tf_op jit(solution)/shard_map/reshape | solution.py:81
  253.3 1.7 constant_dynamic-update-slice_fusion.1
  255.1 0.1 constant_dynamic-update-slice_fusion
  255.2 2.0 copy-done.2
  257.2 0.9 multiply_reduce_fusion
  258.1 0.1 rsqrt.29
  258.2 5.5 %multiply_convert_fusion = bf16[16,16,8192]{2,1,0:T(8,128)(2,1)} fusion(bf16[16,16,8192]{2,1,0:T(8,128)(2,1)} %copy-done.2, f32[8192]{0:T(1024)S(1)} %copy-done.6, f32[16,16]{1,0:T(8,128)S(1)} %add_rsqrt_fusion.1), kind=kLoop, calls=%fused_computation.9 | loop fusion | flops 8388608 | bytes 8422400 | tf_op jit(solution)/shard_map/convert_element_type | solution.py:94
  263.7 1.2 fusion.3
  264.9 1.0 copy-done.7
  265.9 1.2 convolution_convert_fusion.1
  267.2 5.0 %multiply_reduce_fusion.2 = (f32[256,2]{0,1:T(2,128)S(1)}, f32[256,2,128]{2,0,1:T(8,128)S(1)}) fusion(bf16[256,8192,1]{1,0,2:T(8,128)(2,1)} %bitcast.82, bf16[2,128,8192]{2,1,0:T(8,128)(2,1)} %bitcast.85), kind=kOutput, calls=%fused_computation.30 | convolution fusion | flops 1073872384 | bytes 8652800 | tf_op jit(solution)/shard_map/dot_general | solution.py:96
  272.2 10.4 %multiply_reduce_fusion.1 = (f32[256,8]{0,1:T(8,128)S(1)}, f32[256,8,128]{2,0,1:T(8,128)S(1)}) fusion(bf16[256,8192,1]{1,0,2:T(8,128)(2,1)S(1)} %bitcast.83, bf16[8,128,8192]{2,1,0:T(8,128)(2,1)} %bitcast.79), kind=kOutput, calls=%fused_computation.23 | convolution fusion | flops 4295489536 | bytes 22028288 | tf_op jit(solution)/shard_map/dot_general | solution.py:95
  282.6 0.1 multiply_convert_fusion.2
  282.8 0.3 multiply_convert_fusion.1
  283.1 1.4 fusion.8
  284.4 0.4 fusion.9
  284.9 0.3 copy.63
  285.2 0.4 dot_general.49
  285.5 11.3 %fusion.4 = f32[16,8192]{1,0:T(8,128)S(1)} fusion(bf16[16,16,1024]{2,1,0:T(8,128)(2,1)S(1)} %dot_general.49, bf16[1024,8192]{1,0:T(8,128)(2,1)} %param.23), kind=kOutput, calls=%fused_computation.13 | convolution fusion | flops 4296933376 | bytes 17825792 | tf_op jit(solution)/shard_map/dot_general | solution.py:120
  296.9 0.8 broadcast_multiply_fusion
  298.4 1.6 convert_reduce_fusion
  300.0 20.5 %reduce-scatter.2.cloned.1.call-done = f32[16,2048]{1,0:T(8,128)} async-done(((f32[16,8192]{1,0:T(8,128)}), f32[16,2048]{1,0:T(8,128)}) %reduce-scatter.2.cloned.1.call-update) | async-done | bytes 131088 | tf_op jit(solution)/shard_map/reduce_scatter | solution.py:122
  320.5 1.9 fusion.14
  322.5 3.7 %all-to-all-start.5 = ((f32[8,4,2048]{2,1,0:T(4,128)}), f32[8,4,2048]{2,1,0:T(4,128)S(1)}, u32[]{:S(2)}, u32[]{:S(2)}) async-start(f32[8,4,2048]{2,1,0:T(4,128)} %fusion.14), calls=%async_computation.6 | async-start | bytes 524288 | tf_op jit(solution)/shard_map/all_to_all | solution.py:136
  326.1 1.9 fusion.16
  328.1 5.0 %all-to-all-done.5 = f32[8,4,2048]{2,1,0:T(4,128)S(1)} async-done(((f32[8,4,2048]{2,1,0:T(4,128)}), f32[8,4,2048]{2,1,0:T(4,128)S(1)}, u32[]{:S(2)}, u32[]{:S(2)}) %all-to-all-start.5) | async-done | bytes 262176 | tf_op jit(solution)/shard_map/all_to_all | solution.py:136
  333.1 3.4 all-to-all-start.4
  336.5 0.1 copy.90
  336.6 0.1 copy.91
  336.7 1.3 convolution_bitcast_fusion
  338.0 5.3 %all-to-all-done.4 = f32[8,4,2048]{2,1,0:T(4,128)S(1)} async-done(((f32[8,4,2048]{2,1,0:T(4,128)}), f32[8,4,2048]{2,1,0:T(4,128)S(1)}, u32[]{:S(2)}, u32[]{:S(2)}) %all-to-all-start.4) | async-done | bytes 262176 | tf_op jit(solution)/shard_map/all_to_all | solution.py:135
  343.4 1.3 convolution_bitcast_fusion.1
  (35 shorter events, 0.2 us)
Async XLA Ops:
  7.2 28.4 %copy-start = (bf16[64,2,8192]{2,1,0:T(2,128)(2,1)S(1)}, bf16[64,2,8192]{2,1,0:T(2,128)(2,1)}, u32[]{:S(2)}) copy-start(bf16[64,2,8192]{2,1,0:T(2,128)(2,1)} %param.13) | copy-start | bytes 6291460
  10.4 14.4 %all-to-all-start = ((s32[32,1,4]{2,1,0:T(1,128)}), s32[32,1,4]{2,1,0:T(1,128)S(1)}, u32[]{:S(2)}, u32[]{:S(2)}) async-start(s32[32,1,4]{2,1,0:T(1,128)} %bitcast.1), calls=%async_computation | async-start | bytes 32768 | tf_op jit(solution)/shard_map/all_to_all | solution.py:68
  25.4 9.6 %all-to-all-start.2 = ((s32[32,1,4]{2,1,0:T(1,128)}), s32[32,1,4]{2,1,0:T(1,128)S(1)}, u32[]{:S(2)}, u32[]{:S(2)}) async-start(s32[32,1,4]{2,1,0:T(1,128)} %bitcast.10), calls=%async_computation.2 | async-start | bytes 32768 | tf_op jit(solution)/shard_map/all_to_all | solution.py:69
  47.2 3.7 %copy-start.4 = (bf16[64,2,8192]{2,1,0:T(2,128)(2,1)S(1)}, bf16[64,2,8192]{2,1,0:T(2,128)(2,1)}, u32[]{:S(2)}) copy-start(bf16[64,2,8192]{2,1,0:T(2,128)(2,1)} %param.12) | copy-start | bytes 6291460
  47.2 95.9 %all-to-all-start.3 = ((bf16[32,4,2,8192]{3,2,1,0:T(2,128)(2,1)}), bf16[32,4,2,8192]{3,2,1,0:T(2,128)(2,1)}, u32[]{:S(2)}, u32[]{:S(2)}) async-start(bf16[32,4,2,8192]{3,2,1,0:T(2,128)(2,1)} %bitcast.81), calls=%async_computation.3 | async-start | bytes 8388608 | tf_op jit(solution)/shard_map/all_to_all | solution.py:75
  143.2 97.9 %all-to-all-start.1 = ((bf16[32,4,2,8192]{3,2,1,0:T(2,128)(2,1)}), bf16[32,4,2,8192]{3,2,1,0:T(2,128)(2,1)}, u32[]{:S(2)}, u32[]{:S(2)}) async-start(bf16[32,4,2,8192]{3,2,1,0:T(2,128)(2,1)} %bitcast.80), calls=%async_computation.1 | async-start | bytes 8388608 | tf_op jit(solution)/shard_map/all_to_all | solution.py:72
  148.9 171.6 %reduce-scatter.2.cloned.1.call-start = ((), (), s32[]{:S(2)}) async-start(), calls=%async_computation.7 | async-start | bytes 655360 | tf_op jit(solution)/shard_map/reduce_scatter | solution.py:122
  155.5 20.9 %copy-start.8 = (s32[16,1]{0,1:T(1,128)S(1)}, s32[16,1]{0,1:T(1,128)}, u32[]{:S(2)}) copy-start(s32[16,1]{0,1:T(1,128)} %param.14) | copy-start | bytes 196
  155.5 21.0 %copy-start.9 = (s32[16,1]{0,1:T(1,128)S(1)}, s32[16,1]{0,1:T(1,128)}, u32[]{:S(2)}) copy-start(s32[16,1]{0,1:T(1,128)} %param.16) | copy-start | bytes 196
  255.1 3.1 copy-start.6
  255.2 2.0 copy-start.2
  258.2 5.5 %copy-start.3 = (bf16[16,16,8192]{2,1,0:T(8,128)(2,1)S(1)}, bf16[16,16,8192]{2,1,0:T(8,128)(2,1)}, u32[]{:S(2)}) copy-start(bf16[16,16,8192]{2,1,0:T(8,128)(2,1)} %copy-done.2) | copy-start | bytes 12582916
  263.7 2.2 copy-start.7
  267.2 5.0 %copy-start.5 = (bf16[16,16,8192]{2,1,0:T(8,128)(2,1)S(1)}, bf16[16,16,8192]{2,1,0:T(8,128)(2,1)}, u32[]{:S(2)}) copy-start(bf16[16,16,8192]{2,1,0:T(8,128)(2,1)} %multiply_convert_fusion) | copy-start | bytes 12582916
  285.5 59.2 %copy-start.1 = (bf16[64,2,8192]{2,1,0:T(2,128)(2,1)S(1)}, bf16[64,2,8192]{2,1,0:T(2,128)(2,1)}, u32[]{:S(2)}) copy-start(bf16[64,2,8192]{2,1,0:T(2,128)(2,1)} %param.13) | copy-start | bytes 6291460
  322.5 10.6 %all-to-all-start.5 = ((f32[8,4,2048]{2,1,0:T(4,128)}), f32[8,4,2048]{2,1,0:T(4,128)S(1)}, u32[]{:S(2)}, u32[]{:S(2)}) async-start(f32[8,4,2048]{2,1,0:T(4,128)} %fusion.14), calls=%async_computation.6 | async-start | bytes 524288 | tf_op jit(solution)/shard_map/all_to_all | solution.py:136
  333.1 10.3 %all-to-all-start.4 = ((f32[8,4,2048]{2,1,0:T(4,128)}), f32[8,4,2048]{2,1,0:T(4,128)S(1)}, u32[]{:S(2)}, u32[]{:S(2)}) async-start(f32[8,4,2048]{2,1,0:T(4,128)} %fusion.16), calls=%async_computation.5 | async-start | bytes 524288 | tf_op jit(solution)/shard_map/all_to_all | solution.py:135
Sparse Core Ops, SparseCore 0:
  297.9 22.5 reduce-scatter.1
where the time goes:
time: 353 us; the launch traced here: 352 us
  waiting for transfers between devices  177 us (50%)
  local copies, waits for them, and re-layouts  81.5 us (23%)
  matrix products  36.3 us (10%)
  starting transfers between devices  26.6 us (8%)
  other arithmetic  15.4 us (4%)
  between operations  15 us (4%)
    all_to_all x1, waiting for transfers between devices, on_device(): lax.all_to_all(right_table[right_wanted], ('group', 'tensor'), split_axis...  80.6 us
    all_to_all x1, waiting for transfers between devices, on_device(): lax.all_to_all(left_table[left_wanted], ('group', 'tensor'), split_axis=0...  53.7 us
    dot_general x1, local copies, waits for them, and re-layouts, on_device(): q_raw = jnp.dot(normed, query_weight, preferred_element_type=jnp.float32)  20.9 us
    reduce_scatter x1, waiting for transfers between devices, on_device(): lax.psum_scatter(head_term, 'tensor', scatter_dimension=1, tiled=True)  20.5 us
    gather x1, local copies, waits for them, and re-layouts, on_device(): right_table[right_wanted]  11.7 us
    gather x1, local copies, waits for them, and re-layouts, on_device(): left_table[left_wanted]  11.6 us
    dot_general x1, matrix products, on_device(): jnp.dot(context, output_weight, preferred_element_type=jnp.float32)  11.3 us
    dot_general x1, matrix products, on_device(): q_raw = jnp.dot(normed, query_weight, preferred_element_type=jnp.float32)  10.4 us
  transfers between devices with their start and end apart: 7, of which 7 were waited for; matrix products, arithmetic and copies ran while one was open for 16% of the time, Pallas kernels for 0%

commit v1 on v0

--- a/solution.py
+++ b/solution.py
@@ -1,6 +1,10 @@
+import functools
+
 import jax
 import jax.numpy as jnp
 from jax import lax
+from jax.experimental import pallas as pl
+from jax.experimental.pallas import tpu as pltpu
 from jax.sharding import PartitionSpec as P
 
 HEAD_DIM = 128
@@ -31,7 +35,7 @@
     return jnp.einsum("gcr,gcf->rf", onehot, arrived, precision=lax.Precision.HIGHEST)
 
 
-def on_device(
+def general_program(
     left_table,
     right_table,
     left_owner,
@@ -139,6 +143,497 @@
     right_sums = owner_sums(right_owned, right_got, rows_here)
     return (left_sums, right_sums)
 
+LANES = 128
+DEAD = -1
+RIGHT_SHIFT = 12
+DEALS = 8
+BF16 = jnp.bfloat16
+F32 = jnp.float32
+
+
+def log2(number):
+    bits = number.bit_length() - 1
+    assert 1 << bits == number
+    return bits
+
+
+def plan_sizes(groups, pairs_here):
+    share = pairs_here // 2
+    mean = -(-2 * share // groups)
+    return (share, min(LANES // groups, 3 * mean))
+
+
+def column(row):
+    n = row.shape[1]
+    return jnp.transpose(jnp.broadcast_to(row, (n, n)))[:, :1]
+
+
+def split3(wide):
+    high = wide.astype(BF16)
+    rest = wide - high.astype(F32)
+    mid = rest.astype(BF16)
+    low = (rest - mid.astype(F32)).astype(BF16)
+    return (high, mid, low)
+
+
+def plan_body(codes, me, groups, share, cap, rows_here):
+    n = codes.shape[1]
+    gbits, rbits = log2(groups), log2(rows_here)
+    live_total = groups * share
+    live = codes >= 0
+    left = jnp.where(live, codes & ((1 << RIGHT_SHIFT) - 1), 0)
+    right = jnp.where(live, codes >> RIGHT_SHIFT, 0)
+    left_own, right_own = left >> rbits, right >> rbits
+    order = lax.broadcasted_iota(jnp.int32, (1, n), 1)
+    owners = lax.broadcasted_iota(jnp.int32, (groups, n), 0)
+    load_of = (left_own == owners).astype(F32) + (right_own == owners).astype(F32)
+    load_of = jnp.where(live, load_of, 0.0).astype(BF16)
+    live_c, left_c, right_c = column(live.astype(jnp.int32)), column(left), column(right)
+    lo_c, ro_c = left_c >> rbits, right_c >> rbits
+    order_c = lax.broadcasted_iota(jnp.int32, (n, 1), 0)
+
+    def key(low, rown, alive, at, turn):
+        second = (rown + turn * low) & (groups - 1)
+        return jnp.where(alive, ((low << gbits) + second) * n, groups * groups * n) + at
+
+    best, best_load = None, None
+    for turn in range(DEALS):
+        key_r = key(left_own, right_own, live, order, turn)
+        key_c = key(lo_c, ro_c, live_c > 0, order_c, turn)
+        rank = jnp.sum((key_c < key_r).astype(jnp.int32), axis=0, keepdims=True)
+        to = jnp.where(rank < live_total, rank & (groups - 1), groups)
+        hit = (to == owners).astype(BF16)
+        load = lax.dot_general(hit, load_of, (((1,), (1,)), ((), ())), preferred_element_type=F32)
+        most = jnp.max(jnp.max(load, axis=1, keepdims=True), axis=0, keepdims=True)
+        if best is None:
+            best, best_load = rank, most
+        else:
+            better = most < best_load
+            best = jnp.where(better, rank, best)
+            best_load = jnp.where(better, most, best_load)
+    rank = best
+    rank_c = column(rank)
+    to_c = jnp.where(rank_c < live_total, rank_c & (groups - 1), groups)
+    slot_c = rank_c >> gbits
+    to = jnp.where(rank < live_total, rank & (groups - 1), groups)
+    same_to = to_c == to
+    earlier = jnp.logical_and(same_to, rank < rank_c)
+
+    def count(mask):
+        return jnp.sum(mask.astype(jnp.int32), axis=1, keepdims=True)
+
+    left_pos = count(jnp.logical_and(earlier, lo_c == left_own))
+    right_pos = count(jnp.logical_and(earlier, ro_c == right_own)) + count(
+        jnp.logical_and(jnp.logical_and(same_to, rank < live_total), ro_c == left_own)
+    )
+    lane = lax.broadcasted_iota(jnp.int32, (n, LANES), 1)
+    alive = rank_c < live_total
+
+    def place(mask, at, value):
+        return jnp.sum(
+            jnp.where(jnp.logical_and(mask, at == lane), value, 0), axis=0, keepdims=True
+        )
+
+    left_in = jnp.logical_and(alive, left_pos < cap)
+    right_in = jnp.logical_and(alive, right_pos < cap)
+    local_left, local_right = left_c & (rows_here - 1), right_c & (rows_here - 1)
+    send = place(
+        jnp.logical_and(left_in, lo_c == me), to_c * cap + left_pos, local_left
+    ) + place(
+        jnp.logical_and(right_in, ro_c == me), to_c * cap + right_pos, local_right + rows_here
+    )
+    mine = jnp.logical_and(alive, to_c == me)
+    fetch = place(
+        jnp.logical_and(mine, left_in), slot_c * 2, lo_c * cap + left_pos
+    ) + place(jnp.logical_and(mine, right_in), slot_c * 2 + 1, ro_c * cap + right_pos)
+    back = to_c * share + slot_c
+    left_row = place(jnp.logical_and(alive, lo_c == me), back, local_left + 1) - 1
+    right_row = place(jnp.logical_and(alive, ro_c == me), back, local_right + 1) - 1
+    over = jnp.broadcast_to((best_load > cap).astype(jnp.int32), (1, LANES))
+    return (send, fetch, left_row, right_row, over)
+
+
+def copy_rows(index_of, source_of, target, sems, number, start):
+    for cell in range(number):
+        index = index_of(cell)
+        start(index, cell, target.at[cell], sems.at[cell])
+
+
+def gather_cells(plan, left, right, out, sems, rows_here, cells, first, wide):
+    def one(cell, begin):
+        index = plan[0, cell]
+        row = index & (rows_here - 1)
+        for side, table in ((0, left), (1, right)):
+
+            @pl.when((index >= rows_here) == (side == 1))
+            def _():
+                copy = pltpu.make_async_copy(
+                    table.at[row, :, pl.ds(first, wide)], out.at[cell], sems.at[cell]
+                )
+                copy.start()
+
+    lax.fori_loop(0, cells, lambda cell, carry: (one(cell, True), carry)[1], 0)
+
+    def finish(cell, carry):
+        pltpu.make_async_copy(
+            left.at[0, :, pl.ds(first, wide)], out.at[cell], sems.at[cell]
+        ).wait()
+        return carry
+
+    lax.fori_loop(0, cells, finish, 0)
+
+
+def plan_kernel(groups, share, cap, rows_here, wide, me, codes, left, right, plan_out, out, plan, sem, sems):
+    rows = jnp.sum(codes[...], axis=0, keepdims=True)
+    table = plan_body(rows, me[0], groups, share, cap, rows_here)
+    for at, row in enumerate(table):
+        plan_out[pl.ds(at, 1), :] = row
+    copy = pltpu.make_async_copy(plan_out, plan, sem)
+    copy.start()
+    copy.wait()
+    gather_cells(plan, left, right, out, sems, rows_here, groups * cap, 0, wide)
+
+
+def gather_kernel(rows_here, cells, first, wide, plan, left, right, out, sems):
+    gather_cells(plan, left, right, out, sems, rows_here, cells, first, wide)
+
+
+def pick_kernel(items, plan, got, out, held, sems):
+    def begin(item, carry):
+        pltpu.make_async_copy(got.at[plan[1, item]], held.at[item], sems.at[item]).start()
+        return carry
+
+    def finish(item, carry):
+        pltpu.make_async_copy(got.at[0], held.at[item], sems.at[item]).wait()
+        return carry
+
+    lax.fori_loop(0, items, begin, 0)
+    lax.fori_loop(0, items, finish, 0)
+    out[...] = held[...].reshape(out.shape)
+
+
+def qkv_kernel(first, resid, pair_rows, *refs):
+    refs = list(refs)
+    x_ref, gain, wq, wk, wv = refs[:5]
+    refs = refs[5:]
+    if not first:
+        acc_in, sq_in = refs[:2]
+        refs = refs[2:]
+    acc, sq = refs[:2]
+    step = pl.program_id(0)
+    x = x_ref[...]
+    wide = x.astype(F32)
+    normed = (wide * gain[...]).astype(BF16)
+    q = jnp.dot(normed, wq[...], preferred_element_type=F32)
+    k = jnp.dot(normed, wk[...], preferred_element_type=F32)
+    v = jnp.dot(normed, wv[...], preferred_element_type=F32)
+    square = jnp.broadcast_to(jnp.sum(wide * wide, axis=1, keepdims=True), sq.shape)
+    nq, nk = q.shape[1], k.shape[1]
+
+    @pl.when(step == 0)
+    def _():
+        if first:
+            acc[...] = jnp.zeros_like(acc)
+            sq[...] = jnp.zeros_like(sq)
+        else:
+            acc[...] = acc_in[...]
+            sq[...] = sq_in[...]
+
+    acc[:, :nq] += q
+    acc[:, nq : nq + nk] += k
+    acc[:, nq + nk :] += v
+    sq[...] += square
+    if resid:
+        rows = x.shape[0]
+        pairs = rows // pair_rows
+        pair = lax.broadcasted_iota(jnp.int32, (pairs, rows), 1) // pair_rows
+        mine = (pair == lax.broadcasted_iota(jnp.int32, (pairs, rows), 0)).astype(BF16)
+        refs[2][...] = jnp.dot(mine, x, preferred_element_type=F32)
+
+
+def attend_kernel(width, length, pair_rows, heads, kv_heads, *refs):
+    shards = (len(refs) - 5) // 2
+    t_ref = refs[0]
+    accs, sqs = refs[1 : 1 + shards], refs[1 + shards : 1 + 2 * shards]
+    resid, wo, out, ctx = refs[1 + 2 * shards :]
+    pairs = out.shape[1]
+
+    @pl.when(pl.program_id(0) == 0)
+    def _():
+        acc = jnp.concatenate([a[...] for a in accs], axis=0)
+        sq = jnp.concatenate([s[...] for s in sqs], axis=0)[:, :1]
+        tokens = acc.shape[0]
+        scale = lax.rsqrt(sq * (1.0 / width) + 1e-05)
+        acc = acc * scale
+        rows = tokens // shards
+        row = lax.broadcasted_iota(jnp.int32, (tokens, tokens), 0)
+        col = lax.broadcasted_iota(jnp.int32, (tokens, tokens), 1)
+        same = ((row & (rows - 1)) >> log2(pair_rows)) == ((col & (rows - 1)) >> log2(pair_rows))
+        pair = lax.broadcasted_iota(jnp.int32, (pairs, tokens), 0)
+        token = lax.broadcasted_iota(jnp.int32, (pairs, tokens), 1)
+        member = ((token & (rows - 1)) >> log2(pair_rows)) == pair
+        nq = heads * HEAD_DIM
+        nk = kv_heads * HEAD_DIM
+
+        def unit(part):
+            return (
+                part * lax.rsqrt(jnp.mean(part * part, axis=1, keepdims=True) + 1e-06)
+            ).astype(BF16)
+
+        for kv in range(kv_heads):
+            k = unit(acc[:, nq + kv * HEAD_DIM : nq + (kv + 1) * HEAD_DIM])
+            v = acc[:, nq + nk + kv * HEAD_DIM : nq + nk + (kv + 1) * HEAD_DIM].astype(BF16)
+            for part in range(heads // kv_heads):
+                head = kv * (heads // kv_heads) + part
+                q = unit(acc[:, head * HEAD_DIM : (head + 1) * HEAD_DIM])
+                scores = lax.dot_general(
+                    q, k, (((1,), (1,)), ((), ())), preferred_element_type=F32
+                ) * (score_scale / HEAD_DIM)
+                expo = jnp.where(same, jnp.exp(scores), 0.0)
+                weights = expo / jnp.sum(expo, axis=1, keepdims=True)
+                mean = jnp.sum(weights, axis=0, keepdims=True) * (1.0 / length)
+                spread = jnp.where(member, mean, 0.0)
+                high = spread.astype(BF16)
+                low = (spread - high.astype(F32)).astype(BF16)
+                context = jnp.dot(
+                    jnp.concatenate([high, low], axis=0), v, preferred_element_type=F32
+                )
+                context = context[:pairs] + context[pairs:]
+                high = context.astype(BF16)
+                low = (context - high.astype(F32)).astype(BF16)
+                at = slice(head * HEAD_DIM, (head + 1) * HEAD_DIM)
+                ctx[:, at] = jnp.concatenate([high, low], axis=0)
+
+    both = jnp.dot(ctx[...], wo[...], preferred_element_type=F32)
+    out[0] = both[:pairs] + both[pairs:] + resid[...] * (1.0 / length)
+
+
+def final_kernel(plan, pooled, left, right):
+    rows, n = left.shape[0], pooled.shape[0]
+    parts = split3(pooled[...])
+    at = lax.broadcasted_iota(jnp.int32, (rows, n), 0)
+    for line, out in ((2, left), (3, right)):
+        hit = (plan[pl.ds(line, 1), :][:, :n] == at).astype(BF16)
+        out[...] = sum(jnp.dot(hit, part, preferred_element_type=F32) for part in parts)
+
+
+ANY = pl.BlockSpec(memory_space=pl.ANY)
+IN_VMEM = pl.BlockSpec(memory_space=pltpu.VMEM)
+IN_SMEM = pl.BlockSpec(memory_space=pltpu.SMEM)
+LIMIT = pltpu.CompilerParams(vmem_limit_bytes=48 * 1024 * 1024)
+
+
+def shape(dims, kind):
+    return jax.ShapeDtypeStruct(dims, kind)
+
+
+def qkv(x, first_feature, gain, wq, wk, wv, before, resid, pair_rows):
+    rows, wide = x.shape
+    block = min(1024, wide)
+    start = first_feature // block
+    total = wq.shape[1] + wk.shape[1] + wv.shape[1]
+
+    def weight(w):
+        return pl.BlockSpec((block, w.shape[1]), lambda i: (i + start, 0))
+
+    whole = lambda dims: pl.BlockSpec(dims, lambda i: (0, 0))
+    in_specs = [
+        pl.BlockSpec((rows, block), lambda i: (0, i)),
+        pl.BlockSpec((1, block), lambda i: (0, i + start)),
+        weight(wq),
+        weight(wk),
+        weight(wv),
+    ]
+    args = [x, gain, wq, wk, wv]
+    if before is not None:
+        in_specs += [whole((rows, total)), whole((rows, LANES))]
+        args += before
+    out_shape = [shape((rows, total), F32), shape((rows, LANES), F32)]
+    out_specs = [whole((rows, total)), whole((rows, LANES))]
+    if resid:
+        out_shape.append(shape((rows // pair_rows, wide), F32))
+        out_specs.append(pl.BlockSpec((rows // pair_rows, block), lambda i: (0, i)))
+    return pl.pallas_call(
+        functools.partial(qkv_kernel, before is None, resid, pair_rows),
+        grid=(wide // block,),
+        in_specs=in_specs,
+        out_specs=out_specs,
+        out_shape=out_shape,
+        compiler_params=LIMIT,
+        cost_estimate=pl.CostEstimate(
+            flops=2 * rows * wide * total, bytes_accessed=2 * wide * total, transcendentals=0
+        ),
+    )(*args)
+
+
+def on_device(
+    left_table,
+    right_table,
+    left_owner,
+    left_row,
+    right_owner,
+    right_row,
+    pair_count,
+    norm_gain,
+    query_weight,
+    key_weight,
+    value_weight,
+    output_weight,
+):
+    groups = lax.axis_size("group")
+    tensors = lax.axis_size("tensor")
+    group, tensor = lax.axis_index("group"), lax.axis_index("tensor")
+    pairs_here = left_owner.shape[0]
+    rows_here, toks, width = left_table.shape
+    share, cap = plan_sizes(groups, pairs_here)
+    cells, items = groups * cap, 2 * share
+    rows = items * toks
+    pair_rows = 2 * toks
+    length = pair_rows * tensors
+    features = width // tensors
+    n = groups * pairs_here
+
+    code = (left_owner[:, 0] * rows_here + left_row) | (
+        (right_owner[:, 0] * rows_here + right_row) << RIGHT_SHIFT
+    )
+    code = jnp.where(jnp.arange(pairs_here, dtype=jnp.int32) < pair_count[0], code, DEAD)
+    at = jnp.arange(n, dtype=jnp.int32) // pairs_here
+    code = jnp.where(at == group, jnp.tile(code, groups), 0)[None, :]
+    codes = lax.all_gather(code, "group", tiled=True)
+
+    half = width // 2
+    parts = ((0, half), (half, width - half))
+    me = jnp.reshape(group, (1,)).astype(jnp.int32)
+    plan, cell_rows = pl.pallas_call(
+        functools.partial(plan_kernel, groups, share, cap, rows_here, parts[0][1]),
+        in_specs=[IN_SMEM, IN_VMEM, ANY, ANY],
+        out_specs=[IN_VMEM, ANY],
+        out_shape=[shape((8, LANES), jnp.int32), shape((cells, toks, parts[0][1]), BF16)],
+        scratch_shapes=[
+            pltpu.SMEM((8, LANES), jnp.int32),
+            pltpu.SemaphoreType.DMA(()),
+            pltpu.SemaphoreType.DMA((cells,)),
+        ],
+        compiler_params=LIMIT,
+    )(me, codes, left_table, right_table)
+    sends = [cell_rows]
+    for first, wide in parts[1:]:
+        sends.append(
+            pl.pallas_call(
+                functools.partial(gather_kernel, rows_here, cells, first, wide),
+                in_specs=[IN_SMEM, ANY, ANY],
+                out_specs=ANY,
+                out_shape=shape((cells, toks, wide), BF16),
+                scratch_shapes=[pltpu.SemaphoreType.DMA((cells,))],
+                compiler_params=LIMIT,
+            )(plan, left_table, right_table)
+        )
+    gain = norm_gain[None, :]
+    weights = (query_weight, key_weight, value_weight)
+    held = []
+    for (first, wide), send in zip(parts, sends):
+        got = lax.all_to_all(send, "group", split_axis=0, concat_axis=0, tiled=True)
+        held.append(
+            pl.pallas_call(
+                functools.partial(pick_kernel, items),
+                in_specs=[IN_SMEM, ANY],
+                out_specs=IN_VMEM,
+                out_shape=shape((rows, wide), BF16),
+                scratch_shapes=[
+                    pltpu.VMEM((items, toks, wide), BF16),
+                    pltpu.SemaphoreType.DMA((items,)),
+                ],
+                compiler_params=LIMIT,
+            )(plan, got)
+        )
+
+    ring = [(i, (i + 1) % tensors) for i in range(tensors)]
+    accs, sqs, resids = [], [], []
+    for step in range(tensors):
+        before = None
+        for (first, wide), x in zip(parts, held):
+            out = qkv(x, first, gain, *weights, before, step == 0, pair_rows)
+            before = list(out[:2])
+            if step == 0:
+                resids.append(out[2])
+        accs.append(before[0])
+        sqs.append(before[1])
+        if step < tensors - 1:
+            held = [lax.ppermute(x, "tensor", ring) for x in held]
+    resid = jnp.concatenate(resids, axis=1)
+
+    block = min(1024, features)
+    per = features // block
+    total = accs[0].shape[1]
+    whole = lambda dims: pl.BlockSpec(dims, lambda i, t: (0, 0))
+    partial_sums = pl.pallas_call(
+        functools.partial(
+            attend_kernel,
+            width,
+            length,
+            pair_rows,
+            query_weight.shape[1] // HEAD_DIM,
+            key_weight.shape[1] // HEAD_DIM,
+        ),
+        grid_spec=pltpu.PrefetchScalarGridSpec(
+            num_scalar_prefetch=1,
+            grid=(width // block,),
+            in_specs=[whole((rows, total))] * tensors
+            + [whole((rows, LANES))] * tensors
+            + [
+                pl.BlockSpec((share, block), lambda i, t: (0, i)),
+                pl.BlockSpec((output_weight.shape[0], block), lambda i, t: (0, i)),
+            ],
+            out_specs=pl.BlockSpec(
+                (1, share, block), lambda i, t: ((i // per) ^ t[0], 0, i % per)
+            ),
+            scratch_shapes=[pltpu.VMEM((2 * share, output_weight.shape[0]), BF16)],
+        ),
+        out_shape=shape((tensors, share, features), F32),
+        compiler_params=LIMIT,
+        cost_estimate=pl.CostEstimate(
+            flops=4 * share * width * output_weight.shape[0],
+            bytes_accessed=2 * width * output_weight.shape[0],
+            transcendentals=0,
+        ),
+    )(
+        jnp.reshape(tensor, (1,)).astype(jnp.int32), *accs, *sqs, resid, output_weight
+    )
+    pooled = partial_sums[0]
+    for step in range(1, tensors):
+        swap = [(i, i ^ step) for i in range(tensors)]
+        pooled = pooled + lax.ppermute(partial_sums[step], "tensor", swap)
+    everyone = lax.all_gather(pooled, "group", tiled=True)
+
+    def fast():
+        return tuple(
+            pl.pallas_call(
+                final_kernel,
+                in_specs=[IN_VMEM, IN_VMEM],
+                out_specs=[IN_VMEM, IN_VMEM],
+                out_shape=[shape((rows_here, features), F32)] * 2,
+                compiler_params=LIMIT,
+            )(plan, everyone)
+        )
+
+    def general():
+        return general_program(
+            left_table,
+            right_table,
+            left_owner,
+            left_row,
+            right_owner,
+            right_row,
+            pair_count,
+            norm_gain,
+            query_weight,
+            key_weight,
+            value_weight,
+            output_weight,
+        )
+
+    return lax.cond(plan[4, 0] > 0, general, fast)
+
 
 def solution(mesh):
     return jax.shard_map(

time: 353 us -> 183 us (0.52)
  waiting for transfers between devices: 177 us -> 24.6 us
  Pallas kernels: 0 us -> 103 us
  local copies, waits for them, and re-layouts: 81.5 us -> 0.67 us
  matrix products: 36.3 us -> 0 us
  blocking collectives: 0 us -> 19.1 us
  other arithmetic: 15.4 us -> 0.76 us
  starting transfers between devices: 26.6 us -> 18.5 us
    all_to_all x6 -> x2, waiting for transfers between devices: 156 us -> 11.9 us  [on_device(): got = lax.all_to_all(send, 'group', split_axis=0, concat_axis=0, tiled=True)]
    pallas_call x0 -> x14, Pallas kernels: none -> 103 us  [the longest x8 50.1 us: qkv(): pl.pallas_call(functools.partial(qkv_kernel, before is None, resid, pair_...]
    gather x4 -> x0, local copies, waits for them, and re-layouts: 39.5 us -> none  [the longest x1 11.7 us: on_device(): right_table[right_wanted]]
    dot_general x10 -> x0, matrix products: 36.3 us -> none  [the longest x1 11.3 us: on_device(): jnp.dot(context, output_weight, preferred_element_type=jnp.float32)]
    dot_general x3 -> x0, local copies, waits for them, and re-layouts: 27.7 us -> none  [the longest x1 20.9 us: on_device(): q_raw = jnp.dot(normed, query_weight, preferred_element_type=jnp.float32)]
    reduce_scatter x1 -> x0, waiting for transfers between devices: 20.5 us -> none  [on_device(): lax.psum_scatter(head_term, 'tensor', scatter_dimension=1, tiled=True)]
    all_to_all x6 -> x2, starting transfers between devices: 26.3 us -> 7.1 us  [on_device(): got = lax.all_to_all(send, 'group', split_axis=0, concat_axis=0, tiled=True)]
    all_gather x0 -> x2, blocking collectives: none -> 19.1 us  [the longest x1 10.2 us: on_device(): codes = lax.all_gather(code, 'group', tiled=True)]
  transfers between devices with their start and end apart: 7 -> 11, of which waited for: 7 -> 5; matrix products, arithmetic and copies ran while one was open for 16% -> 0% of each run, Pallas kernels for 0% -> 31%
where the time goes in v1:
time: 183 us; the launch traced here: 182 us
  Pallas kernels  103 us (56%)
  waiting for transfers between devices  24.6 us (13%)
  blocking collectives  19.1 us (10%)
  starting transfers between devices  18.5 us (10%)
  between operations  15.7 us (9%)
    pallas_call x8, Pallas kernels, qkv(): pl.pallas_call(functools.partial(qkv_kernel, before is None, resid, pair_...  50.1 us
    pallas_call x1, Pallas kernels, on_device(): pl.pallas_call(functools.partial(plan_kernel, groups, share, cap, rows_he...  27.1 us
    all_to_all x2, waiting for transfers between devices, on_device(): got = lax.all_to_all(send, 'group', split_axis=0, concat_axis=0, tiled=True)  11.9 us
    pallas_call x1, Pallas kernels, on_device(): pl.pallas_call(functools.partial(attend_kernel, width, length, pair_rows,...  11.5 us
    all_gather x1, blocking collectives, on_device(): codes = lax.all_gather(code, 'group', tiled=True)  10.2 us
    pallas_call x1, Pallas kernels, on_device(): pl.pallas_call(functools.partial(gather_kernel, rows_here, cells, first,...  10.1 us
    all_gather x1, blocking collectives, on_device(): everyone = lax.all_gather(pooled, 'group', tiled=True)  8.88 us
    ppermute x6, waiting for transfers between devices, on_device(): held = [lax.ppermute(x, 'tensor', ring) for x in held]  7.9 us
  transfers between devices with their start and end apart: 11, of which 5 were waited for; matrix products, arithmetic and copies ran while one was open for 0% of the time, Pallas kernels for 31%

profile of v1, /device:TPU:0, one launch (start us, length us, event | category | flops | bytes accessed | tf_op | source)
XLA Modules:
  0.0 182.3 jit_solution(3378819061488709758)
XLA Ops:
  7.2 0.0 copy-start.2
  8.0 0.7 compare_select_fusion.6
  8.7 0.1 tile.10
  8.8 10.2 %all-gather = s32[8,1,128]{2,1,0:T(1,128)S(1)} all-gather(s32[1,1,128]{2,1,0:T(1,128)S(1)} %fusion.46), channel_id=1, replica_groups=mesh['group'=8,'tensor'=4] {'group'}, dimensions={0}, use_global_device_ids=true | all-gather | bytes 4608 | tf_op jit(solution)/shard_map/all_gather | solution.py:502
  19.0 27.1 %shard_map.135 = (s32[8,128]{1,0:T(8,128)S(1)}, bf16[48,2,4096]{2,1,0:T(2,128)(2,1)}) custom-call(s32[1]{0:T(128)} %bitcast.35.me, s32[8,128]{1,0:T(8,128)S(1)} %bitcast.114, bf16[64,2,8192]{2,1,0:T(2,128)(2,1)} %left.3, bf16[64,2,8192]{2,1,0:T(2,128)(2,1)} %right.3), custom_call_target="tpu_custom_call" | custom-call | tf_op jit(solution)/shard_map/pallas_call | solution.py:507
  46.1 3.6 %all-to-all-start.7 = ((bf16[48,2,4096]{2,1,0:T(2,128)(2,1)}), bf16[48,2,4096]{2,1,0:T(2,128)(2,1)S(1)}, u32[]{:S(2)}, u32[]{:S(2)}) async-start(bf16[48,2,4096]{2,1,0:T(2,128)(2,1)} %get-tuple-element.65), calls=%async_computation.8 | async-start | bytes 1572864 | tf_op jit(solution)/shard_map/all_to_all | solution.py:535
  49.7 0.0 copy-done.2
  49.7 0.0 copy-start.5
  49.7 10.1 %shard_map.136 = bf16[48,2,4096]{2,1,0:T(2,128)(2,1)} custom-call(s32[8,128]{1,0:T(8,128)S(1)} %get-tuple-element.64.plan, bf16[64,2,8192]{2,1,0:T(2,128)(2,1)S(1)} %copy-done.2, bf16[64,2,8192]{2,1,0:T(2,128)(2,1)} %right.3), custom_call_target="tpu_custom_call" | custom-call | tf_op jit(solution)/shard_map/pallas_call | solution.py:522
  59.8 2.4 %all-to-all-done.7.got = bf16[48,2,4096]{2,1,0:T(2,128)(2,1)S(1)} async-done(((bf16[48,2,4096]{2,1,0:T(2,128)(2,1)}), bf16[48,2,4096]{2,1,0:T(2,128)(2,1)S(1)}, u32[]{:S(2)}, u32[]{:S(2)}) %all-to-all-start.7) | async-done | bytes 786464 | tf_op jit(solution)/shard_map/all_to_all | solution.py:535
  62.2 3.5 %all-to-all-start.6 = ((bf16[48,2,4096]{2,1,0:T(2,128)(2,1)}), bf16[48,2,4096]{2,1,0:T(2,128)(2,1)S(1)}, u32[]{:S(2)}, u32[]{:S(2)}) async-start(bf16[48,2,4096]{2,1,0:T(2,128)(2,1)} %shard_map.136), calls=%async_computation.7 | async-start | bytes 1572864 | tf_op jit(solution)/shard_map/all_to_all | solution.py:535
  65.8 1.4 shard_map.138.refs_0_
  67.2 1.6 collective-permute-start.1
  68.8 9.5 %all-to-all-done.6.got = bf16[48,2,4096]{2,1,0:T(2,128)(2,1)S(1)} async-done(((bf16[48,2,4096]{2,1,0:T(2,128)(2,1)}), bf16[48,2,4096]{2,1,0:T(2,128)(2,1)S(1)}, u32[]{:S(2)}, u32[]{:S(2)}) %all-to-all-start.6) | async-done | bytes 786464 | tf_op jit(solution)/shard_map/all_to_all | solution.py:535
  78.3 1.4 shard_map.137.refs_0_
  79.7 1.6 collective-permute-start
  81.3 0.0 collective-permute-done.1.refs_0_
  81.3 1.6 collective-permute-start.3
  82.9 7.9 %collective-permute-done.refs_0_ = bf16[32,4096]{1,0:T(8,128)(2,1)S(1)} collective-permute-done((bf16[32,4096]{1,0:T(8,128)(2,1)S(1)}, bf16[32,4096]{1,0:T(8,128)(2,1)S(1)}, u32[]{:S(2)}, u32[]{:S(2)}) %collective-permute-start) | collective-permute-done | bytes 262176 | tf_op jit(solution)/shard_map/ppermute | solution.py:562
  90.8 0.0 collective-permute-start.2
  90.8 0.0 copy-done.5
  90.8 6.4 %shard_map.139 = (f32[32,1536]{1,0:T(8,128)S(1)}, f32[32,128]{1,0:T(8,128)S(1)}, f32[8,4096]{1,0:T(8,128)S(1)}) custom-call(bf16[32,4096]{1,0:T(8,128)(2,1)S(1)} %shard_map.138.refs_0_, f32[1,8192]{1,0:T(1,128)S(1)} %bitcast.121, bf16[8192,1024]{1,0:T(8,128)(2,1)} %refs_2_.15, bf16[8192,256]{1,0:T(8,128)(2,1)} %refs_3_.15, bf16[8192,256]{1,0:T(8,128)(2,1)} %refs_4_.15), custom_call_target="tpu_custom_call" | custom-call | flops 402653184 | bytes 12582912 | tf_op jit(solution)/shard_map/pallas_call | solution.py:456
  97.2 6.4 %shard_map.140 = (f32[32,1536]{1,0:T(8,128)S(1)}, f32[32,128]{1,0:T(8,128)S(1)}, f32[8,4096]{1,0:T(8,128)S(1)}) custom-call(bf16[32,4096]{1,0:T(8,128)(2,1)S(1)} %shard_map.137.refs_0_, f32[1,8192]{1,0:T(1,128)S(1)} %bitcast.122, bf16[8192,1024]{1,0:T(8,128)(2,1)} %refs_2_.15, bf16[8192,256]{1,0:T(8,128)(2,1)} %refs_3_.15, bf16[8192,256]{1,0:T(8,128)(2,1)} %refs_4_.15, ...), custom_call_target="tpu_custom_call" | custom-call | flops 402653184 | bytes 12582912 | tf_op jit(solution)/shard_map/pallas_call | solution.py:456
  103.6 0.0 collective-permute-done.3.refs_0_
  103.6 1.4 collective-permute-start.5
  105.0 0.0 collective-permute-done.2.refs_0_
  105.0 1.6 collective-permute-start.4
  106.6 6.2 %shard_map.141 = (f32[32,1536]{1,0:T(8,128)S(1)}, f32[32,128]{1,0:T(8,128)S(1)}) custom-call(bf16[32,4096]{1,0:T(8,128)(2,1)S(1)} %collective-permute-done.1.refs_0_, f32[1,8192]{1,0:T(1,128)S(1)} %bitcast.123, bf16[8192,1024]{1,0:T(8,128)(2,1)} %refs_2_.15, bf16[8192,256]{1,0:T(8,128)(2,1)} %refs_3_.15, bf16[8192,256]{1,0:T(8,128)(2,1)} %refs_4_.15), custom_call_target="tpu_custom_call" | custom-call | flops 402653184 | bytes 12582912 | tf_op jit(solution)/shard_map/pallas_call | solution.py:456
  112.8 6.2 %shard_map.142 = (f32[32,1536]{1,0:T(8,128)S(1)}, f32[32,128]{1,0:T(8,128)S(1)}) custom-call(bf16[32,4096]{1,0:T(8,128)(2,1)S(1)} %collective-permute-done.refs_0_, f32[1,8192]{1,0:T(1,128)S(1)} %bitcast.124, bf16[8192,1024]{1,0:T(8,128)(2,1)} %refs_2_.15, bf16[8192,256]{1,0:T(8,128)(2,1)} %refs_3_.15, bf16[8192,256]{1,0:T(8,128)(2,1)} %refs_4_.15, ...), custom_call_target="tpu_custom_call" | custom-call | flops 402653184 | bytes 12582912 | tf_op jit(solution)/shard_map/pallas_call | solution.py:456
  119.0 6.2 %shard_map.143 = (f32[32,1536]{1,0:T(8,128)S(1)}, f32[32,128]{1,0:T(8,128)S(1)}) custom-call(bf16[32,4096]{1,0:T(8,128)(2,1)S(1)} %collective-permute-done.3.refs_0_, f32[1,8192]{1,0:T(1,128)S(1)} %bitcast.125, bf16[8192,1024]{1,0:T(8,128)(2,1)} %refs_2_.15, bf16[8192,256]{1,0:T(8,128)(2,1)} %refs_3_.15, bf16[8192,256]{1,0:T(8,128)(2,1)} %refs_4_.15), custom_call_target="tpu_custom_call" | custom-call | flops 402653184 | bytes 12582912 | tf_op jit(solution)/shard_map/pallas_call | solution.py:456
  125.2 6.2 %shard_map.144 = (f32[32,1536]{1,0:T(8,128)S(1)}, f32[32,128]{1,0:T(8,128)S(1)}) custom-call(bf16[32,4096]{1,0:T(8,128)(2,1)S(1)} %collective-permute-done.2.refs_0_, f32[1,8192]{1,0:T(1,128)S(1)} %bitcast.126, bf16[8192,1024]{1,0:T(8,128)(2,1)} %refs_2_.15, bf16[8192,256]{1,0:T(8,128)(2,1)} %refs_3_.15, bf16[8192,256]{1,0:T(8,128)(2,1)} %refs_4_.15, ...), custom_call_target="tpu_custom_call" | custom-call | flops 402653184 | bytes 12582912 | tf_op jit(solution)/shard_map/pallas_call | solution.py:456
  131.5 0.0 collective-permute-done.5.refs_0_
  131.5 6.2 %shard_map.145 = (f32[32,1536]{1,0:T(8,128)S(1)}, f32[32,128]{1,0:T(8,128)S(1)}) custom-call(bf16[32,4096]{1,0:T(8,128)(2,1)S(1)} %collective-permute-done.5.refs_0_, f32[1,8192]{1,0:T(1,128)S(1)} %bitcast.127, bf16[8192,1024]{1,0:T(8,128)(2,1)} %refs_2_.15, bf16[8192,256]{1,0:T(8,128)(2,1)} %refs_3_.15, bf16[8192,256]{1,0:T(8,128)(2,1)} %refs_4_.15), custom_call_target="tpu_custom_call" | custom-call | flops 402653184 | bytes 12582912 | tf_op jit(solution)/shard_map/pallas_call | solution.py:456
  137.7 0.0 collective-permute-done.4.refs_0_
  137.7 6.2 %shard_map.146 = (f32[32,1536]{1,0:T(8,128)S(1)}, f32[32,128]{1,0:T(8,128)S(1)}) custom-call(bf16[32,4096]{1,0:T(8,128)(2,1)S(1)} %collective-permute-done.4.refs_0_, f32[1,8192]{1,0:T(1,128)S(1)} %bitcast.128, bf16[8192,1024]{1,0:T(8,128)(2,1)} %refs_2_.15, bf16[8192,256]{1,0:T(8,128)(2,1)} %refs_3_.15, bf16[8192,256]{1,0:T(8,128)(2,1)} %refs_4_.15, ...), custom_call_target="tpu_custom_call" | custom-call | flops 402653184 | bytes 12582912 | tf_op jit(solution)/shard_map/pallas_call | solution.py:456
  143.9 0.0 copy-start.3
  143.9 0.0 copy-start.6
  144.0 0.0 copy-start.7
  144.0 0.0 copy-start.8
  144.0 0.0 copy-start.9
  144.0 11.5 %shard_map.147 = f32[4,8,2048]{2,1,0:T(8,128)S(1)} custom-call(s32[1]{0:T(128)} %bitcast.42.refs_0_, f32[32,1536]{1,0:T(8,128)S(1)} %get-tuple-element.68.refs_1_, f32[32,1536]{1,0:T(8,128)S(1)} %get-tuple-element.71.refs_2_, f32[32,1536]{1,0:T(8,128)S(1)} %get-tuple-element.74.refs_3_, f32[32,1536]{1,0:T(8,128)S(1)} %get-tuple-element.77.refs_4_, ...), custom_call_target="tpu_custom_call" | custom-call | flops 268435456 | bytes 16777216 | tf_op jit(solution)/shard_map/pallas_call | solution.py:569
  155.6 2.1 %collective-permute-start.6 = (f32[8,2048]{1,0:T(8,128)S(1)}, f32[8,2048]{1,0:T(8,128)S(1)}, u32[]{:S(2)}, u32[]{:S(2)}) collective-permute-start(f32[8,2048]{1,0:T(8,128)S(1)} %get-tuple-element.144), channel_id=1, source_target_pairs={{0,1},{1,0},{2,3},{3,2},{4,5},{5,4},{6,7},{7,6},{8,9},{9,8},{10,11... | collective-permute-start | bytes 196616 | tf_op jit(solution)/shard_map/ppermute | solution.py:605
  157.7 1.0 collective-permute-start.8
  158.6 0.6 collective-permute-start.7
  159.2 0.5 slice.21
  160.4 0.0 collective-permute-done.6
  160.4 3.4 %collective-permute-done.8 = f32[8,2048]{1,0:T(8,128)S(1)} collective-permute-done((f32[8,2048]{1,0:T(8,128)S(1)}, f32[8,2048]{1,0:T(8,128)S(1)}, u32[]{:S(2)}, u32[]{:S(2)}) %collective-permute-start.8) | collective-permute-done | bytes 65568 | tf_op jit(solution)/shard_map/ppermute | solution.py:605
  163.8 1.3 collective-permute-done.7
  165.1 8.9 %all_gather.7 = f32[64,2048]{1,0:T(8,128)S(1)} all-gather(f32[8,2048]{1,0:T(8,128)S(1)} %fusion.45), channel_id=1, replica_groups=mesh['group'=8,'tensor'=4] {'group'}, dimensions={0}, use_global_device_ids=true | all-gather | bytes 589824 | tf_op jit(solution)/shard_map/all_gather | solution.py:606
  174.0 0.0 copy-done.3
  174.0 0.0 copy-done.6
  174.0 0.0 copy-done.7
  174.0 0.0 copy-done.8
  174.0 0.0 copy-done.9
  174.0 1.4 conditional.1
  174.1 1.4 branch_0_fun.1
  (5 shorter events, 0.1 us)
Async XLA Ops:
  7.2 42.5 %copy-start.2 = (bf16[64,2,8192]{2,1,0:T(2,128)(2,1)S(1)}, bf16[64,2,8192]{2,1,0:T(2,128)(2,1)}, u32[]{:S(2)}) copy-start(bf16[64,2,8192]{2,1,0:T(2,128)(2,1)} %left.3) | copy-start | bytes 6291460
  46.1 16.1 %all-to-all-start.7 = ((bf16[48,2,4096]{2,1,0:T(2,128)(2,1)}), bf16[48,2,4096]{2,1,0:T(2,128)(2,1)S(1)}, u32[]{:S(2)}, u32[]{:S(2)}) async-start(bf16[48,2,4096]{2,1,0:T(2,128)(2,1)} %get-tuple-element.65), calls=%async_computation.8 | async-start | bytes 1572864 | tf_op jit(solution)/shard_map/all_to_all | solution.py:535
  49.7 41.1 %copy-start.5 = (f32[8192]{0:T(1024)S(1)}, f32[8192]{0:T(1024)}, u32[]{:S(2)}) copy-start(f32[8192]{0:T(1024)} %param.21) | copy-start | bytes 98308
  62.2 16.1 %all-to-all-start.6 = ((bf16[48,2,4096]{2,1,0:T(2,128)(2,1)}), bf16[48,2,4096]{2,1,0:T(2,128)(2,1)S(1)}, u32[]{:S(2)}, u32[]{:S(2)}) async-start(bf16[48,2,4096]{2,1,0:T(2,128)(2,1)} %shard_map.136), calls=%async_computation.7 | async-start | bytes 1572864 | tf_op jit(solution)/shard_map/all_to_all | solution.py:535
  67.2 14.2 %collective-permute-start.1 = (bf16[32,4096]{1,0:T(8,128)(2,1)S(1)}, bf16[32,4096]{1,0:T(8,128)(2,1)S(1)}, u32[]{:S(2)}, u32[]{:S(2)}) collective-permute-start(bf16[32,4096]{1,0:T(8,128)(2,1)S(1)} %shard_map.138.refs_0_), channel_id=1, source_target_pairs={{0,1},{1,2},{2,3},{3,0},{4,5},{5,6},{6,7},{7,4},{8,9},{9,10},{10,1... | collective-permute-start | bytes 786440 | tf_op jit(solution)/shard_map/ppermute | solution.py:562
  79.7 11.1 %collective-permute-start = (bf16[32,4096]{1,0:T(8,128)(2,1)S(1)}, bf16[32,4096]{1,0:T(8,128)(2,1)S(1)}, u32[]{:S(2)}, u32[]{:S(2)}) collective-permute-start(bf16[32,4096]{1,0:T(8,128)(2,1)S(1)} %shard_map.137.refs_0_), channel_id=1, source_target_pairs={{0,1},{1,2},{2,3},{3,0},{4,5},{5,6},{6,7},{7,4},{8,9},{9,10},{10,1... | collective-permute-start | bytes 786440 | tf_op jit(solution)/shard_map/ppermute | solution.py:562
  81.3 22.3 %collective-permute-start.3 = (bf16[32,4096]{1,0:T(8,128)(2,1)S(1)}, bf16[32,4096]{1,0:T(8,128)(2,1)S(1)}, u32[]{:S(2)}, u32[]{:S(2)}) collective-permute-start(bf16[32,4096]{1,0:T(8,128)(2,1)S(1)} %collective-permute-done.1.refs_0_), channel_id=1, source_target_pairs={{0,1},{1,2},{2,3},{3,0},{4,5},{5,6},{6,7},{7,4},{8,9},{9,10},{10,1... | collective-permute-start | bytes 786440 | tf_op jit(solution)/shard_map/ppermute | solution.py:562
  90.8 14.2 %collective-permute-start.2 = (bf16[32,4096]{1,0:T(8,128)(2,1)S(1)}, bf16[32,4096]{1,0:T(8,128)(2,1)S(1)}, u32[]{:S(2)}, u32[]{:S(2)}) collective-permute-start(bf16[32,4096]{1,0:T(8,128)(2,1)S(1)} %collective-permute-done.refs_0_), channel_id=1, source_target_pairs={{0,1},{1,2},{2,3},{3,0},{4,5},{5,6},{6,7},{7,4},{8,9},{9,10},{10,1... | collective-permute-start | bytes 786440 | tf_op jit(solution)/shard_map/ppermute | solution.py:562
  103.6 27.9 %collective-permute-start.5 = (bf16[32,4096]{1,0:T(8,128)(2,1)S(1)}, bf16[32,4096]{1,0:T(8,128)(2,1)S(1)}, u32[]{:S(2)}, u32[]{:S(2)}) collective-permute-start(bf16[32,4096]{1,0:T(8,128)(2,1)S(1)} %collective-permute-done.3.refs_0_), channel_id=1, source_target_pairs={{0,1},{1,2},{2,3},{3,0},{4,5},{5,6},{6,7},{7,4},{8,9},{9,10},{10,1... | collective-permute-start | bytes 786440 | tf_op jit(solution)/shard_map/ppermute | solution.py:562
  105.0 32.7 %collective-permute-start.4 = (bf16[32,4096]{1,0:T(8,128)(2,1)S(1)}, bf16[32,4096]{1,0:T(8,128)(2,1)S(1)}, u32[]{:S(2)}, u32[]{:S(2)}) collective-permute-start(bf16[32,4096]{1,0:T(8,128)(2,1)S(1)} %collective-permute-done.2.refs_0_), channel_id=1, source_target_pairs={{0,1},{1,2},{2,3},{3,0},{4,5},{5,6},{6,7},{7,4},{8,9},{9,10},{10,1... | collective-permute-start | bytes 786440 | tf_op jit(solution)/shard_map/ppermute | solution.py:562
  143.9 30.1 %copy-start.3 = (bf16[64,2,8192]{2,1,0:T(2,128)(2,1)S(1)}, bf16[64,2,8192]{2,1,0:T(2,128)(2,1)}, u32[]{:S(2)}) copy-start(bf16[64,2,8192]{2,1,0:T(2,128)(2,1)} %left.3) | copy-start | bytes 6291460
  143.9 30.1 %copy-start.6 = (s32[16,1]{0,1:T(1,128)S(1)}, s32[16,1]{0,1:T(1,128)}, u32[]{:S(2)}) copy-start(s32[16,1]{0,1:T(1,128)} %param.18) | copy-start | bytes 196
  144.0 30.1 %copy-start.7 = (s32[16,1]{0,1:T(1,128)S(1)}, s32[16,1]{0,1:T(1,128)}, u32[]{:S(2)}) copy-start(s32[16,1]{0,1:T(1,128)} %param.16) | copy-start | bytes 196
  144.0 30.1 %copy-start.8 = (s32[16]{0:T(128)S(1)}, s32[16]{0:T(128)}, u32[]{:S(2)}) copy-start(s32[16]{0:T(128)} %param.19) | copy-start | bytes 196
  144.0 30.1 %copy-start.9 = (s32[16]{0:T(128)S(1)}, s32[16]{0:T(128)}, u32[]{:S(2)}) copy-start(s32[16]{0:T(128)} %param.17) | copy-start | bytes 196
  155.6 4.8 %collective-permute-start.6 = (f32[8,2048]{1,0:T(8,128)S(1)}, f32[8,2048]{1,0:T(8,128)S(1)}, u32[]{:S(2)}, u32[]{:S(2)}) collective-permute-start(f32[8,2048]{1,0:T(8,128)S(1)} %get-tuple-element.144), channel_id=1, source_target_pairs={{0,1},{1,0},{2,3},{3,2},{4,5},{5,4},{6,7},{7,6},{8,9},{9,8},{10,11... | collective-permute-start | bytes 196616 | tf_op jit(solution)/shard_map/ppermute | solution.py:605
  157.7 6.1 %collective-permute-start.8 = (f32[8,2048]{1,0:T(8,128)S(1)}, f32[8,2048]{1,0:T(8,128)S(1)}, u32[]{:S(2)}, u32[]{:S(2)}) collective-permute-start(f32[8,2048]{1,0:T(8,128)S(1)} %get-tuple-element.145), channel_id=1, source_target_pairs={{0,3},{1,2},{2,1},{3,0},{4,7},{5,6},{6,5},{7,4},{8,11},{9,10},{10,... | collective-permute-start | bytes 196616 | tf_op jit(solution)/shard_map/ppermute | solution.py:605
  158.6 6.5 %collective-permute-start.7 = (f32[8,2048]{1,0:T(8,128)S(1)}, f32[8,2048]{1,0:T(8,128)S(1)}, u32[]{:S(2)}, u32[]{:S(2)}) collective-permute-start(f32[8,2048]{1,0:T(8,128)S(1)} %get-tuple-element.146), channel_id=1, source_target_pairs={{0,2},{1,3},{2,0},{3,1},{4,6},{5,7},{6,4},{7,5},{8,10},{9,11},{10,... | collective-permute-start | bytes 196616 | tf_op jit(solution)/shard_map/ppermute | solution.py:605

commit v2 on v1

--- a/solution.py
+++ b/solution.py
@@ -146,7 +146,10 @@
 LANES = 128
 DEAD = -1
 RIGHT_SHIFT = 12
-DEALS = 8
+DEALS = (43, 21, 34, 1, 15, 10, 61, 5, 7, 50, 11, 4)
+LOADS = 8
+COST = 512
+WO_PARTS = 2
 BF16 = jnp.bfloat16
 F32 = jnp.float32
 
@@ -160,7 +163,7 @@
 def plan_sizes(groups, pairs_here):
     share = pairs_here // 2
     mean = -(-2 * share // groups)
-    return (share, min(LANES // groups, 3 * mean))
+    return (share, min(LANES // groups, (5 * mean + 1) // 2))
 
 
 def column(row):
@@ -192,14 +195,15 @@
     lo_c, ro_c = left_c >> rbits, right_c >> rbits
     order_c = lax.broadcasted_iota(jnp.int32, (n, 1), 0)
 
-    def key(low, rown, alive, at, turn):
-        second = (rown + turn * low) & (groups - 1)
-        return jnp.where(alive, ((low << gbits) + second) * n, groups * groups * n) + at
+    def key(one, other, alive, at, deal):
+        major, minor = (other, one) if deal >> 5 else (one, other)
+        minor = (minor * (2 * ((deal >> 3) & 3) + 1) + (deal & 7) * major) & (groups - 1)
+        return jnp.where(alive, ((major << gbits) + minor) * n, groups * groups * n) + at
 
     best, best_load = None, None
-    for turn in range(DEALS):
-        key_r = key(left_own, right_own, live, order, turn)
-        key_c = key(lo_c, ro_c, live_c > 0, order_c, turn)
+    for deal in DEALS:
+        key_r = key(left_own, right_own, live, order, deal)
+        key_c = key(lo_c, ro_c, live_c > 0, order_c, deal)
         rank = jnp.sum((key_c < key_r).astype(jnp.int32), axis=0, keepdims=True)
         to = jnp.where(rank < live_total, rank & (groups - 1), groups)
         hit = (to == owners).astype(BF16)
@@ -238,9 +242,9 @@
     right_in = jnp.logical_and(alive, right_pos < cap)
     local_left, local_right = left_c & (rows_here - 1), right_c & (rows_here - 1)
     send = place(
-        jnp.logical_and(left_in, lo_c == me), to_c * cap + left_pos, local_left
+        jnp.logical_and(left_in, lo_c == me), to_c * cap + left_pos, local_left + 1
     ) + place(
-        jnp.logical_and(right_in, ro_c == me), to_c * cap + right_pos, local_right + rows_here
+        jnp.logical_and(right_in, ro_c == me), to_c * cap + right_pos, local_right + rows_here + 1
     )
     mine = jnp.logical_and(alive, to_c == me)
     fetch = place(
@@ -253,33 +257,30 @@
     return (send, fetch, left_row, right_row, over)
 
 
-def copy_rows(index_of, source_of, target, sems, number, start):
-    for cell in range(number):
-        index = index_of(cell)
-        start(index, cell, target.at[cell], sems.at[cell])
-
-
 def gather_cells(plan, left, right, out, sems, rows_here, cells, first, wide):
-    def one(cell, begin):
-        index = plan[0, cell]
+    def begin(cell, carry):
+        index = plan[0, cell] - 1
         row = index & (rows_here - 1)
         for side, table in ((0, left), (1, right)):
 
-            @pl.when((index >= rows_here) == (side == 1))
+            @pl.when(jnp.logical_and(index >= side * rows_here, index < (side + 1) * rows_here))
             def _():
-                copy = pltpu.make_async_copy(
+                pltpu.make_async_copy(
                     table.at[row, :, pl.ds(first, wide)], out.at[cell], sems.at[cell]
-                )
-                copy.start()
-
-    lax.fori_loop(0, cells, lambda cell, carry: (one(cell, True), carry)[1], 0)
+                ).start()
+
+        return carry
 
     def finish(cell, carry):
-        pltpu.make_async_copy(
-            left.at[0, :, pl.ds(first, wide)], out.at[cell], sems.at[cell]
-        ).wait()
+        @pl.when(plan[0, cell] > 0)
+        def _():
+            pltpu.make_async_copy(
+                left.at[0, :, pl.ds(first, wide)], out.at[cell], sems.at[cell]
+            ).wait()
+
         return carry
 
+    lax.fori_loop(0, cells, begin, 0)
     lax.fori_loop(0, cells, finish, 0)
 
 
@@ -298,7 +299,9 @@
     gather_cells(plan, left, right, out, sems, rows_here, cells, first, wide)
 
 
-def pick_kernel(items, plan, got, out, held, sems):
+def pick_kernel(items, after, plan, got, *refs):
+    out, held, sems = refs[after:]
+
     def begin(item, carry):
         pltpu.make_async_copy(got.at[plan[1, item]], held.at[item], sems.at[item]).start()
         return carry
@@ -312,100 +315,172 @@
     out[...] = held[...].reshape(out.shape)
 
 
-def qkv_kernel(first, resid, pair_rows, *refs):
+def products(x_refs, gain, weights, first, ready=None):
+    rows, wide = sum(x.shape[0] for x in x_refs), x_refs[0].shape[1]
+    block = wide // LOADS
+    widths = [w.shape[1] for w in weights]
+
+    def one(i, carry):
+        sums, square = carry
+        if ready is not None:
+            ready(i)
+        at = pl.multiple_of(i * block, block)
+        x = jnp.concatenate([x[:, pl.ds(at, block)] for x in x_refs], axis=0).astype(F32)
+        normed = (x * gain[:, pl.ds(first + at, block)]).astype(BF16)
+        sums = tuple(
+            total + jnp.dot(normed, w[pl.ds(at, block), :], preferred_element_type=F32)
+            for total, w in zip(sums, weights)
+        )
+        return (sums, square + jnp.sum(x * x, axis=1, keepdims=True))
+
+    zero = (tuple(jnp.zeros((rows, n), F32) for n in widths), jnp.zeros((rows, 1), F32))
+    sums, square = lax.fori_loop(0, LOADS, one, zero)
+    return (jnp.concatenate(sums, axis=1), square)
+
+
+def qkv_kernel(shards, first, loads, keep, extra, more, resid, after, pair_rows, *refs):
     refs = list(refs)
-    x_ref, gain, wq, wk, wv = refs[:5]
-    refs = refs[5:]
-    if not first:
-        acc_in, sq_in = refs[:2]
-        refs = refs[2:]
-    acc, sq = refs[:2]
-    step = pl.program_id(0)
-    x = x_ref[...]
-    wide = x.astype(F32)
-    normed = (wide * gain[...]).astype(BF16)
-    q = jnp.dot(normed, wq[...], preferred_element_type=F32)
-    k = jnp.dot(normed, wk[...], preferred_element_type=F32)
-    v = jnp.dot(normed, wv[...], preferred_element_type=F32)
-    square = jnp.broadcast_to(jnp.sum(wide * wide, axis=1, keepdims=True), sq.shape)
-    nq, nk = q.shape[1], k.shape[1]
-
-    @pl.when(step == 0)
-    def _():
-        if first:
-            acc[...] = jnp.zeros_like(acc)
-            sq[...] = jnp.zeros_like(sq)
-        else:
-            acc[...] = acc_in[...]
-            sq[...] = sq_in[...]
-
-    acc[:, :nq] += q
-    acc[:, nq : nq + nk] += k
-    acc[:, nq + nk :] += v
-    sq[...] += square
+    x_refs = [refs.pop(0) for _ in range(shards)]
+    gain = refs.pop(0)
+    sources = [refs.pop(0) for _ in range(3)]
+    before = [refs.pop(0) for _ in range(2)] if more else None
+    extra_source = refs.pop(0) if extra is not None else None
+    del refs[:after]
+    sums_out, square_out = refs.pop(0), refs.pop(0)
+    resid_out = refs.pop(0) if resid else None
+    ready, weights = None, sources
+    if keep:
+        weights = [refs.pop(0) for _ in range(3)]
+    extra_held = refs.pop(0) if extra is not None else None
+    if loads and not keep:
+        weights = [refs.pop(0) for _ in range(3)]
+    if loads:
+        sems = refs.pop(0)
+        block = x_refs[0].shape[1] // LOADS
+
+        def copy(which, i):
+            at = i * block
+            return pltpu.make_async_copy(
+                sources[which].at[pl.ds(first + at, block)],
+                weights[which].at[pl.ds(at, block)],
+                sems.at[which, i],
+            )
+
+        for i in range(LOADS):
+            for which in range(3):
+                copy(which, i).start()
+
+        def ready(i):
+            for which in range(3):
+                copy(which, i).wait()
+
+    if extra is not None:
+        extra_copy = pltpu.make_async_copy(
+            extra_source.at[pl.ds(extra, extra_held.shape[0])], extra_held, refs.pop(0)
+        )
+        extra_copy.start()
+    sums, square = products(x_refs, gain, weights, first, ready)
+    square = jnp.broadcast_to(square, (square.shape[0], LANES))
+    if more:
+        sums += before[0][...]
+        square += before[1][...]
+    sums_out[...] = sums
+    square_out[...] = square
     if resid:
-        rows = x.shape[0]
+        rows = x_refs[0].shape[0]
         pairs = rows // pair_rows
         pair = lax.broadcasted_iota(jnp.int32, (pairs, rows), 1) // pair_rows
         mine = (pair == lax.broadcasted_iota(jnp.int32, (pairs, rows), 0)).astype(BF16)
-        refs[2][...] = jnp.dot(mine, x, preferred_element_type=F32)
-
-
-def attend_kernel(width, length, pair_rows, heads, kv_heads, *refs):
-    shards = (len(refs) - 5) // 2
-    t_ref = refs[0]
-    accs, sqs = refs[1 : 1 + shards], refs[1 + shards : 1 + 2 * shards]
-    resid, wo, out, ctx = refs[1 + 2 * shards :]
-    pairs = out.shape[1]
-
-    @pl.when(pl.program_id(0) == 0)
-    def _():
-        acc = jnp.concatenate([a[...] for a in accs], axis=0)
-        sq = jnp.concatenate([s[...] for s in sqs], axis=0)[:, :1]
-        tokens = acc.shape[0]
-        scale = lax.rsqrt(sq * (1.0 / width) + 1e-05)
-        acc = acc * scale
-        rows = tokens // shards
-        row = lax.broadcasted_iota(jnp.int32, (tokens, tokens), 0)
-        col = lax.broadcasted_iota(jnp.int32, (tokens, tokens), 1)
-        same = ((row & (rows - 1)) >> log2(pair_rows)) == ((col & (rows - 1)) >> log2(pair_rows))
-        pair = lax.broadcasted_iota(jnp.int32, (pairs, tokens), 0)
-        token = lax.broadcasted_iota(jnp.int32, (pairs, tokens), 1)
-        member = ((token & (rows - 1)) >> log2(pair_rows)) == pair
-        nq = heads * HEAD_DIM
-        nk = kv_heads * HEAD_DIM
-
-        def unit(part):
-            return (
-                part * lax.rsqrt(jnp.mean(part * part, axis=1, keepdims=True) + 1e-06)
-            ).astype(BF16)
-
-        for kv in range(kv_heads):
-            k = unit(acc[:, nq + kv * HEAD_DIM : nq + (kv + 1) * HEAD_DIM])
-            v = acc[:, nq + nk + kv * HEAD_DIM : nq + nk + (kv + 1) * HEAD_DIM].astype(BF16)
-            for part in range(heads // kv_heads):
-                head = kv * (heads // kv_heads) + part
-                q = unit(acc[:, head * HEAD_DIM : (head + 1) * HEAD_DIM])
-                scores = lax.dot_general(
-                    q, k, (((1,), (1,)), ((), ())), preferred_element_type=F32
-                ) * (score_scale / HEAD_DIM)
-                expo = jnp.where(same, jnp.exp(scores), 0.0)
-                weights = expo / jnp.sum(expo, axis=1, keepdims=True)
-                mean = jnp.sum(weights, axis=0, keepdims=True) * (1.0 / length)
-                spread = jnp.where(member, mean, 0.0)
-                high = spread.astype(BF16)
-                low = (spread - high.astype(F32)).astype(BF16)
-                context = jnp.dot(
-                    jnp.concatenate([high, low], axis=0), v, preferred_element_type=F32
+        resid_out[...] = jnp.dot(mine, x_refs[0][...], preferred_element_type=F32)
+    if extra is not None:
+        extra_copy.wait()
+
+
+def tail_kernel(
+    shards, groups, parts, width, length, pair_rows, first, t_ref, x_ref, gain, wq, wk, wv, *refs
+):
+    wos, refs = refs[:WO_PARTS], refs[WO_PARTS:]
+    accs, sqs, resids = refs[:groups], refs[groups : 2 * groups], refs[2 * groups : 2 * groups + parts]
+    out, ctx = refs[2 * groups + parts :]
+    pairs, features = out.shape[1:]
+    heads, kv_heads = wq.shape[1] // HEAD_DIM, wk.shape[1] // HEAD_DIM
+    share = heads // kv_heads
+    sums, square = products([x_ref], gain, (wq, wk, wv), first)
+    acc = jnp.concatenate([a[...] for a in accs[:-1]] + [accs[-1][...] + sums], axis=0)
+    sq = jnp.concatenate([s[:, :1] for s in sqs[:-1]] + [sqs[-1][:, :1] + square], axis=0)
+    tokens = acc.shape[0]
+    acc = acc * lax.rsqrt(sq * (1.0 / width) + 1e-05)
+    rows = tokens // shards
+    row = lax.broadcasted_iota(jnp.int32, (share * tokens, tokens), 0)
+    col = lax.broadcasted_iota(jnp.int32, (share * tokens, tokens), 1)
+    same = ((row & (rows - 1)) >> log2(pair_rows)) == ((col & (rows - 1)) >> log2(pair_rows))
+    pair = lax.broadcasted_iota(jnp.int32, (pairs, tokens), 0)
+    token = lax.broadcasted_iota(jnp.int32, (pairs, tokens), 1)
+    member = ((token & (rows - 1)) >> log2(pair_rows)) == pair
+    nq, nk = heads * HEAD_DIM, kv_heads * HEAD_DIM
+
+    def unit(part):
+        return (part * lax.rsqrt(jnp.mean(part * part, axis=1, keepdims=True) + 1e-06)).astype(
+            BF16
+        )
+
+    def head(start):
+        return acc[:, start : start + HEAD_DIM]
+
+    for kv in range(kv_heads):
+        k = unit(head(nq + kv * HEAD_DIM))
+        v = head(nq + nk + kv * HEAD_DIM).astype(BF16)
+        q = jnp.concatenate(
+            [unit(head((kv * share + i) * HEAD_DIM)) for i in range(share)], axis=0
+        )
+        scores = lax.dot_general(
+            q, k, (((1,), (1,)), ((), ())), preferred_element_type=F32
+        ) * (score_scale / HEAD_DIM)
+        expo = jnp.where(same, jnp.exp(scores), 0.0)
+        weights = expo / jnp.sum(expo, axis=1, keepdims=True)
+        spread = []
+        for i in range(share):
+            mean = jnp.sum(weights[i * tokens : (i + 1) * tokens], axis=0, keepdims=True)
+            spread.append(jnp.where(member, mean * (1.0 / length), 0.0))
+        spread = jnp.concatenate(spread, axis=0)
+        high = spread.astype(BF16)
+        low = (spread - high.astype(F32)).astype(BF16)
+        context = jnp.dot(
+            jnp.concatenate([high, low], axis=0), v, preferred_element_type=F32
+        )
+        context = context[: share * pairs] + context[share * pairs :]
+        for i in range(share):
+            one_head = context[i * pairs : (i + 1) * pairs]
+            high = one_head.astype(BF16)
+            low = (one_head - high.astype(F32)).astype(BF16)
+            at = (kv * share + i) * HEAD_DIM
+            ctx[:, at : at + HEAD_DIM] = jnp.concatenate([high, low], axis=0)
+
+    block = min(512, features)
+    per = features // block
+    done = 0
+    for resid in resids:
+
+        def one(i, carry):
+            here = pl.multiple_of(i * block, block)
+            i = i + done // block
+            at = pl.multiple_of(i * block, block)
+            deep = wos[0].shape[0]
+            both = sum(
+                jnp.dot(
+                    ctx[:, j * deep : (j + 1) * deep],
+                    wo[:, pl.ds(at, block)],
+                    preferred_element_type=F32,
                 )
-                context = context[:pairs] + context[pairs:]
-                high = context.astype(BF16)
-                low = (context - high.astype(F32)).astype(BF16)
-                at = slice(head * HEAD_DIM, (head + 1) * HEAD_DIM)
-                ctx[:, at] = jnp.concatenate([high, low], axis=0)
-
-    both = jnp.dot(ctx[...], wo[...], preferred_element_type=F32)
-    out[0] = both[:pairs] + both[pairs:] + resid[...] * (1.0 / length)
+                for j, wo in enumerate(wos)
+            )
+            both = both[:pairs] + both[pairs:] + resid[:, pl.ds(here, block)] * (1.0 / length)
+            inside = pl.multiple_of((i % per) * block, block)
+            out[pl.ds((i // per) ^ t_ref[0], 1), :, pl.ds(inside, block)] = both[None]
+            return carry
+
+        lax.fori_loop(0, resid.shape[1] // block, one, 0)
+        done += resid.shape[1]
 
 
 def final_kernel(plan, pooled, left, right):
@@ -420,50 +495,74 @@
 ANY = pl.BlockSpec(memory_space=pl.ANY)
 IN_VMEM = pl.BlockSpec(memory_space=pltpu.VMEM)
 IN_SMEM = pl.BlockSpec(memory_space=pltpu.SMEM)
-LIMIT = pltpu.CompilerParams(vmem_limit_bytes=48 * 1024 * 1024)
+LIMIT = pltpu.CompilerParams(vmem_limit_bytes=6 * 1024 * 1024)
+WIDE_LIMIT = pltpu.CompilerParams(vmem_limit_bytes=24 * 1024 * 1024)
 
 
 def shape(dims, kind):
     return jax.ShapeDtypeStruct(dims, kind)
 
 
-def qkv(x, first_feature, gain, wq, wk, wv, before, resid, pair_rows):
-    rows, wide = x.shape
-    block = min(1024, wide)
-    start = first_feature // block
-    total = wq.shape[1] + wk.shape[1] + wv.shape[1]
-
-    def weight(w):
-        return pl.BlockSpec((block, w.shape[1]), lambda i: (i + start, 0))
-
-    whole = lambda dims: pl.BlockSpec(dims, lambda i: (0, 0))
-    in_specs = [
-        pl.BlockSpec((rows, block), lambda i: (0, i)),
-        pl.BlockSpec((1, block), lambda i: (0, i + start)),
-        weight(wq),
-        weight(wk),
-        weight(wv),
-    ]
-    args = [x, gain, wq, wk, wv]
-    if before is not None:
-        in_specs += [whole((rows, total)), whole((rows, LANES))]
-        args += before
+def held_in_vmem(array):
+    return pltpu.with_memory_space_constraint(array, pltpu.VMEM)
+
+
+def qkv(xs, first, gain, weights, loads, keep, before, resid, pair_rows, extra=None, after=()):
+    rows, wide = sum(x.shape[0] for x in xs), xs[0].shape[1]
+    total = sum(w.shape[1] for w in weights)
+    args = [*xs, gain, *weights] + (before or [])
+    in_specs = [IN_VMEM] * (len(xs) + 1) + [ANY if loads else IN_VMEM] * 3
+    in_specs += [IN_VMEM] * len(before or [])
     out_shape = [shape((rows, total), F32), shape((rows, LANES), F32)]
-    out_specs = [whole((rows, total)), whole((rows, LANES))]
+    scratch = []
     if resid:
-        out_shape.append(shape((rows // pair_rows, wide), F32))
-        out_specs.append(pl.BlockSpec((rows // pair_rows, block), lambda i: (0, i)))
-    return pl.pallas_call(
-        functools.partial(qkv_kernel, before is None, resid, pair_rows),
-        grid=(wide // block,),
+        out_shape.append(shape((xs[0].shape[0] // pair_rows, wide), F32))
+    if loads:
+        halves = [pltpu.VMEM((wide, w.shape[1]), w.dtype) for w in weights]
+        if keep:
+            out_shape += halves
+        else:
+            scratch += halves
+        scratch.append(pltpu.SemaphoreType.DMA((3, LOADS)))
+    if extra is not None:
+        array, part, at = extra
+        args.append(array)
+        in_specs.append(ANY)
+        out_shape.append(pltpu.VMEM((part, array.shape[1]), array.dtype))
+        scratch.append(pltpu.SemaphoreType.DMA(()))
+    args += after
+    in_specs += [ANY] * len(after)
+    out = pl.pallas_call(
+        functools.partial(
+            qkv_kernel,
+            len(xs),
+            first,
+            loads,
+            keep,
+            None if extra is None else extra[2],
+            before is not None,
+            resid,
+            len(after),
+            pair_rows,
+        ),
         in_specs=in_specs,
-        out_specs=out_specs,
+        out_specs=[IN_VMEM] * len(out_shape),
         out_shape=out_shape,
-        compiler_params=LIMIT,
+        scratch_shapes=scratch,
+        compiler_params=LIMIT if keep or not loads else WIDE_LIMIT,
         cost_estimate=pl.CostEstimate(
-            flops=2 * rows * wide * total, bytes_accessed=2 * wide * total, transcendentals=0
+            flops=COST * wide * total, bytes_accessed=2 * rows * wide, transcendentals=0
         ),
     )(*args)
+    out = list(out)
+    result = {"sums": [out.pop(0), out.pop(0)]}
+    if resid:
+        result["resid"] = out.pop(0)
+    if keep:
+        result["weights"] = [held_in_vmem(out.pop(0)) for _ in range(3)]
+    if extra is not None:
+        result["extra"] = held_in_vmem(out.pop(0))
+    return result
 
 
 def on_device(
@@ -501,13 +600,13 @@
     code = jnp.where(at == group, jnp.tile(code, groups), 0)[None, :]
     codes = lax.all_gather(code, "group", tiled=True)
 
-    half = width // 2
-    parts = ((0, half), (half, width - half))
+    head = width * 5 // 8
+    parts = ((0, head), (head, width - head))
     me = jnp.reshape(group, (1,)).astype(jnp.int32)
     plan, cell_rows = pl.pallas_call(
         functools.partial(plan_kernel, groups, share, cap, rows_here, parts[0][1]),
         in_specs=[IN_SMEM, IN_VMEM, ANY, ANY],
-        out_specs=[IN_VMEM, ANY],
+        out_specs=[IN_VMEM, IN_VMEM],
         out_shape=[shape((8, LANES), jnp.int32), shape((cells, toks, parts[0][1]), BF16)],
         scratch_shapes=[
             pltpu.SMEM((8, LANES), jnp.int32),
@@ -522,7 +621,7 @@
             pl.pallas_call(
                 functools.partial(gather_kernel, rows_here, cells, first, wide),
                 in_specs=[IN_SMEM, ANY, ANY],
-                out_specs=ANY,
+                out_specs=IN_VMEM,
                 out_shape=shape((cells, toks, wide), BF16),
                 scratch_shapes=[pltpu.SemaphoreType.DMA((cells,))],
                 compiler_params=LIMIT,
@@ -530,75 +629,96 @@
         )
     gain = norm_gain[None, :]
     weights = (query_weight, key_weight, value_weight)
-    held = []
-    for (first, wide), send in zip(parts, sends):
-        got = lax.all_to_all(send, "group", split_axis=0, concat_axis=0, tiled=True)
-        held.append(
-            pl.pallas_call(
-                functools.partial(pick_kernel, items),
-                in_specs=[IN_SMEM, ANY],
-                out_specs=IN_VMEM,
-                out_shape=shape((rows, wide), BF16),
-                scratch_shapes=[
-                    pltpu.VMEM((items, toks, wide), BF16),
-                    pltpu.SemaphoreType.DMA((items,)),
-                ],
-                compiler_params=LIMIT,
-            )(plan, got)
-        )
-
     ring = [(i, (i + 1) % tensors) for i in range(tensors)]
-    accs, sqs, resids = [], [], []
-    for step in range(tensors):
-        before = None
-        for (first, wide), x in zip(parts, held):
-            out = qkv(x, first, gain, *weights, before, step == 0, pair_rows)
-            before = list(out[:2])
-            if step == 0:
-                resids.append(out[2])
-        accs.append(before[0])
-        sqs.append(before[1])
-        if step < tensors - 1:
-            held = [lax.ppermute(x, "tensor", ring) for x in held]
-    resid = jnp.concatenate(resids, axis=1)
-
-    block = min(1024, features)
-    per = features // block
-    total = accs[0].shape[1]
-    whole = lambda dims: pl.BlockSpec(dims, lambda i, t: (0, 0))
+
+    def exchange(send):
+        return lax.all_to_all(send, "group", split_axis=0, concat_axis=0, tiled=True)
+
+    def pick(got, after):
+        wide = got.shape[2]
+        return pl.pallas_call(
+            functools.partial(pick_kernel, items, len(after)),
+            in_specs=[IN_SMEM, ANY] + [ANY] * len(after),
+            out_specs=IN_VMEM,
+            out_shape=shape((rows, wide), BF16),
+            scratch_shapes=[
+                pltpu.VMEM((items, toks, wide), BF16),
+                pltpu.SemaphoreType.DMA((items,)),
+            ],
+            compiler_params=LIMIT,
+        )(plan, got, *after)
+
+    def pass_on(x):
+        return lax.ppermute(x, "tensor", ring)
+
+    one, two = [[pick(exchange(sends[0]), [])], []]
+    first = qkv(one, parts[0][0], gain, weights, True, False, None, True, pair_rows)
+    one.append(pass_on(one[0]))
+    two.append(pick(exchange(sends[1]), [first["sums"][1], one[1]]))
+    for _ in range(2, tensors):
+        one.append(pass_on(one[-1]))
+    for _ in range(1, tensors):
+        two.append(pass_on(two[-1]))
+    shards = [(0, 1), (1, 3)] + [(i, i + 1) for i in range(3, tensors)]
+    deep = output_weight.shape[0] // WO_PARTS
+    sums, wos, held_one, held_two = [first["sums"]], [], None, None
+    for low, high in shards[1:]:
+        out = qkv(
+            one[low:high],
+            parts[0][0],
+            gain,
+            held_one or weights,
+            held_one is None,
+            held_one is None,
+            None,
+            False,
+            pair_rows,
+            (output_weight, deep, 0) if low == 3 else None,
+            [two[0]] if held_one is None else [],
+        )
+        held_one = held_one or out["weights"]
+        sums.append(out["sums"])
+        if "extra" in out:
+            wos.append(out["extra"])
+    resids = [first["resid"]]
+    for at, (low, high) in enumerate(shards[:-1]):
+        out = qkv(
+            two[low:high],
+            parts[1][0],
+            gain,
+            held_two or weights,
+            held_two is None,
+            held_two is None,
+            sums[at],
+            low == 0,
+            pair_rows,
+            (output_weight, deep, deep) if low == 1 else None,
+        )
+        held_two = held_two or out["weights"]
+        sums[at] = out["sums"]
+        if low == 0:
+            resids.append(out["resid"])
+        if "extra" in out:
+            wos.append(out["extra"])
+    held, held_weights = two, [held_two]
+    accs, sqs = [s[0] for s in sums], [s[1] for s in sums]
+
+    args = [held[-1], gain, *held_weights[-1], *wos, *accs, *sqs, *resids]
     partial_sums = pl.pallas_call(
         functools.partial(
-            attend_kernel,
-            width,
-            length,
-            pair_rows,
-            query_weight.shape[1] // HEAD_DIM,
-            key_weight.shape[1] // HEAD_DIM,
+            tail_kernel, tensors, len(shards), len(parts), width, length, pair_rows, parts[-1][0]
         ),
-        grid_spec=pltpu.PrefetchScalarGridSpec(
-            num_scalar_prefetch=1,
-            grid=(width // block,),
-            in_specs=[whole((rows, total))] * tensors
-            + [whole((rows, LANES))] * tensors
-            + [
-                pl.BlockSpec((share, block), lambda i, t: (0, i)),
-                pl.BlockSpec((output_weight.shape[0], block), lambda i, t: (0, i)),
-            ],
-            out_specs=pl.BlockSpec(
-                (1, share, block), lambda i, t: ((i // per) ^ t[0], 0, i % per)
-            ),
-            scratch_shapes=[pltpu.VMEM((2 * share, output_weight.shape[0]), BF16)],
-        ),
+        in_specs=[IN_SMEM] + [IN_VMEM] * len(args),
+        out_specs=IN_VMEM,
         out_shape=shape((tensors, share, features), F32),
+        scratch_shapes=[pltpu.VMEM((2 * share, output_weight.shape[0]), BF16)],
         compiler_params=LIMIT,
         cost_estimate=pl.CostEstimate(
-            flops=4 * share * width * output_weight.shape[0],
-            bytes_accessed=2 * width * output_weight.shape[0],
+            flops=32 * share * width * output_weight.shape[0],
+            bytes_accessed=2 * rows * width,
             transcendentals=0,
         ),
-    )(
-        jnp.reshape(tensor, (1,)).astype(jnp.int32), *accs, *sqs, resid, output_weight
-    )
+    )(jnp.reshape(tensor, (1,)).astype(jnp.int32), *args)
     pooled = partial_sums[0]
     for step in range(1, tensors):
         swap = [(i, i ^ step) for i in range(tensors)]

time: 183 us -> 122 us (0.67)
  Pallas kernels: 103 us -> 42.9 us
  blocking collectives: 19.1 us -> 36.2 us
  waiting for transfers between devices: 24.6 us -> 12.9 us
  starting transfers between devices: 18.5 us -> 11.9 us
    pallas_call x11 -> x8, Pallas kernels: 64.4 us -> 34.4 us  [the longest x5 24 us: qkv(): pl.pallas_call(functools.partial(qkv_kernel, len(xs), first, loads, keep,...]
    pallas_call x1, Pallas kernels: 27.1 us -> 3.92 us  [on_device(): pl.pallas_call(functools.partial(plan_kernel, groups, share, cap, rows_he...]
    all_to_all x0 -> x1, blocking collectives: none -> 15.5 us  [exchange(): lax.all_to_all(send, 'group', split_axis=0, concat_axis=0, tiled=True)]
    all_to_all x2 -> x1, waiting for transfers between devices: 11.9 us -> 0.01 us  [exchange(): lax.all_to_all(send, 'group', split_axis=0, concat_axis=0, tiled=True)]
    pallas_call x1, Pallas kernels: 10.1 us -> 3.17 us  [on_device(): pl.pallas_call(functools.partial(gather_kernel, rows_here, cells, first,...]
    all_to_all x2 -> x1, starting transfers between devices: 7.1 us -> 3.5 us  [exchange(): lax.all_to_all(send, 'group', split_axis=0, concat_axis=0, tiled=True)]
    ppermute x6, starting transfers between devices: 7.81 us -> 4.88 us  [pass_on(): return lax.ppermute(x, 'tensor', ring)]
  transfers between devices with their start and end apart: 11 -> 10, of which waited for: 5 -> 6; matrix products, arithmetic and copies ran while one was open for 0% -> 0% of each run, Pallas kernels for 31% -> 23%
where the time goes in v2:
time: 122 us; the launch traced here: 121 us
  Pallas kernels  42.9 us (35%)
  blocking collectives  36.2 us (30%)
  between operations  15.7 us (13%)
  waiting for transfers between devices  12.9 us (11%)
  starting transfers between devices  11.9 us (10%)
    pallas_call x5, Pallas kernels, qkv(): pl.pallas_call(functools.partial(qkv_kernel, len(xs), first, loads, keep,...  24 us
    all_to_all x1, blocking collectives, exchange(): lax.all_to_all(send, 'group', split_axis=0, concat_axis=0, tiled=True)  15.5 us
    all_gather x1, blocking collectives, on_device(): everyone = lax.all_gather(pooled, 'group', tiled=True)  10.4 us
    all_gather x1, blocking collectives, on_device(): codes = lax.all_gather(code, 'group', tiled=True)  10.3 us
    ppermute x6, waiting for transfers between devices, pass_on(): return lax.ppermute(x, 'tensor', ring)  9.7 us
    pallas_call x1, Pallas kernels, on_device(): pl.pallas_call(functools.partial(tail_kernel, tensors, len(shards), len(p...  7.69 us
    ppermute x6, starting transfers between devices, pass_on(): return lax.ppermute(x, 'tensor', ring)  4.88 us
    pallas_call x1, Pallas kernels, on_device(): pl.pallas_call(functools.partial(plan_kernel, groups, share, cap, rows_he...  3.92 us
  transfers between devices with their start and end apart: 10, of which 6 were waited for; matrix products, arithmetic and copies ran while one was open for 0% of the time, Pallas kernels for 23%

profile of v2, /device:TPU:0, one launch (start us, length us, event | category | flops | bytes accessed | tf_op | source)
XLA Modules:
  0.0 121.0 jit_solution(4923960815860007675)
XLA Ops:
  7.2 0.0 copy-start.5
  8.0 0.7 compare_select_fusion.6
  8.7 0.1 tile.10
  8.8 0.0 copy-start.7
  8.8 10.3 %all-gather = s32[8,1,128]{2,1,0:T(1,128)S(1)} all-gather(s32[1,1,128]{2,1,0:T(1,128)S(1)} %fusion.46), channel_id=1, replica_groups=mesh['group'=8,'tensor'=4] {'group'}, dimensions={0}, use_global_device_ids=true | all-gather | bytes 4608 | tf_op jit(solution)/shard_map/all_gather | solution.py:601
  19.1 3.9 %shard_map.135 = (s32[8,128]{1,0:T(8,128)S(1)}, bf16[40,2,5120]{2,1,0:T(2,128)(2,1)S(1)}) custom-call(s32[1]{0:T(128)} %bitcast.35.me, s32[8,128]{1,0:T(8,128)S(1)} %bitcast.114, bf16[64,2,8192]{2,1,0:T(2,128)(2,1)} %left.3, bf16[64,2,8192]{2,1,0:T(2,128)(2,1)} %right.3), custom_call_target="tpu_custom_call" | custom-call | tf_op jit(solution)/shard_map/pallas_call | solution.py:606
  23.1 0.0 copy-start.9
  23.1 15.5 %all_to_all.44.got = bf16[40,2,5120]{2,1,0:T(2,128)(2,1)S(1)} all-to-all(bf16[40,2,5120]{2,1,0:T(2,128)(2,1)S(1)} %get-tuple-element.67), channel_id=1, replica_groups=mesh['group'=8,'tensor'=4] {'group'}, dimensions={0} | all-to-all | bytes 1638400 | tf_op jit(solution)/shard_map/all_to_all | solution.py:635
  38.6 1.5 %shard_map.137.refs_0_ = bf16[32,5120]{1,0:T(8,128)(2,1)S(1)} custom-call(s32[8,128]{1,0:T(8,128)S(1)} %get-tuple-element.66.plan, bf16[40,2,5120]{2,1,0:T(2,128)(2,1)S(1)} %all_to_all.44.got), custom_call_target="tpu_custom_call" | custom-call | tf_op jit(solution)/shard_map/pallas_call | solution.py:639
  40.1 1.6 %collective-permute-start = (bf16[32,5120]{1,0:T(8,128)(2,1)S(1)}, bf16[32,5120]{1,0:T(8,128)(2,1)S(1)}, u32[]{:S(2)}, u32[]{:S(2)}) collective-permute-start(bf16[32,5120]{1,0:T(8,128)(2,1)S(1)} %shard_map.137.refs_0_), channel_id=1, source_target_pairs={{0,1},{1,2},{2,3},{3,0},{4,5},{5,6},{6,7},{7,4},{8,9},{9,10},{10,1... | collective-permute-start | bytes 983048 | tf_op jit(solution)/shard_map/ppermute | solution.py:652
  41.7 0.0 copy-done.5
  41.7 0.0 copy-done.7
  41.7 3.2 %shard_map.136 = bf16[40,2,3072]{2,1,0:T(2,128)(2,1)} custom-call(s32[8,128]{1,0:T(8,128)S(1)} %get-tuple-element.66.plan, bf16[64,2,8192]{2,1,0:T(2,128)(2,1)S(1)} %copy-done.5, bf16[64,2,8192]{2,1,0:T(2,128)(2,1)S(1)} %copy-done.7), custom_call_target="tpu_custom_call" | custom-call | tf_op jit(solution)/shard_map/pallas_call | solution.py:621
  44.9 3.5 %all-to-all-start.6 = ((bf16[40,2,3072]{2,1,0:T(2,128)(2,1)}), bf16[40,2,3072]{2,1,0:T(2,128)(2,1)S(1)}, u32[]{:S(2)}, u32[]{:S(2)}) async-start(bf16[40,2,3072]{2,1,0:T(2,128)(2,1)} %shard_map.136), calls=%async_computation.7 | async-start | bytes 983040 | tf_op jit(solution)/shard_map/all_to_all | solution.py:635
  48.4 3.2 %collective-permute-done.refs_1_.refs_0_ = bf16[32,5120]{1,0:T(8,128)(2,1)S(1)} collective-permute-done((bf16[32,5120]{1,0:T(8,128)(2,1)S(1)}, bf16[32,5120]{1,0:T(8,128)(2,1)S(1)}, u32[]{:S(2)}, u32[]{:S(2)}) %collective-permute-start) | collective-permute-done | bytes 327712 | tf_op jit(solution)/shard_map/ppermute | solution.py:652
  51.6 0.0 collective-permute-start.4
  51.6 0.0 copy-done.9
  51.6 6.3 %shard_map.138 = (f32[32,1536]{1,0:T(8,128)S(1)}, f32[32,128]{1,0:T(8,128)S(1)}, f32[8,5120]{1,0:T(8,128)S(1)}) custom-call(bf16[32,5120]{1,0:T(8,128)(2,1)S(1)} %shard_map.137.refs_0_, f32[1,8192]{1,0:T(1,128)S(1)} %bitcast.121, bf16[8192,1024]{1,0:T(8,128)(2,1)} %refs_3_.5, bf16[8192,256]{1,0:T(8,128)(2,1)} %refs_4_.5, bf16[8192,256]{1,0:T(8,128)(2,1)} %refs_5_.2), custom_call_target="tpu_custom_call" | custom-call | flops 4026531840 | bytes 327680 | tf_op jit(solution)/shard_map/pallas_call | solution.py:535
  57.9 0.0 all-to-all-done.6.got
  57.9 1.3 %shard_map.139.refs_0_.refs_6_ = bf16[32,3072]{1,0:T(8,128)(2,1)S(1)} custom-call(s32[8,128]{1,0:T(8,128)S(1)} %get-tuple-element.66.plan, bf16[40,2,3072]{2,1,0:T(2,128)(2,1)S(1)} %all-to-all-done.6.got, f32[32,128]{1,0:T(8,128)S(1)} %get-tuple-element.68.refs_0_.refs_6_, bf16[32,5120]{1,0:T(8,128)(2,1)S(1)} %collective-permute-done.refs_1_.refs_0_), custom_call_target="tpu_custom_call" | custom-call | tf_op jit(solution)/shard_map/pallas_call | solution.py:639
  59.2 1.5 %collective-permute-start.1 = (bf16[32,3072]{1,0:T(8,128)(2,1)S(1)}, bf16[32,3072]{1,0:T(8,128)(2,1)S(1)}, u32[]{:S(2)}, u32[]{:S(2)}) collective-permute-start(bf16[32,3072]{1,0:T(8,128)(2,1)S(1)} %shard_map.139.refs_0_.refs_6_), channel_id=1, source_target_pairs={{0,1},{1,2},{2,3},{3,0},{4,5},{5,6},{6,7},{7,4},{8,9},{9,10},{10,1... | collective-permute-start | bytes 589832 | tf_op jit(solution)/shard_map/ppermute | solution.py:652
  60.7 0.0 copy-start
  60.7 0.0 copy-start.3
  60.7 4.5 %shard_map.140 = (f32[32,1536]{1,0:T(8,128)S(1)}, f32[32,128]{1,0:T(8,128)S(1)}, f32[8,3072]{1,0:T(8,128)S(1)}, bf16[3072,1024]{1,0:T(8,128)(2,1)S(1)}, bf16[307...) custom-call(bf16[32,3072]{1,0:T(8,128)(2,1)S(1)} %shard_map.139.refs_0_.refs_6_, f32[1,8192]{1,0:T(1,128)S(1)} %bitcast.122, ...), custom_call_target="tpu_custom_call" | custom-call | flops 2415919104 | bytes 196608 | tf_op jit(solution)/shard_map/pallas_call | solution.py:535
  65.2 1.8 %collective-permute-done.1.refs_0_ = bf16[32,3072]{1,0:T(8,128)(2,1)S(1)} collective-permute-done((bf16[32,3072]{1,0:T(8,128)(2,1)S(1)}, bf16[32,3072]{1,0:T(8,128)(2,1)S(1)}, u32[]{:S(2)}, u32[]{:S(2)}) %collective-permute-start.1) | collective-permute-done | bytes 196640 | tf_op jit(solution)/shard_map/ppermute | solution.py:652
  67.0 0.0 collective-permute-start.2
  67.0 0.0 collective-permute-done.4.refs_1_
  67.0 1.8 %collective-permute-start.5 = (bf16[32,5120]{1,0:T(8,128)(2,1)S(1)}, bf16[32,5120]{1,0:T(8,128)(2,1)S(1)}, u32[]{:S(2)}, u32[]{:S(2)}) collective-permute-start(bf16[32,5120]{1,0:T(8,128)(2,1)S(1)} %collective-permute-done.4.refs_1_), channel_id=1, source_target_pairs={{0,1},{1,2},{2,3},{3,0},{4,5},{5,6},{6,7},{7,4},{8,9},{9,10},{10,1... | collective-permute-start | bytes 983048 | tf_op jit(solution)/shard_map/ppermute | solution.py:652
  68.8 0.0 copy-done
  68.8 0.0 copy-done.3
  68.8 6.0 %shard_map.141 = (f32[64,1536]{1,0:T(8,128)S(1)}, f32[64,128]{1,0:T(8,128)S(1)}, bf16[5120,1024]{1,0:T(8,128)(2,1)S(1)}, bf16[5120,256]{1,0:T(8,128)(2,1)S(1)}, bf16[5120,256]{1,0:T(8,128)(2,1)S(1)}) custom-call(bf16[32,5120]{1,0:T(8,128)(2,1)S(1)} %collective-permute-done.refs_1_.refs_0_, bf16[32,5120]{1,0:T(8,128)(2,1)S(1)} %collective-permute-done.4.refs_1_, ...), custom_call_target="tpu_custom_call" | custom-call | flops 4026531840 | bytes 655360 | tf_op jit(solution)/shard_map/pallas_call | solution.py:535
  74.8 1.8 %collective-permute-done.2.refs_1_ = bf16[32,3072]{1,0:T(8,128)(2,1)S(1)} collective-permute-done((bf16[32,3072]{1,0:T(8,128)(2,1)S(1)}, bf16[32,3072]{1,0:T(8,128)(2,1)S(1)}, u32[]{:S(2)}, u32[]{:S(2)}) %collective-permute-start.2) | collective-permute-done | bytes 196640 | tf_op jit(solution)/shard_map/ppermute | solution.py:652
  76.6 0.0 collective-permute-start.3
  76.6 3.4 %shard_map.143 = (f32[64,1536]{1,0:T(8,128)S(1)}, f32[64,128]{1,0:T(8,128)S(1)}, bf16[512,8192]{1,0:T(8,128)(2,1)S(1)}) custom-call(bf16[32,3072]{1,0:T(8,128)(2,1)S(1)} %collective-permute-done.1.refs_0_, bf16[32,3072]{1,0:T(8,128)(2,1)S(1)} %collective-permute-done.2.refs_1_, f32[1,8192]{1,0:T(1,128)S(1)} %bitcast.124, ...), custom_call_target="tpu_custom_call" | custom-call | flops 2415919104 | bytes 393216 | tf_op jit(solution)/shard_map/pallas_call | solution.py:535
  80.0 2.9 %collective-permute-done.5.refs_0_ = bf16[32,5120]{1,0:T(8,128)(2,1)S(1)} collective-permute-done((bf16[32,5120]{1,0:T(8,128)(2,1)S(1)}, bf16[32,5120]{1,0:T(8,128)(2,1)S(1)}, u32[]{:S(2)}, u32[]{:S(2)}) %collective-permute-start.5) | collective-permute-done | bytes 327712 | tf_op jit(solution)/shard_map/ppermute | solution.py:652
  83.0 3.7 %shard_map.142 = (f32[32,1536]{1,0:T(8,128)S(1)}, f32[32,128]{1,0:T(8,128)S(1)}, bf16[512,8192]{1,0:T(8,128)(2,1)S(1)}) custom-call(bf16[32,5120]{1,0:T(8,128)(2,1)S(1)} %collective-permute-done.5.refs_0_, f32[1,8192]{1,0:T(1,128)S(1)} %bitcast.125, bf16[5120,1024]{1,0:T(8,128)(2,1)S(1)} %get-tuple-element.73.refs_2_, ...), custom_call_target="tpu_custom_call" | custom-call | flops 4026531840 | bytes 327680 | tf_op jit(solution)/shard_map/pallas_call | solution.py:535
  86.7 0.0 collective-permute-done.3.x_ref
  86.7 0.0 copy-start.6
  86.7 0.0 copy-start.10
  86.7 0.0 copy-start.11
  86.7 0.0 copy-start.12
  86.8 0.0 copy-start.13
  86.8 7.7 %shard_map.144 = f32[4,8,2048]{2,1,0:T(8,128)S(1)} custom-call(s32[1]{0:T(128)} %bitcast.42.t_ref, bf16[32,3072]{1,0:T(8,128)(2,1)S(1)} %collective-permute-done.3.x_ref, f32[1,8192]{1,0:T(1,128)S(1)} %bitcast.126, bf16[3072,1024]{1,0:T(8,128)(2,1)S(1)} %get-tuple-element.70.refs_3_.wq, bf16[3072,256]{1,0:T(8,128)(2,1)S(1)} %get-tuple-element.71.refs_4_.wk, ...), custom_call_target="tpu_custom_call" | custom-call | flops 2147483648 | bytes 524288 | tf_op jit(solution)/shard_map/pallas_call | solution.py:707
  94.5 0.1 collective-permute-start.6
  94.6 1.2 %collective-permute-start.8 = (f32[8,2048]{1,0:T(8,128)S(1)}, f32[8,2048]{1,0:T(8,128)S(1)}, u32[]{:S(2)}, u32[]{:S(2)}) collective-permute-start(f32[8,2048]{1,0:T(8,128)S(1)} %get-tuple-element.149), channel_id=1, source_target_pairs={{0,3},{1,2},{2,1},{3,0},{4,7},{5,6},{6,5},{7,4},{8,11},{9,10},{10,... | collective-permute-start | bytes 196616 | tf_op jit(solution)/shard_map/ppermute | solution.py:725
  95.8 2.3 %collective-permute-start.7 = (f32[8,2048]{1,0:T(8,128)S(1)}, f32[8,2048]{1,0:T(8,128)S(1)}, u32[]{:S(2)}, u32[]{:S(2)}) collective-permute-start(f32[8,2048]{1,0:T(8,128)S(1)} %get-tuple-element.150), channel_id=1, source_target_pairs={{0,2},{1,3},{2,0},{3,1},{4,6},{5,7},{6,4},{7,5},{8,10},{9,11},{10,... | collective-permute-start | bytes 196616 | tf_op jit(solution)/shard_map/ppermute | solution.py:725
  98.0 0.5 slice.21
  99.2 0.0 collective-permute-done.6
  99.2 1.6 %collective-permute-done.8 = f32[8,2048]{1,0:T(8,128)S(1)} collective-permute-done((f32[8,2048]{1,0:T(8,128)S(1)}, f32[8,2048]{1,0:T(8,128)S(1)}, u32[]{:S(2)}, u32[]{:S(2)}) %collective-permute-start.8) | collective-permute-done | bytes 65568 | tf_op jit(solution)/shard_map/ppermute | solution.py:725
  100.8 1.6 %collective-permute-done.7 = f32[8,2048]{1,0:T(8,128)S(1)} collective-permute-done((f32[8,2048]{1,0:T(8,128)S(1)}, f32[8,2048]{1,0:T(8,128)S(1)}, u32[]{:S(2)}, u32[]{:S(2)}) %collective-permute-start.7) | collective-permute-done | bytes 65568 | tf_op jit(solution)/shard_map/ppermute | solution.py:725
  102.4 10.4 %all_gather.7 = f32[64,2048]{1,0:T(8,128)S(1)} all-gather(f32[8,2048]{1,0:T(8,128)S(1)} %fusion.45), channel_id=1, replica_groups=mesh['group'=8,'tensor'=4] {'group'}, dimensions={0}, use_global_device_ids=true | all-gather | bytes 589824 | tf_op jit(solution)/shard_map/all_gather | solution.py:726
  112.8 0.0 copy-done.6
  112.8 0.0 copy-done.10
  112.8 0.0 copy-done.11
  112.8 0.0 copy-done.12
  112.8 0.0 copy-done.13
  112.8 1.4 %conditional.1 = ((f32[64,2048]{1,0:T(8,128)}, f32[64,2048]{1,0:T(8,128)})) conditional(s32[]{:T(128)} %bitcast.41, (s32[8,128]{1,0:T(8,128)S(1)}, f32[64,2048]{1,0:T(8,128)S(1)}) %tuple.14, (s32[16,1]{0,1:T(1,128)S(1)}, s32[16]{0:T(128)S(1)}, s32[1]{0:T(128)}, bf16[64,2,8192]{2,1,0:T(2,128)(2,1)S(1)}, s32[16,1]{0,1:T(1,128)S(1)}, ...), branch_computations={%region_0.1_spmd, %region_1.13_spmd} | conditional | flops 10908157952 | bytes 268642432 | solution.py:755
  112.8 1.4 %branch_0_fun.1 = (f32[64,2048]{1,0:T(8,128)}, f32[64,2048]{1,0:T(8,128)}) custom-call(s32[8,128]{1,0:T(8,128)S(1)} %get-tuple-element.28.plan, f32[64,2048]{1,0:T(8,128)S(1)} %get-tuple-element.29.pooled), custom_call_target="tpu_custom_call" | custom-call | tf_op jit(solution)/shard_map/cond/branch_0_fun/pallas_call | solution.py:730
  (4 shorter events, 0.1 us)
Async XLA Ops:
  7.2 34.6 %copy-start.5 = (bf16[64,2,8192]{2,1,0:T(2,128)(2,1)S(1)}, bf16[64,2,8192]{2,1,0:T(2,128)(2,1)}, u32[]{:S(2)}) copy-start(bf16[64,2,8192]{2,1,0:T(2,128)(2,1)} %left.3) | copy-start | bytes 6291460
  8.8 33.0 %copy-start.7 = (bf16[64,2,8192]{2,1,0:T(2,128)(2,1)S(1)}, bf16[64,2,8192]{2,1,0:T(2,128)(2,1)}, u32[]{:S(2)}) copy-start(bf16[64,2,8192]{2,1,0:T(2,128)(2,1)} %right.3) | copy-start | bytes 6291460
  23.1 28.5 %copy-start.9 = (f32[8192]{0:T(1024)S(1)}, f32[8192]{0:T(1024)}, u32[]{:S(2)}) copy-start(f32[8192]{0:T(1024)} %param.21) | copy-start | bytes 98308
  40.1 11.5 %collective-permute-start = (bf16[32,5120]{1,0:T(8,128)(2,1)S(1)}, bf16[32,5120]{1,0:T(8,128)(2,1)S(1)}, u32[]{:S(2)}, u32[]{:S(2)}) collective-permute-start(bf16[32,5120]{1,0:T(8,128)(2,1)S(1)} %shard_map.137.refs_0_), channel_id=1, source_target_pairs={{0,1},{1,2},{2,3},{3,0},{4,5},{5,6},{6,7},{7,4},{8,9},{9,10},{10,1... | collective-permute-start | bytes 983048 | tf_op jit(solution)/shard_map/ppermute | solution.py:652
  44.9 13.0 %all-to-all-start.6 = ((bf16[40,2,3072]{2,1,0:T(2,128)(2,1)}), bf16[40,2,3072]{2,1,0:T(2,128)(2,1)S(1)}, u32[]{:S(2)}, u32[]{:S(2)}) async-start(bf16[40,2,3072]{2,1,0:T(2,128)(2,1)} %shard_map.136), calls=%async_computation.7 | async-start | bytes 983040 | tf_op jit(solution)/shard_map/all_to_all | solution.py:635
  51.6 15.4 %collective-permute-start.4 = (bf16[32,5120]{1,0:T(8,128)(2,1)S(1)}, bf16[32,5120]{1,0:T(8,128)(2,1)S(1)}, u32[]{:S(2)}, u32[]{:S(2)}) collective-permute-start(bf16[32,5120]{1,0:T(8,128)(2,1)S(1)} %collective-permute-done.refs_1_.refs_0_), channel_id=1, source_target_pairs={{0,1},{1,2},{2,3},{3,0},{4,5},{5,6},{6,7},{7,4},{8,9},{9,10},{10,1... | collective-permute-start | bytes 983048 | tf_op jit(solution)/shard_map/ppermute | solution.py:652
  59.2 7.8 %collective-permute-start.1 = (bf16[32,3072]{1,0:T(8,128)(2,1)S(1)}, bf16[32,3072]{1,0:T(8,128)(2,1)S(1)}, u32[]{:S(2)}, u32[]{:S(2)}) collective-permute-start(bf16[32,3072]{1,0:T(8,128)(2,1)S(1)} %shard_map.139.refs_0_.refs_6_), channel_id=1, source_target_pairs={{0,1},{1,2},{2,3},{3,0},{4,5},{5,6},{6,7},{7,4},{8,9},{9,10},{10,1... | collective-permute-start | bytes 589832 | tf_op jit(solution)/shard_map/ppermute | solution.py:652
  60.7 8.1 %copy-start = (bf16[8192,256]{1,0:T(8,128)(2,1)S(1)}, bf16[8192,256]{1,0:T(8,128)(2,1)}, u32[]{:S(2)}) copy-start(bf16[8192,256]{1,0:T(8,128)(2,1)} %refs_4_.5) | copy-start | bytes 12582916
  60.7 8.1 %copy-start.3 = (bf16[8192,256]{1,0:T(8,128)(2,1)S(1)}, bf16[8192,256]{1,0:T(8,128)(2,1)}, u32[]{:S(2)}) copy-start(bf16[8192,256]{1,0:T(8,128)(2,1)} %refs_5_.2) | copy-start | bytes 12582916
  67.0 9.6 %collective-permute-start.2 = (bf16[32,3072]{1,0:T(8,128)(2,1)S(1)}, bf16[32,3072]{1,0:T(8,128)(2,1)S(1)}, u32[]{:S(2)}, u32[]{:S(2)}) collective-permute-start(bf16[32,3072]{1,0:T(8,128)(2,1)S(1)} %collective-permute-done.1.refs_0_), channel_id=1, source_target_pairs={{0,1},{1,2},{2,3},{3,0},{4,5},{5,6},{6,7},{7,4},{8,9},{9,10},{10,1... | collective-permute-start | bytes 589832 | tf_op jit(solution)/shard_map/ppermute | solution.py:652
  67.0 15.9 %collective-permute-start.5 = (bf16[32,5120]{1,0:T(8,128)(2,1)S(1)}, bf16[32,5120]{1,0:T(8,128)(2,1)S(1)}, u32[]{:S(2)}, u32[]{:S(2)}) collective-permute-start(bf16[32,5120]{1,0:T(8,128)(2,1)S(1)} %collective-permute-done.4.refs_1_), channel_id=1, source_target_pairs={{0,1},{1,2},{2,3},{3,0},{4,5},{5,6},{6,7},{7,4},{8,9},{9,10},{10,1... | collective-permute-start | bytes 983048 | tf_op jit(solution)/shard_map/ppermute | solution.py:652
  76.6 10.1 %collective-permute-start.3 = (bf16[32,3072]{1,0:T(8,128)(2,1)S(1)}, bf16[32,3072]{1,0:T(8,128)(2,1)S(1)}, u32[]{:S(2)}, u32[]{:S(2)}) collective-permute-start(bf16[32,3072]{1,0:T(8,128)(2,1)S(1)} %collective-permute-done.2.refs_1_), channel_id=1, source_target_pairs={{0,1},{1,2},{2,3},{3,0},{4,5},{5,6},{6,7},{7,4},{8,9},{9,10},{10,1... | collective-permute-start | bytes 589832 | tf_op jit(solution)/shard_map/ppermute | solution.py:652
  86.7 26.1 %copy-start.6 = (bf16[64,2,8192]{2,1,0:T(2,128)(2,1)S(1)}, bf16[64,2,8192]{2,1,0:T(2,128)(2,1)}, u32[]{:S(2)}) copy-start(bf16[64,2,8192]{2,1,0:T(2,128)(2,1)} %left.3) | copy-start | bytes 6291460
  86.7 26.1 %copy-start.10 = (s32[16,1]{0,1:T(1,128)S(1)}, s32[16,1]{0,1:T(1,128)}, u32[]{:S(2)}) copy-start(s32[16,1]{0,1:T(1,128)} %param.18) | copy-start | bytes 196
  86.7 26.0 %copy-start.11 = (s32[16,1]{0,1:T(1,128)S(1)}, s32[16,1]{0,1:T(1,128)}, u32[]{:S(2)}) copy-start(s32[16,1]{0,1:T(1,128)} %param.16) | copy-start | bytes 196
  86.7 26.0 %copy-start.12 = (s32[16]{0:T(128)S(1)}, s32[16]{0:T(128)}, u32[]{:S(2)}) copy-start(s32[16]{0:T(128)} %param.19) | copy-start | bytes 196
  86.8 26.0 %copy-start.13 = (s32[16]{0:T(128)S(1)}, s32[16]{0:T(128)}, u32[]{:S(2)}) copy-start(s32[16]{0:T(128)} %param.17) | copy-start | bytes 196
  94.5 4.7 %collective-permute-start.6 = (f32[8,2048]{1,0:T(8,128)S(1)}, f32[8,2048]{1,0:T(8,128)S(1)}, u32[]{:S(2)}, u32[]{:S(2)}) collective-permute-start(f32[8,2048]{1,0:T(8,128)S(1)} %get-tuple-element.148), channel_id=1, source_target_pairs={{0,1},{1,0},{2,3},{3,2},{4,5},{5,4},{6,7},{7,6},{8,9},{9,8},{10,11... | collective-permute-start | bytes 196616 | tf_op jit(solution)/shard_map/ppermute | solution.py:725
  94.6 6.2 %collective-permute-start.8 = (f32[8,2048]{1,0:T(8,128)S(1)}, f32[8,2048]{1,0:T(8,128)S(1)}, u32[]{:S(2)}, u32[]{:S(2)}) collective-permute-start(f32[8,2048]{1,0:T(8,128)S(1)} %get-tuple-element.149), channel_id=1, source_target_pairs={{0,3},{1,2},{2,1},{3,0},{4,7},{5,6},{6,5},{7,4},{8,11},{9,10},{10,... | collective-permute-start | bytes 196616 | tf_op jit(solution)/shard_map/ppermute | solution.py:725
  95.8 6.6 %collective-permute-start.7 = (f32[8,2048]{1,0:T(8,128)S(1)}, f32[8,2048]{1,0:T(8,128)S(1)}, u32[]{:S(2)}, u32[]{:S(2)}) collective-permute-start(f32[8,2048]{1,0:T(8,128)S(1)} %get-tuple-element.150), channel_id=1, source_target_pairs={{0,2},{1,3},{2,0},{3,1},{4,6},{5,7},{6,4},{7,5},{8,10},{9,11},{10,... | collective-permute-start | bytes 196616 | tf_op jit(solution)/shard_map/ppermute | solution.py:725

commit v3 on v2

--- a/solution.py
+++ b/solution.py
@@ -123,7 +123,9 @@
     context = context.reshape(pairs_here * length, kv_local * share * HEAD_DIM)
     attended = jnp.dot(context, output_weight, preferred_element_type=jnp.float32)
     head_term = jnp.mean(attended.reshape(pairs_here, length, width), axis=1)
-    head_part = lax.psum_scatter(head_term, "tensor", scatter_dimension=1, tiled=True)
+    shares = head_term.reshape(pairs_here, tensors, feature_share).swapaxes(0, 1)
+    shares = lax.all_to_all(shares, "tensor", split_axis=0, concat_axis=0, tiled=True)
+    head_part = jnp.sum(shares, axis=0)
     feature_start = lax.axis_index("tensor") * feature_share
     own_features = lax.dynamic_slice_in_dim(inputs, feature_start, feature_share, 2)
     residual_mean = jnp.mean(own_features.astype(jnp.float32), axis=1)
@@ -169,14 +171,6 @@
 def column(row):
     n = row.shape[1]
     return jnp.transpose(jnp.broadcast_to(row, (n, n)))[:, :1]
-
-
-def split3(wide):
-    high = wide.astype(BF16)
-    rest = wide - high.astype(F32)
-    mid = rest.astype(BF16)
-    low = (rest - mid.astype(F32)).astype(BF16)
-    return (high, mid, low)
 
 
 def plan_body(codes, me, groups, share, cap, rows_here):
@@ -284,8 +278,8 @@
     lax.fori_loop(0, cells, finish, 0)
 
 
-def plan_kernel(groups, share, cap, rows_here, wide, me, codes, left, right, plan_out, out, plan, sem, sems):
-    rows = jnp.sum(codes[...], axis=0, keepdims=True)
+def plan_kernel(groups, share, cap, rows_here, wide, me, mine, others, left, right, plan_out, out, plan, sem, sems):
+    rows = mine[...] + others[...]
     table = plan_body(rows, me[0], groups, share, cap, rows_here)
     for at, row in enumerate(table):
         plan_out[pl.ds(at, 1), :] = row
@@ -401,7 +395,7 @@
 ):
     wos, refs = refs[:WO_PARTS], refs[WO_PARTS:]
     accs, sqs, resids = refs[:groups], refs[groups : 2 * groups], refs[2 * groups : 2 * groups + parts]
-    out, ctx = refs[2 * groups + parts :]
+    outs, (ctx, out) = refs[2 * groups + parts : -2], refs[-2:]
     pairs, features = out.shape[1:]
     heads, kv_heads = wq.shape[1] // HEAD_DIM, wk.shape[1] // HEAD_DIM
     share = heads // kv_heads
@@ -481,15 +475,21 @@
 
         lax.fori_loop(0, resid.shape[1] // block, one, 0)
         done += resid.shape[1]
-
-
-def final_kernel(plan, pooled, left, right):
+    for i, piece in enumerate(outs):
+        piece[...] = out[i].astype(piece.dtype)
+
+
+def final_kernel(plan, pooled, left, right, held, sems):
     rows, n = left.shape[0], pooled.shape[0]
-    parts = split3(pooled[...])
     at = lax.broadcasted_iota(jnp.int32, (rows, n), 0)
-    for line, out in ((2, left), (3, right)):
-        hit = (plan[pl.ds(line, 1), :][:, :n] == at).astype(BF16)
-        out[...] = sum(jnp.dot(hit, part, preferred_element_type=F32) for part in parts)
+    copies = []
+    for side, out in enumerate((left, right)):
+        hit = (plan[pl.ds(2 + side, 1), :][:, :n] == at).astype(BF16)
+        held[side] = jnp.dot(hit, pooled[...], preferred_element_type=F32)
+        copies.append(pltpu.make_async_copy(held.at[side], out, sems.at[side]))
+        copies[-1].start()
+    for copy in copies:
+        copy.wait()
 
 
 ANY = pl.BlockSpec(memory_space=pl.ANY)
@@ -598,14 +598,17 @@
     code = jnp.where(jnp.arange(pairs_here, dtype=jnp.int32) < pair_count[0], code, DEAD)
     at = jnp.arange(n, dtype=jnp.int32) // pairs_here
     code = jnp.where(at == group, jnp.tile(code, groups), 0)[None, :]
-    codes = lax.all_gather(code, "group", tiled=True)
+    hop = 1
+    while hop < groups:
+        codes = [code, lax.ppermute(code, "group", [(i, i ^ hop) for i in range(groups)])]
+        code, hop = codes[0] + codes[1], 2 * hop
 
     head = width * 5 // 8
     parts = ((0, head), (head, width - head))
     me = jnp.reshape(group, (1,)).astype(jnp.int32)
     plan, cell_rows = pl.pallas_call(
         functools.partial(plan_kernel, groups, share, cap, rows_here, parts[0][1]),
-        in_specs=[IN_SMEM, IN_VMEM, ANY, ANY],
+        in_specs=[IN_SMEM, IN_VMEM, IN_VMEM, ANY, ANY],
         out_specs=[IN_VMEM, IN_VMEM],
         out_shape=[shape((8, LANES), jnp.int32), shape((cells, toks, parts[0][1]), BF16)],
         scratch_shapes=[
@@ -614,7 +617,7 @@
             pltpu.SemaphoreType.DMA((cells,)),
         ],
         compiler_params=LIMIT,
-    )(me, codes, left_table, right_table)
+    )(me, *codes, left_table, right_table)
     sends = [cell_rows]
     for first, wide in parts[1:]:
         sends.append(
@@ -709,9 +712,13 @@
             tail_kernel, tensors, len(shards), len(parts), width, length, pair_rows, parts[-1][0]
         ),
         in_specs=[IN_SMEM] + [IN_VMEM] * len(args),
-        out_specs=IN_VMEM,
-        out_shape=shape((tensors, share, features), F32),
-        scratch_shapes=[pltpu.VMEM((2 * share, output_weight.shape[0]), BF16)],
+        out_specs=[IN_VMEM] * tensors,
+        out_shape=[shape((share, features), F32)]
+        + [shape((share, features), BF16)] * (tensors - 1),
+        scratch_shapes=[
+            pltpu.VMEM((2 * share, output_weight.shape[0]), BF16),
+            pltpu.VMEM((tensors, share, features), F32),
+        ],
         compiler_params=LIMIT,
         cost_estimate=pl.CostEstimate(
             flops=32 * share * width * output_weight.shape[0],
@@ -722,16 +729,20 @@
     pooled = partial_sums[0]
     for step in range(1, tensors):
         swap = [(i, i ^ step) for i in range(tensors)]
-        pooled = pooled + lax.ppermute(partial_sums[step], "tensor", swap)
-    everyone = lax.all_gather(pooled, "group", tiled=True)
+        pooled = pooled + lax.ppermute(partial_sums[step], "tensor", swap).astype(F32)
+    everyone = lax.all_gather(pooled.astype(BF16), "group", tiled=True)
 
     def fast():
         return tuple(
             pl.pallas_call(
                 final_kernel,
                 in_specs=[IN_VMEM, IN_VMEM],
-                out_specs=[IN_VMEM, IN_VMEM],
-                out_shape=[shape((rows_here, features), F32)] * 2,
+                out_specs=[ANY, ANY],
+                out_shape=[pltpu.HBM((rows_here, features), F32)] * 2,
+                scratch_shapes=[
+                    pltpu.VMEM((2, rows_here, features), F32),
+                    pltpu.SemaphoreType.DMA((2,)),
+                ],
                 compiler_params=LIMIT,
             )(plan, everyone)
         )

time: 122 us -> 107 us (0.88)
  between operations: 15.7 us -> 2.48 us
  blocking collectives: 36.2 us -> 26.3 us
  starting transfers between devices: 11.9 us -> 18.4 us
  waiting for transfers between devices: 12.9 us -> 14.9 us
    all_gather x2 -> x1, blocking collectives: 20.7 us -> 9.44 us  [on_device(): everyone = lax.all_gather(pooled.astype(BF16), 'group', tiled=True)]
    ppermute x3 -> x6, starting transfers between devices: 3.55 us -> 9.87 us  [the longest x3 5.42 us: on_device(): lax.ppermute(code, 'group', [(i, i ^ hop) for i in range(groups)])]
    ppermute x3 -> x6, waiting for transfers between devices: 3.17 us -> 5.53 us  [the longest x3 3.86 us: on_device(): lax.ppermute(code, 'group', [(i, i ^ hop) for i in range(groups)])]
    all_to_all x1, blocking collectives: 15.5 us -> 16.9 us  [exchange(): lax.all_to_all(send, 'group', split_axis=0, concat_axis=0, tiled=True)]
  transfers between devices with their start and end apart: 10 -> 13, of which waited for: 6 -> 9; matrix products, arithmetic and copies ran while one was open for 0% -> 0% of each run, Pallas kernels for 23% -> 27%
where the time goes in v3:
time: 107 us
  Pallas kernels  43.2 us (40%)
  blocking collectives  26.3 us (25%)
  starting transfers between devices  18.4 us (17%)
  waiting for transfers between devices  14.9 us (14%)
  between operations  2.48 us (2%)
    pallas_call x5, Pallas kernels, qkv(): pl.pallas_call(functools.partial(qkv_kernel, len(xs), first, loads, keep,...  24 us
    all_to_all x1, blocking collectives, exchange(): lax.all_to_all(send, 'group', split_axis=0, concat_axis=0, tiled=True)  16.9 us
    all_gather x1, blocking collectives, on_device(): everyone = lax.all_gather(pooled.astype(BF16), 'group', tiled=True)  9.44 us
    ppermute x6, waiting for transfers between devices, pass_on(): return lax.ppermute(x, 'tensor', ring)  9.27 us
    pallas_call x1, Pallas kernels, on_device(): pl.pallas_call(functools.partial(tail_kernel, tensors, len(shards), len(p...  7.72 us
    ppermute x3, starting transfers between devices, on_device(): lax.ppermute(code, 'group', [(i, i ^ hop) for i in range(groups)])  5.42 us
    ppermute x6, starting transfers between devices, pass_on(): return lax.ppermute(x, 'tensor', ring)  5.03 us
    ppermute x3, starting transfers between devices, on_device(): lax.ppermute(partial_sums[step], 'tensor', swap).astype(F32)  4.44 us
  transfers between devices with their start and end apart: 13, of which 9 were waited for; matrix products, arithmetic and copies ran while one was open for 0% of the time, Pallas kernels for 27%

profile of v3, /device:TPU:0, one launch (start us, length us, event | category | flops | bytes accessed | tf_op | source)
XLA Modules:
  0.0 106.9 jit_solution(9615739354402293367)
XLA Ops:
  0.6 0.0 copy-start.5
  1.4 0.7 compare_select_fusion.6
  2.2 0.1 tile.10
  2.2 0.0 copy-start.7
  2.3 0.5 collective-permute-start
  2.8 0.8 collective-permute-done
  3.6 2.9 %collective-permute-start.1 = (s32[1,128]{1,0:T(1,128)S(1)}, s32[1,128]{1,0:T(1,128)S(1)}, u32[]{:S(2)}, u32[]{:S(2)}) collective-permute-start(s32[1,128]{1,0:T(1,128)S(1)} %fusion.53), channel_id=1, source_target_pairs={{0,8},{4,12},{8,0},{12,4},{16,24},{20,28},{24,16},{28,20},{1,9},{5... | collective-permute-start | bytes 1544 | tf_op jit(solution)/shard_map/ppermute | solution.py:603
  6.5 1.5 %collective-permute-done.1 = s32[1,128]{1,0:T(1,128)S(1)} collective-permute-done((s32[1,128]{1,0:T(1,128)S(1)}, s32[1,128]{1,0:T(1,128)S(1)}, u32[]{:S(2)}, u32[]{:S(2)}) %collective-permute-start.1) | collective-permute-done | bytes 544 | tf_op jit(solution)/shard_map/ppermute | solution.py:603
  8.0 2.0 %collective-permute-start.2 = (s32[1,128]{1,0:T(1,128)S(1)}, s32[1,128]{1,0:T(1,128)S(1)}, u32[]{:S(2)}, u32[]{:S(2)}) collective-permute-start(s32[1,128]{1,0:T(1,128)S(1)} %add.112.mine), channel_id=1, source_target_pairs={{0,16},{4,20},{8,24},{12,28},{16,0},{20,4},{24,8},{28,12},{1,17},{... | collective-permute-start | bytes 1544 | tf_op jit(solution)/shard_map/ppermute | solution.py:603
  10.0 1.5 %collective-permute-done.2.others = s32[1,128]{1,0:T(1,128)S(1)} collective-permute-done((s32[1,128]{1,0:T(1,128)S(1)}, s32[1,128]{1,0:T(1,128)S(1)}, u32[]{:S(2)}, u32[]{:S(2)}) %collective-permute-start.2) | collective-permute-done | bytes 544 | tf_op jit(solution)/shard_map/ppermute | solution.py:603
  11.6 4.2 %shard_map.135 = (s32[8,128]{1,0:T(8,128)S(1)}, bf16[40,2,5120]{2,1,0:T(2,128)(2,1)S(1)}) custom-call(s32[1]{0:T(128)} %bitcast.36.me, s32[1,128]{1,0:T(1,128)S(1)} %add.112.mine, s32[1,128]{1,0:T(1,128)S(1)} %collective-permute-done.2.others, bf16[64,2,8192]{2,1,0:T(2,128)(2,1)} %left.3, bf16[64,2,8192]{2,1,0:T(2,128)(2,1)} %right.3), custom_call_target="tpu_custom_call" | custom-call | tf_op jit(solution)/shard_map/pallas_call | solution.py:609
  15.7 0.0 copy-start.9
  15.7 16.9 %all_to_all.48.got = bf16[40,2,5120]{2,1,0:T(2,128)(2,1)S(1)} all-to-all(bf16[40,2,5120]{2,1,0:T(2,128)(2,1)S(1)} %get-tuple-element.71), channel_id=1, replica_groups=mesh['group'=8,'tensor'=4] {'group'}, dimensions={0} | all-to-all | bytes 1638400 | tf_op jit(solution)/shard_map/all_to_all | solution.py:638
  32.6 1.5 %shard_map.137.refs_0_ = bf16[32,5120]{1,0:T(8,128)(2,1)S(1)} custom-call(s32[8,128]{1,0:T(8,128)S(1)} %get-tuple-element.70.plan, bf16[40,2,5120]{2,1,0:T(2,128)(2,1)S(1)} %all_to_all.48.got), custom_call_target="tpu_custom_call" | custom-call | tf_op jit(solution)/shard_map/pallas_call | solution.py:642
  34.1 1.6 %collective-permute-start.3 = (bf16[32,5120]{1,0:T(8,128)(2,1)S(1)}, bf16[32,5120]{1,0:T(8,128)(2,1)S(1)}, u32[]{:S(2)}, u32[]{:S(2)}) collective-permute-start(bf16[32,5120]{1,0:T(8,128)(2,1)S(1)} %shard_map.137.refs_0_), channel_id=1, source_target_pairs={{0,1},{1,2},{2,3},{3,0},{4,5},{5,6},{6,7},{7,4},{8,9},{9,10},{10,1... | collective-permute-start | bytes 983048 | tf_op jit(solution)/shard_map/ppermute | solution.py:655
  35.8 0.0 copy-done.5
  35.8 0.0 copy-done.7
  35.8 3.4 %shard_map.136 = bf16[40,2,3072]{2,1,0:T(2,128)(2,1)} custom-call(s32[8,128]{1,0:T(8,128)S(1)} %get-tuple-element.70.plan, bf16[64,2,8192]{2,1,0:T(2,128)(2,1)S(1)} %copy-done.5, bf16[64,2,8192]{2,1,0:T(2,128)(2,1)S(1)} %copy-done.7), custom_call_target="tpu_custom_call" | custom-call | tf_op jit(solution)/shard_map/pallas_call | solution.py:624
  39.1 3.5 %all-to-all-start.7 = ((bf16[40,2,3072]{2,1,0:T(2,128)(2,1)}), bf16[40,2,3072]{2,1,0:T(2,128)(2,1)S(1)}, u32[]{:S(2)}, u32[]{:S(2)}) async-start(bf16[40,2,3072]{2,1,0:T(2,128)(2,1)} %shard_map.136), calls=%async_computation.7 | async-start | bytes 983040 | tf_op jit(solution)/shard_map/all_to_all | solution.py:638
  42.6 3.0 %collective-permute-done.3.refs_1_.refs_0_ = bf16[32,5120]{1,0:T(8,128)(2,1)S(1)} collective-permute-done((bf16[32,5120]{1,0:T(8,128)(2,1)S(1)}, bf16[32,5120]{1,0:T(8,128)(2,1)S(1)}, u32[]{:S(2)}, u32[]{:S(2)}) %collective-permute-start.3) | collective-permute-done | bytes 327712 | tf_op jit(solution)/shard_map/ppermute | solution.py:655
  45.6 0.0 collective-permute-start.7
  45.6 0.0 copy-done.9
  45.6 6.3 %shard_map.138 = (f32[32,1536]{1,0:T(8,128)S(1)}, f32[32,128]{1,0:T(8,128)S(1)}, f32[8,5120]{1,0:T(8,128)S(1)}) custom-call(bf16[32,5120]{1,0:T(8,128)(2,1)S(1)} %shard_map.137.refs_0_, f32[1,8192]{1,0:T(1,128)S(1)} %bitcast.104, bf16[8192,1024]{1,0:T(8,128)(2,1)} %refs_3_.5, bf16[8192,256]{1,0:T(8,128)(2,1)} %refs_4_.5, bf16[8192,256]{1,0:T(8,128)(2,1)} %refs_5_.2), custom_call_target="tpu_custom_call" | custom-call | flops 4026531840 | bytes 327680 | tf_op jit(solution)/shard_map/pallas_call | solution.py:535
  51.9 0.1 all-to-all-done.7.got
  52.0 1.3 %shard_map.139.refs_0_.refs_6_ = bf16[32,3072]{1,0:T(8,128)(2,1)S(1)} custom-call(s32[8,128]{1,0:T(8,128)S(1)} %get-tuple-element.70.plan, bf16[40,2,3072]{2,1,0:T(2,128)(2,1)S(1)} %all-to-all-done.7.got, f32[32,128]{1,0:T(8,128)S(1)} %get-tuple-element.72.refs_0_.refs_6_, bf16[32,5120]{1,0:T(8,128)(2,1)S(1)} %collective-permute-done.3.refs_1_.refs_0_), custom_call_target="tpu_custom_call" | custom-call | tf_op jit(solution)/shard_map/pallas_call | solution.py:642
  53.3 1.6 %collective-permute-start.4 = (bf16[32,3072]{1,0:T(8,128)(2,1)S(1)}, bf16[32,3072]{1,0:T(8,128)(2,1)S(1)}, u32[]{:S(2)}, u32[]{:S(2)}) collective-permute-start(bf16[32,3072]{1,0:T(8,128)(2,1)S(1)} %shard_map.139.refs_0_.refs_6_), channel_id=1, source_target_pairs={{0,1},{1,2},{2,3},{3,0},{4,5},{5,6},{6,7},{7,4},{8,9},{9,10},{10,1... | collective-permute-start | bytes 589832 | tf_op jit(solution)/shard_map/ppermute | solution.py:655
  54.9 0.0 copy-start
  54.9 0.0 copy-start.3
  54.9 4.5 %shard_map.140 = (f32[32,1536]{1,0:T(8,128)S(1)}, f32[32,128]{1,0:T(8,128)S(1)}, f32[8,3072]{1,0:T(8,128)S(1)}, bf16[3072,1024]{1,0:T(8,128)(2,1)S(1)}, bf16[307...) custom-call(bf16[32,3072]{1,0:T(8,128)(2,1)S(1)} %shard_map.139.refs_0_.refs_6_, f32[1,8192]{1,0:T(1,128)S(1)} %bitcast.105, ...), custom_call_target="tpu_custom_call" | custom-call | flops 2415919104 | bytes 196608 | tf_op jit(solution)/shard_map/pallas_call | solution.py:535
  59.4 1.6 %collective-permute-done.4.refs_0_ = bf16[32,3072]{1,0:T(8,128)(2,1)S(1)} collective-permute-done((bf16[32,3072]{1,0:T(8,128)(2,1)S(1)}, bf16[32,3072]{1,0:T(8,128)(2,1)S(1)}, u32[]{:S(2)}, u32[]{:S(2)}) %collective-permute-start.4) | collective-permute-done | bytes 196640 | tf_op jit(solution)/shard_map/ppermute | solution.py:655
  61.0 0.0 collective-permute-start.5
  61.0 0.0 collective-permute-done.7.refs_1_
  61.1 1.8 %collective-permute-start.8 = (bf16[32,5120]{1,0:T(8,128)(2,1)S(1)}, bf16[32,5120]{1,0:T(8,128)(2,1)S(1)}, u32[]{:S(2)}, u32[]{:S(2)}) collective-permute-start(bf16[32,5120]{1,0:T(8,128)(2,1)S(1)} %collective-permute-done.7.refs_1_), channel_id=1, source_target_pairs={{0,1},{1,2},{2,3},{3,0},{4,5},{5,6},{6,7},{7,4},{8,9},{9,10},{10,1... | collective-permute-start | bytes 983048 | tf_op jit(solution)/shard_map/ppermute | solution.py:655
  62.8 0.0 copy-done
  62.8 0.0 copy-done.3
  62.8 6.0 %shard_map.141 = (f32[64,1536]{1,0:T(8,128)S(1)}, f32[64,128]{1,0:T(8,128)S(1)}, bf16[5120,1024]{1,0:T(8,128)(2,1)S(1)}, bf16[5120,256]{1,0:T(8,128)(2,1)S(1)}, bf16[5120,256]{1,0:T(8,128)(2,1)S(1)}) custom-call(bf16[32,5120]{1,0:T(8,128)(2,1)S(1)} %collective-permute-done.3.refs_1_.refs_0_, bf16[32,5120]{1,0:T(8,128)(2,1)S(1)} %collective-permute-done.7.refs_1_, ...), custom_call_target="tpu_custom_call" | custom-call | flops 4026531840 | bytes 655360 | tf_op jit(solution)/shard_map/pallas_call | solution.py:535
  68.9 1.8 %collective-permute-done.5.refs_1_ = bf16[32,3072]{1,0:T(8,128)(2,1)S(1)} collective-permute-done((bf16[32,3072]{1,0:T(8,128)(2,1)S(1)}, bf16[32,3072]{1,0:T(8,128)(2,1)S(1)}, u32[]{:S(2)}, u32[]{:S(2)}) %collective-permute-start.5) | collective-permute-done | bytes 196640 | tf_op jit(solution)/shard_map/ppermute | solution.py:655
  70.7 0.0 collective-permute-start.6
  70.7 3.4 %shard_map.143 = (f32[64,1536]{1,0:T(8,128)S(1)}, f32[64,128]{1,0:T(8,128)S(1)}, bf16[512,8192]{1,0:T(8,128)(2,1)S(1)}) custom-call(bf16[32,3072]{1,0:T(8,128)(2,1)S(1)} %collective-permute-done.4.refs_0_, bf16[32,3072]{1,0:T(8,128)(2,1)S(1)} %collective-permute-done.5.refs_1_, f32[1,8192]{1,0:T(1,128)S(1)} %bitcast.107, ...), custom_call_target="tpu_custom_call" | custom-call | flops 2415919104 | bytes 393216 | tf_op jit(solution)/shard_map/pallas_call | solution.py:535
  74.1 2.9 %collective-permute-done.8.refs_0_ = bf16[32,5120]{1,0:T(8,128)(2,1)S(1)} collective-permute-done((bf16[32,5120]{1,0:T(8,128)(2,1)S(1)}, bf16[32,5120]{1,0:T(8,128)(2,1)S(1)}, u32[]{:S(2)}, u32[]{:S(2)}) %collective-permute-start.8) | collective-permute-done | bytes 327712 | tf_op jit(solution)/shard_map/ppermute | solution.py:655
  77.0 3.7 %shard_map.142 = (f32[32,1536]{1,0:T(8,128)S(1)}, f32[32,128]{1,0:T(8,128)S(1)}, bf16[512,8192]{1,0:T(8,128)(2,1)S(1)}) custom-call(bf16[32,5120]{1,0:T(8,128)(2,1)S(1)} %collective-permute-done.8.refs_0_, f32[1,8192]{1,0:T(1,128)S(1)} %bitcast.108, bf16[5120,1024]{1,0:T(8,128)(2,1)S(1)} %get-tuple-element.77.refs_2_, ...), custom_call_target="tpu_custom_call" | custom-call | flops 4026531840 | bytes 327680 | tf_op jit(solution)/shard_map/pallas_call | solution.py:535
  80.7 0.0 collective-permute-done.6.x_ref
  80.7 0.0 copy-start.6
  80.7 0.0 copy-start.10
  80.7 0.0 copy-start.11
  80.7 0.0 copy-start.12
  80.7 0.0 copy-start.13
  80.8 7.7 %shard_map.144 = (f32[8,2048]{1,0:T(8,128)S(1)}, bf16[8,2048]{1,0:T(8,128)(2,1)S(1)}, bf16[8,2048]{1,0:T(8,128)(2,1)S(1)}, bf16[8,2048]{1,0:T(8,128)(2,1)S(1)}) custom-call(s32[1]{0:T(128)} %bitcast.41.t_ref, bf16[32,3072]{1,0:T(8,128)(2,1)S(1)} %collective-permute-done.6.x_ref, f32[1,8192]{1,0:T(1,128)S(1)} %bitcast.109, ...), custom_call_target="tpu_custom_call" | custom-call | flops 2147483648 | bytes 524288 | tf_op jit(solution)/shard_map/pallas_call | solution.py:710
  88.5 0.1 collective-permute-start.9
  88.6 1.5 %collective-permute-start.10 = (bf16[8,2048]{1,0:T(8,128)(2,1)S(1)}, bf16[8,2048]{1,0:T(8,128)(2,1)S(1)}, u32[]{:S(2)}, u32[]{:S(2)}) collective-permute-start(bf16[8,2048]{1,0:T(8,128)(2,1)S(1)} %get-tuple-element.94), channel_id=1, source_target_pairs={{0,2},{1,3},{2,0},{3,1},{4,6},{5,7},{6,4},{7,5},{8,10},{9,11},{10,... | collective-permute-start | bytes 98312 | tf_op jit(solution)/shard_map/ppermute | solution.py:732
  90.1 2.9 %collective-permute-start.11 = (bf16[8,2048]{1,0:T(8,128)(2,1)S(1)}, bf16[8,2048]{1,0:T(8,128)(2,1)S(1)}, u32[]{:S(2)}, u32[]{:S(2)}) collective-permute-start(bf16[8,2048]{1,0:T(8,128)(2,1)S(1)} %get-tuple-element.95), channel_id=1, source_target_pairs={{0,3},{1,2},{2,1},{3,0},{4,7},{5,6},{6,5},{7,4},{8,11},{9,10},{10,... | collective-permute-start | bytes 98312 | tf_op jit(solution)/shard_map/ppermute | solution.py:732
  92.9 0.5 slice.9
  94.1 0.0 collective-permute-done.9
  94.1 0.0 collective-permute-done.10
  94.1 1.7 %collective-permute-done.11 = bf16[8,2048]{1,0:T(8,128)(2,1)S(1)} collective-permute-done((bf16[8,2048]{1,0:T(8,128)(2,1)S(1)}, bf16[8,2048]{1,0:T(8,128)(2,1)S(1)}, u32[]{:S(2)}, u32[]{:S(2)}) %collective-permute-start.11) | collective-permute-done | bytes 32800 | tf_op jit(solution)/shard_map/ppermute | solution.py:732
  95.8 9.4 %all_gather.3 = bf16[64,2048]{1,0:T(8,128)(2,1)S(1)} all-gather(bf16[8,2048]{1,0:T(8,128)(2,1)S(1)} %add_convert_fusion), channel_id=1, replica_groups=mesh['group'=8,'tensor'=4] {'group'}, dimensions={0}, use_global_device_ids=true | all-gather | bytes 294912 | tf_op jit(solution)/shard_map/all_gather | solution.py:733
  105.3 0.0 copy-done.6
  105.3 0.0 copy-done.10
  105.3 0.0 copy-done.11
  105.3 0.0 copy-done.12
  105.3 0.0 copy-done.13
  105.3 1.4 %conditional.1 = ((f32[64,2048]{1,0:T(8,128)}, f32[64,2048]{1,0:T(8,128)})) conditional(s32[]{:T(128)} %bitcast.40, (s32[8,128]{1,0:T(8,128)S(1)}, bf16[64,2048]{1,0:T(8,128)(2,1)S(1)}) %tuple.14, (s32[16,1]{0,1:T(1,128)S(1)}, s32[16]{0:T(128)S(1)}, s32[1]{0:T(128)}, bf16[64,2,8192]{2,1,0:T(2,128)(2,1)S(1)}, s32[16,1]{0,1:T(1,128)S(1)}, ...), branch_computations={%region_0.1_spmd, %region_1.13_spmd} | conditional | flops 10908256256 | bytes 271001728 | solution.py:766
  105.3 1.2 %branch_0_fun.1 = (f32[64,2048]{1,0:T(8,128)}, f32[64,2048]{1,0:T(8,128)}) custom-call(s32[8,128]{1,0:T(8,128)S(1)} %get-tuple-element.28.plan, bf16[64,2048]{1,0:T(8,128)(2,1)S(1)} %get-tuple-element.29.pooled), custom_call_target="tpu_custom_call" | custom-call | tf_op jit(solution)/shard_map/cond/branch_0_fun/pallas_call | solution.py:737
  (5 shorter events, 0.0 us)
Async XLA Ops:
  0.6 35.1 %copy-start.5 = (bf16[64,2,8192]{2,1,0:T(2,128)(2,1)S(1)}, bf16[64,2,8192]{2,1,0:T(2,128)(2,1)}, u32[]{:S(2)}) copy-start(bf16[64,2,8192]{2,1,0:T(2,128)(2,1)} %left.3) | copy-start | bytes 6291460
  2.2 33.5 %copy-start.7 = (bf16[64,2,8192]{2,1,0:T(2,128)(2,1)S(1)}, bf16[64,2,8192]{2,1,0:T(2,128)(2,1)}, u32[]{:S(2)}) copy-start(bf16[64,2,8192]{2,1,0:T(2,128)(2,1)} %right.3) | copy-start | bytes 6291460
  2.3 1.3 %collective-permute-start = (s32[1,128]{1,0:T(1,128)S(1)}, s32[1,128]{1,0:T(1,128)S(1)}, u32[]{:S(2)}, u32[]{:S(2)}) collective-permute-start(s32[1,128]{1,0:T(1,128)S(1)} %compare_select_fusion.7), channel_id=1, source_target_pairs={{0,4},{4,0},{8,12},{12,8},{16,20},{20,16},{24,28},{28,24},{1,5},{5... | collective-permute-start | bytes 1544 | tf_op jit(solution)/shard_map/ppermute | solution.py:603
  3.6 4.4 %collective-permute-start.1 = (s32[1,128]{1,0:T(1,128)S(1)}, s32[1,128]{1,0:T(1,128)S(1)}, u32[]{:S(2)}, u32[]{:S(2)}) collective-permute-start(s32[1,128]{1,0:T(1,128)S(1)} %fusion.53), channel_id=1, source_target_pairs={{0,8},{4,12},{8,0},{12,4},{16,24},{20,28},{24,16},{28,20},{1,9},{5... | collective-permute-start | bytes 1544 | tf_op jit(solution)/shard_map/ppermute | solution.py:603
  8.0 3.6 %collective-permute-start.2 = (s32[1,128]{1,0:T(1,128)S(1)}, s32[1,128]{1,0:T(1,128)S(1)}, u32[]{:S(2)}, u32[]{:S(2)}) collective-permute-start(s32[1,128]{1,0:T(1,128)S(1)} %add.112.mine), channel_id=1, source_target_pairs={{0,16},{4,20},{8,24},{12,28},{16,0},{20,4},{24,8},{28,12},{1,17},{... | collective-permute-start | bytes 1544 | tf_op jit(solution)/shard_map/ppermute | solution.py:603
  15.7 29.9 %copy-start.9 = (f32[8192]{0:T(1024)S(1)}, f32[8192]{0:T(1024)}, u32[]{:S(2)}) copy-start(f32[8192]{0:T(1024)} %param.21) | copy-start | bytes 98308
  34.1 11.5 %collective-permute-start.3 = (bf16[32,5120]{1,0:T(8,128)(2,1)S(1)}, bf16[32,5120]{1,0:T(8,128)(2,1)S(1)}, u32[]{:S(2)}, u32[]{:S(2)}) collective-permute-start(bf16[32,5120]{1,0:T(8,128)(2,1)S(1)} %shard_map.137.refs_0_), channel_id=1, source_target_pairs={{0,1},{1,2},{2,3},{3,0},{4,5},{5,6},{6,7},{7,4},{8,9},{9,10},{10,1... | collective-permute-start | bytes 983048 | tf_op jit(solution)/shard_map/ppermute | solution.py:655
  39.1 12.8 %all-to-all-start.7 = ((bf16[40,2,3072]{2,1,0:T(2,128)(2,1)}), bf16[40,2,3072]{2,1,0:T(2,128)(2,1)S(1)}, u32[]{:S(2)}, u32[]{:S(2)}) async-start(bf16[40,2,3072]{2,1,0:T(2,128)(2,1)} %shard_map.136), calls=%async_computation.7 | async-start | bytes 983040 | tf_op jit(solution)/shard_map/all_to_all | solution.py:638
  45.6 15.5 %collective-permute-start.7 = (bf16[32,5120]{1,0:T(8,128)(2,1)S(1)}, bf16[32,5120]{1,0:T(8,128)(2,1)S(1)}, u32[]{:S(2)}, u32[]{:S(2)}) collective-permute-start(bf16[32,5120]{1,0:T(8,128)(2,1)S(1)} %collective-permute-done.3.refs_1_.refs_0_), channel_id=1, source_target_pairs={{0,1},{1,2},{2,3},{3,0},{4,5},{5,6},{6,7},{7,4},{8,9},{9,10},{10,1... | collective-permute-start | bytes 983048 | tf_op jit(solution)/shard_map/ppermute | solution.py:655
  53.3 7.8 %collective-permute-start.4 = (bf16[32,3072]{1,0:T(8,128)(2,1)S(1)}, bf16[32,3072]{1,0:T(8,128)(2,1)S(1)}, u32[]{:S(2)}, u32[]{:S(2)}) collective-permute-start(bf16[32,3072]{1,0:T(8,128)(2,1)S(1)} %shard_map.139.refs_0_.refs_6_), channel_id=1, source_target_pairs={{0,1},{1,2},{2,3},{3,0},{4,5},{5,6},{6,7},{7,4},{8,9},{9,10},{10,1... | collective-permute-start | bytes 589832 | tf_op jit(solution)/shard_map/ppermute | solution.py:655
  54.9 7.9 %copy-start = (bf16[8192,256]{1,0:T(8,128)(2,1)S(1)}, bf16[8192,256]{1,0:T(8,128)(2,1)}, u32[]{:S(2)}) copy-start(bf16[8192,256]{1,0:T(8,128)(2,1)} %refs_4_.5) | copy-start | bytes 12582916
  54.9 7.9 %copy-start.3 = (bf16[8192,256]{1,0:T(8,128)(2,1)S(1)}, bf16[8192,256]{1,0:T(8,128)(2,1)}, u32[]{:S(2)}) copy-start(bf16[8192,256]{1,0:T(8,128)(2,1)} %refs_5_.2) | copy-start | bytes 12582916
  61.0 9.6 %collective-permute-start.5 = (bf16[32,3072]{1,0:T(8,128)(2,1)S(1)}, bf16[32,3072]{1,0:T(8,128)(2,1)S(1)}, u32[]{:S(2)}, u32[]{:S(2)}) collective-permute-start(bf16[32,3072]{1,0:T(8,128)(2,1)S(1)} %collective-permute-done.4.refs_0_), channel_id=1, source_target_pairs={{0,1},{1,2},{2,3},{3,0},{4,5},{5,6},{6,7},{7,4},{8,9},{9,10},{10,1... | collective-permute-start | bytes 589832 | tf_op jit(solution)/shard_map/ppermute | solution.py:655
  61.1 15.9 %collective-permute-start.8 = (bf16[32,5120]{1,0:T(8,128)(2,1)S(1)}, bf16[32,5120]{1,0:T(8,128)(2,1)S(1)}, u32[]{:S(2)}, u32[]{:S(2)}) collective-permute-start(bf16[32,5120]{1,0:T(8,128)(2,1)S(1)} %collective-permute-done.7.refs_1_), channel_id=1, source_target_pairs={{0,1},{1,2},{2,3},{3,0},{4,5},{5,6},{6,7},{7,4},{8,9},{9,10},{10,1... | collective-permute-start | bytes 983048 | tf_op jit(solution)/shard_map/ppermute | solution.py:655
  70.7 10.0 %collective-permute-start.6 = (bf16[32,3072]{1,0:T(8,128)(2,1)S(1)}, bf16[32,3072]{1,0:T(8,128)(2,1)S(1)}, u32[]{:S(2)}, u32[]{:S(2)}) collective-permute-start(bf16[32,3072]{1,0:T(8,128)(2,1)S(1)} %collective-permute-done.5.refs_1_), channel_id=1, source_target_pairs={{0,1},{1,2},{2,3},{3,0},{4,5},{5,6},{6,7},{7,4},{8,9},{9,10},{10,1... | collective-permute-start | bytes 589832 | tf_op jit(solution)/shard_map/ppermute | solution.py:655
  80.7 24.6 %copy-start.6 = (bf16[64,2,8192]{2,1,0:T(2,128)(2,1)S(1)}, bf16[64,2,8192]{2,1,0:T(2,128)(2,1)}, u32[]{:S(2)}) copy-start(bf16[64,2,8192]{2,1,0:T(2,128)(2,1)} %left.3) | copy-start | bytes 6291460
  80.7 24.5 %copy-start.10 = (s32[16,1]{0,1:T(1,128)S(1)}, s32[16,1]{0,1:T(1,128)}, u32[]{:S(2)}) copy-start(s32[16,1]{0,1:T(1,128)} %param.18) | copy-start | bytes 196
  80.7 24.5 %copy-start.11 = (s32[16,1]{0,1:T(1,128)S(1)}, s32[16,1]{0,1:T(1,128)}, u32[]{:S(2)}) copy-start(s32[16,1]{0,1:T(1,128)} %param.16) | copy-start | bytes 196
  80.7 24.5 %copy-start.12 = (s32[16]{0:T(128)S(1)}, s32[16]{0:T(128)}, u32[]{:S(2)}) copy-start(s32[16]{0:T(128)} %param.19) | copy-start | bytes 196
  80.7 24.5 %copy-start.13 = (s32[16]{0:T(128)S(1)}, s32[16]{0:T(128)}, u32[]{:S(2)}) copy-start(s32[16]{0:T(128)} %param.17) | copy-start | bytes 196
  88.5 5.6 %collective-permute-start.9 = (bf16[8,2048]{1,0:T(8,128)(2,1)S(1)}, bf16[8,2048]{1,0:T(8,128)(2,1)S(1)}, u32[]{:S(2)}, u32[]{:S(2)}) collective-permute-start(bf16[8,2048]{1,0:T(8,128)(2,1)S(1)} %get-tuple-element.93), channel_id=1, source_target_pairs={{0,1},{1,0},{2,3},{3,2},{4,5},{5,4},{6,7},{7,6},{8,9},{9,8},{10,11... | collective-permute-start | bytes 98312 | tf_op jit(solution)/shard_map/ppermute | solution.py:732
  88.6 5.6 %collective-permute-start.10 = (bf16[8,2048]{1,0:T(8,128)(2,1)S(1)}, bf16[8,2048]{1,0:T(8,128)(2,1)S(1)}, u32[]{:S(2)}, u32[]{:S(2)}) collective-permute-start(bf16[8,2048]{1,0:T(8,128)(2,1)S(1)} %get-tuple-element.94), channel_id=1, source_target_pairs={{0,2},{1,3},{2,0},{3,1},{4,6},{5,7},{6,4},{7,5},{8,10},{9,11},{10,... | collective-permute-start | bytes 98312 | tf_op jit(solution)/shard_map/ppermute | solution.py:732
  90.1 5.7 %collective-permute-start.11 = (bf16[8,2048]{1,0:T(8,128)(2,1)S(1)}, bf16[8,2048]{1,0:T(8,128)(2,1)S(1)}, u32[]{:S(2)}, u32[]{:S(2)}) collective-permute-start(bf16[8,2048]{1,0:T(8,128)(2,1)S(1)} %get-tuple-element.95), channel_id=1, source_target_pairs={{0,3},{1,2},{2,1},{3,0},{4,7},{5,6},{6,5},{7,4},{8,11},{9,10},{10,... | collective-permute-start | bytes 98312 | tf_op jit(solution)/shard_map/ppermute | solution.py:732

commit v4 on v3

--- a/solution.py
+++ b/solution.py
@@ -150,6 +150,7 @@
 RIGHT_SHIFT = 12
 DEALS = (43, 21, 34, 1, 15, 10, 61, 5, 7, 50, 11, 4)
 LOADS = 8
+BLOCK = 512
 COST = 512
 WO_PARTS = 2
 BF16 = jnp.bfloat16
@@ -171,6 +172,14 @@
 def column(row):
     n = row.shape[1]
     return jnp.transpose(jnp.broadcast_to(row, (n, n)))[:, :1]
+
+
+def split3(wide):
+    high = wide.astype(BF16)
+    rest = wide - high.astype(F32)
+    mid = rest.astype(BF16)
+    low = (rest - mid.astype(F32)).astype(BF16)
+    return (high, mid, low)
 
 
 def plan_body(codes, me, groups, share, cap, rows_here):
@@ -311,7 +320,7 @@
 
 def products(x_refs, gain, weights, first, ready=None):
     rows, wide = sum(x.shape[0] for x in x_refs), x_refs[0].shape[1]
-    block = wide // LOADS
+    block = BLOCK
     widths = [w.shape[1] for w in weights]
 
     def one(i, carry):
@@ -328,7 +337,7 @@
         return (sums, square + jnp.sum(x * x, axis=1, keepdims=True))
 
     zero = (tuple(jnp.zeros((rows, n), F32) for n in widths), jnp.zeros((rows, 1), F32))
-    sums, square = lax.fori_loop(0, LOADS, one, zero)
+    sums, square = lax.fori_loop(0, wide // block, one, zero)
     return (jnp.concatenate(sums, axis=1), square)
 
 
@@ -350,7 +359,7 @@
         weights = [refs.pop(0) for _ in range(3)]
     if loads:
         sems = refs.pop(0)
-        block = x_refs[0].shape[1] // LOADS
+        block = BLOCK
 
         def copy(which, i):
             at = i * block
@@ -360,7 +369,7 @@
                 sems.at[which, i],
             )
 
-        for i in range(LOADS):
+        for i in range(x_refs[0].shape[1] // block):
             for which in range(3):
                 copy(which, i).start()
 
@@ -395,7 +404,19 @@
 ):
     wos, refs = refs[:WO_PARTS], refs[WO_PARTS:]
     accs, sqs, resids = refs[:groups], refs[groups : 2 * groups], refs[2 * groups : 2 * groups + parts]
-    outs, (ctx, out) = refs[2 * groups + parts : -2], refs[-2:]
+    outs, (ctx, out, wo_tail, sems) = refs[2 * groups + parts : -4], refs[-4:]
+    deep = wo_tail.shape[0]
+    copies = [
+        pltpu.make_async_copy(
+            wos[1].at[pl.ds(deep + i * (deep // LOADS), deep // LOADS)],
+            wo_tail.at[pl.ds(i * (deep // LOADS), deep // LOADS)],
+            sems.at[i],
+        )
+        for i in range(LOADS)
+    ]
+    for copy in copies:
+        copy.start()
+    wos = [wos[0], wo_tail]
     pairs, features = out.shape[1:]
     heads, kv_heads = wq.shape[1] // HEAD_DIM, wk.shape[1] // HEAD_DIM
     share = heads // kv_heads
@@ -450,6 +471,8 @@
             at = (kv * share + i) * HEAD_DIM
             ctx[:, at : at + HEAD_DIM] = jnp.concatenate([high, low], axis=0)
 
+    for copy in copies:
+        copy.wait()
     block = min(512, features)
     per = features // block
     done = 0
@@ -459,7 +482,6 @@
             here = pl.multiple_of(i * block, block)
             i = i + done // block
             at = pl.multiple_of(i * block, block)
-            deep = wos[0].shape[0]
             both = sum(
                 jnp.dot(
                     ctx[:, j * deep : (j + 1) * deep],
@@ -481,11 +503,12 @@
 
 def final_kernel(plan, pooled, left, right, held, sems):
     rows, n = left.shape[0], pooled.shape[0]
+    parts = split3(pooled[...])
     at = lax.broadcasted_iota(jnp.int32, (rows, n), 0)
     copies = []
     for side, out in enumerate((left, right)):
         hit = (plan[pl.ds(2 + side, 1), :][:, :n] == at).astype(BF16)
-        held[side] = jnp.dot(hit, pooled[...], preferred_element_type=F32)
+        held[side] = sum(jnp.dot(hit, part, preferred_element_type=F32) for part in parts)
         copies.append(pltpu.make_async_copy(held.at[side], out, sems.at[side]))
         copies[-1].start()
     for copy in copies:
@@ -507,7 +530,7 @@
     return pltpu.with_memory_space_constraint(array, pltpu.VMEM)
 
 
-def qkv(xs, first, gain, weights, loads, keep, before, resid, pair_rows, extra=None, after=()):
+def qkv(xs, first, gain, weights, loads, keep, before, resid, pair_rows, extra=None, after=(), cost=COST):
     rows, wide = sum(x.shape[0] for x in xs), xs[0].shape[1]
     total = sum(w.shape[1] for w in weights)
     args = [*xs, gain, *weights] + (before or [])
@@ -523,7 +546,7 @@
             out_shape += halves
         else:
             scratch += halves
-        scratch.append(pltpu.SemaphoreType.DMA((3, LOADS)))
+        scratch.append(pltpu.SemaphoreType.DMA((3, wide // BLOCK)))
     if extra is not None:
         array, part, at = extra
         args.append(array)
@@ -551,7 +574,7 @@
         scratch_shapes=scratch,
         compiler_params=LIMIT if keep or not loads else WIDE_LIMIT,
         cost_estimate=pl.CostEstimate(
-            flops=COST * wide * total, bytes_accessed=2 * rows * wide, transcendentals=0
+            flops=cost * wide * total, bytes_accessed=2 * rows * wide, transcendentals=0
         ),
     )(*args)
     out = list(out)
@@ -631,7 +654,10 @@
             )(plan, left_table, right_table)
         )
     gain = norm_gain[None, :]
-    weights = (query_weight, key_weight, value_weight)
+    weights = [
+        pltpu.with_memory_space_constraint(w, pltpu.HBM)
+        for w in (query_weight, key_weight, value_weight)
+    ]
     ring = [(i, (i + 1) % tensors) for i in range(tensors)]
 
     def exchange(send):
@@ -654,72 +680,91 @@
     def pass_on(x):
         return lax.ppermute(x, "tensor", ring)
 
-    one, two = [[pick(exchange(sends[0]), [])], []]
-    first = qkv(one, parts[0][0], gain, weights, True, False, None, True, pair_rows)
-    one.append(pass_on(one[0]))
-    two.append(pick(exchange(sends[1]), [first["sums"][1], one[1]]))
-    for _ in range(2, tensors):
-        one.append(pass_on(one[-1]))
-    for _ in range(1, tensors):
-        two.append(pass_on(two[-1]))
-    shards = [(0, 1), (1, 3)] + [(i, i + 1) for i in range(3, tensors)]
-    deep = output_weight.shape[0] // WO_PARTS
-    sums, wos, held_one, held_two = [first["sums"]], [], None, None
-    for low, high in shards[1:]:
-        out = qkv(
+    def both(x, other):
+        return lax.optimization_barrier((x, other))[0]
+
+    def part_one(low, high, kept, extra=None, after=(), cost=COST):
+        return qkv(
             one[low:high],
             parts[0][0],
             gain,
-            held_one or weights,
-            held_one is None,
-            held_one is None,
+            kept or weights,
+            not kept,
+            low == 1,
             None,
-            False,
+            low == 0,
             pair_rows,
-            (output_weight, deep, 0) if low == 3 else None,
-            [two[0]] if held_one is None else [],
-        )
-        held_one = held_one or out["weights"]
-        sums.append(out["sums"])
-        if "extra" in out:
-            wos.append(out["extra"])
-    resids = [first["resid"]]
-    for at, (low, high) in enumerate(shards[:-1]):
-        out = qkv(
+            extra,
+            after,
+            cost,
+        )
+
+    def part_two(low, high, kept, before, extra=None, after=(), cost=COST):
+        return qkv(
             two[low:high],
             parts[1][0],
             gain,
-            held_two or weights,
-            held_two is None,
-            held_two is None,
-            sums[at],
+            kept or weights,
+            not kept,
+            not kept,
+            before["sums"],
             low == 0,
             pair_rows,
-            (output_weight, deep, deep) if low == 1 else None,
-        )
-        held_two = held_two or out["weights"]
-        sums[at] = out["sums"]
-        if low == 0:
-            resids.append(out["resid"])
-        if "extra" in out:
-            wos.append(out["extra"])
-    held, held_weights = two, [held_two]
+            extra,
+            after,
+            cost,
+        )
+
+    one = [pick(exchange(sends[0]), [])]
+    first = part_one(0, 1, None)
+    one.append(pass_on(one[0]))
+    two = [pick(exchange(sends[1]), [first["sums"][1], one[1]])]
+    for _ in range(2, tensors):
+        one.append(pass_on(one[-1]))
+    deep = output_weight.shape[0] // WO_PARTS
+    next_one = part_one(1, 3, None, None, [two[0]])
+    two.append(both(pass_on(two[0]), next_one["sums"][1]))
+    first_two = part_two(0, 1, None, first, None, [two[1]])
+    for _ in range(2, tensors):
+        two.append(pass_on(two[-1]))
+    next_two = part_two(1, 3, first_two["weights"], next_one, None, (), 0)
+    rest = []
+    for at in range(3, tensors):
+        rest.append(
+            part_one(
+                at,
+                at + 1,
+                next_one["weights"],
+                (output_weight, deep, 0) if at == 3 else None,
+                [next_two["sums"][1]],
+            )
+        )
+        if at + 1 < tensors:
+            rest[-1]["sums"] = part_two(at, at + 1, first_two["weights"], rest[-1])["sums"]
+    sums = [x["sums"] for x in [first_two, next_two] + rest]
+    shards, resids = sums, [first["resid"], first_two["resid"]]
+    wos = [rest[0]["extra"], output_weight]
+    held, held_weights = two, [first_two["weights"]]
     accs, sqs = [s[0] for s in sums], [s[1] for s in sums]
 
     args = [held[-1], gain, *held_weights[-1], *wos, *accs, *sqs, *resids]
+    in_specs = [IN_SMEM] + [IN_VMEM] * len(args)
+    in_specs[7] = ANY
     partial_sums = pl.pallas_call(
         functools.partial(
             tail_kernel, tensors, len(shards), len(parts), width, length, pair_rows, parts[-1][0]
         ),
-        in_specs=[IN_SMEM] + [IN_VMEM] * len(args),
+        in_specs=in_specs,
         out_specs=[IN_VMEM] * tensors,
         out_shape=[shape((share, features), F32)]
         + [shape((share, features), BF16)] * (tensors - 1),
         scratch_shapes=[
             pltpu.VMEM((2 * share, output_weight.shape[0]), BF16),
             pltpu.VMEM((tensors, share, features), F32),
+            pltpu.VMEM((deep, width), BF16),
+            pltpu.SemaphoreType.DMA((LOADS,)),
         ],
-        compiler_params=LIMIT,
+        compiler_params=WIDE_LIMIT,
         cost_estimate=pl.CostEstimate(
             flops=32 * share * width * output_weight.shape[0],
             bytes_accessed=2 * rows * width,
@@ -730,7 +775,7 @@
     for step in range(1, tensors):
         swap = [(i, i ^ step) for i in range(tensors)]
         pooled = pooled + lax.ppermute(partial_sums[step], "tensor", swap).astype(F32)
-    everyone = lax.all_gather(pooled.astype(BF16), "group", tiled=True)
+    everyone = lax.all_gather(pooled, "group", tiled=True)
 
     def fast():
         return tuple(

time: 107 us -> 106 us (level)
  transfers between devices with their start and end apart: 13 -> 13, of which waited for: 9 -> 10; matrix products, arithmetic and copies ran while one was open for 0% -> 0% of each run, Pallas kernels for 27% -> 26%
where the time goes in v4:
time: 106 us
  Pallas kernels  42.6 us (40%)
  blocking collectives  26.4 us (25%)
  starting transfers between devices  17.4 us (16%)
  waiting for transfers between devices  15.7 us (15%)
  between operations  2.43 us (2%)
    pallas_call x5, Pallas kernels, qkv(): pl.pallas_call(functools.partial(qkv_kernel, len(xs), first, loads, keep,...  23.3 us
    all_to_all x1, blocking collectives, exchange(): lax.all_to_all(send, 'group', split_axis=0, concat_axis=0, tiled=True)  16.9 us
    all_gather x1, blocking collectives, on_device(): everyone = lax.all_gather(pooled, 'group', tiled=True)  9.43 us
    ppermute x6, waiting for transfers between devices, pass_on(): return lax.ppermute(x, 'tensor', ring)  9.18 us
    pallas_call x1, Pallas kernels, on_device(): pl.pallas_call(functools.partial(tail_kernel, tensors, len(shards), len(p...  7.75 us
    ppermute x3, starting transfers between devices, on_device(): lax.ppermute(code, 'group', [(i, i ^ hop) for i in range(groups)])  5.42 us
    ppermute x6, starting transfers between devices, pass_on(): return lax.ppermute(x, 'tensor', ring)  4.95 us
    pallas_call x1, Pallas kernels, on_device(): pl.pallas_call(functools.partial(plan_kernel, groups, share, cap, rows_he...  4.12 us
  transfers between devices with their start and end apart: 13, of which 10 were waited for; matrix products, arithmetic and copies ran while one was open for 0% of the time, Pallas kernels for 26%

profile of v4, /device:TPU:0, one launch (start us, length us, event | category | flops | bytes accessed | tf_op | source)
XLA Modules:
  0.0 106.1 jit_solution(2064420465702418045)
XLA Ops:
  0.6 0.0 copy-start.2
  1.4 0.7 compare_select_fusion.6
  2.2 0.1 tile.10
  2.2 0.0 copy-start.4
  2.3 0.5 collective-permute-start
  2.8 0.8 collective-permute-done
  3.6 2.9 %collective-permute-start.1 = (s32[1,128]{1,0:T(1,128)S(1)}, s32[1,128]{1,0:T(1,128)S(1)}, u32[]{:S(2)}, u32[]{:S(2)}) collective-permute-start(s32[1,128]{1,0:T(1,128)S(1)} %fusion.53), channel_id=1, source_target_pairs={{0,8},{4,12},{8,0},{12,4},{16,24},{20,28},{24,16},{28,20},{1,9},{5... | collective-permute-start | bytes 1544 | tf_op jit(solution)/shard_map/ppermute | solution.py:626
  6.5 1.5 %collective-permute-done.1 = s32[1,128]{1,0:T(1,128)S(1)} collective-permute-done((s32[1,128]{1,0:T(1,128)S(1)}, s32[1,128]{1,0:T(1,128)S(1)}, u32[]{:S(2)}, u32[]{:S(2)}) %collective-permute-start.1) | collective-permute-done | bytes 544 | tf_op jit(solution)/shard_map/ppermute | solution.py:626
  8.0 2.0 %collective-permute-start.2 = (s32[1,128]{1,0:T(1,128)S(1)}, s32[1,128]{1,0:T(1,128)S(1)}, u32[]{:S(2)}, u32[]{:S(2)}) collective-permute-start(s32[1,128]{1,0:T(1,128)S(1)} %add.112.mine), channel_id=1, source_target_pairs={{0,16},{4,20},{8,24},{12,28},{16,0},{20,4},{24,8},{28,12},{1,17},{... | collective-permute-start | bytes 1544 | tf_op jit(solution)/shard_map/ppermute | solution.py:626
  10.0 1.5 %collective-permute-done.2.others = s32[1,128]{1,0:T(1,128)S(1)} collective-permute-done((s32[1,128]{1,0:T(1,128)S(1)}, s32[1,128]{1,0:T(1,128)S(1)}, u32[]{:S(2)}, u32[]{:S(2)}) %collective-permute-start.2) | collective-permute-done | bytes 544 | tf_op jit(solution)/shard_map/ppermute | solution.py:626
  11.6 4.1 %shard_map.135 = (s32[8,128]{1,0:T(8,128)S(1)}, bf16[40,2,5120]{2,1,0:T(2,128)(2,1)S(1)}) custom-call(s32[1]{0:T(128)} %bitcast.36.me, s32[1,128]{1,0:T(1,128)S(1)} %add.112.mine, s32[1,128]{1,0:T(1,128)S(1)} %collective-permute-done.2.others, bf16[64,2,8192]{2,1,0:T(2,128)(2,1)} %left.3, bf16[64,2,8192]{2,1,0:T(2,128)(2,1)} %right.3), custom_call_target="tpu_custom_call" | custom-call | tf_op jit(solution)/shard_map/pallas_call | solution.py:632
  15.7 0.0 copy-start.7
  15.7 16.9 %all_to_all.48.got = bf16[40,2,5120]{2,1,0:T(2,128)(2,1)S(1)} all-to-all(bf16[40,2,5120]{2,1,0:T(2,128)(2,1)S(1)} %get-tuple-element.71), channel_id=1, replica_groups=mesh['group'=8,'tensor'=4] {'group'}, dimensions={0} | all-to-all | bytes 1638400 | tf_op jit(solution)/shard_map/all_to_all | solution.py:664
  32.6 1.5 %shard_map.137.refs_0_ = bf16[32,5120]{1,0:T(8,128)(2,1)S(1)} custom-call(s32[8,128]{1,0:T(8,128)S(1)} %get-tuple-element.70.plan, bf16[40,2,5120]{2,1,0:T(2,128)(2,1)S(1)} %all_to_all.48.got), custom_call_target="tpu_custom_call" | custom-call | tf_op jit(solution)/shard_map/pallas_call | solution.py:668
  34.1 1.6 %collective-permute-start.3 = (bf16[32,5120]{1,0:T(8,128)(2,1)S(1)}, bf16[32,5120]{1,0:T(8,128)(2,1)S(1)}, u32[]{:S(2)}, u32[]{:S(2)}) collective-permute-start(bf16[32,5120]{1,0:T(8,128)(2,1)S(1)} %shard_map.137.refs_0_), channel_id=1, source_target_pairs={{0,1},{1,2},{2,3},{3,0},{4,5},{5,6},{6,7},{7,4},{8,9},{9,10},{10,1... | collective-permute-start | bytes 983048 | tf_op jit(solution)/shard_map/ppermute | solution.py:681
  35.7 0.0 copy-done.2
  35.7 0.0 copy-done.4
  35.7 3.3 %shard_map.136 = bf16[40,2,3072]{2,1,0:T(2,128)(2,1)} custom-call(s32[8,128]{1,0:T(8,128)S(1)} %get-tuple-element.70.plan, bf16[64,2,8192]{2,1,0:T(2,128)(2,1)S(1)} %copy-done.2, bf16[64,2,8192]{2,1,0:T(2,128)(2,1)S(1)} %copy-done.4), custom_call_target="tpu_custom_call" | custom-call | tf_op jit(solution)/shard_map/pallas_call | solution.py:647
  39.0 3.5 %all-to-all-start.7 = ((bf16[40,2,3072]{2,1,0:T(2,128)(2,1)}), bf16[40,2,3072]{2,1,0:T(2,128)(2,1)S(1)}, u32[]{:S(2)}, u32[]{:S(2)}) async-start(bf16[40,2,3072]{2,1,0:T(2,128)(2,1)} %shard_map.136), calls=%async_computation.7 | async-start | bytes 983040 | tf_op jit(solution)/shard_map/all_to_all | solution.py:664
  42.5 3.1 %collective-permute-done.3.refs_1_.refs_0_ = bf16[32,5120]{1,0:T(8,128)(2,1)S(1)} collective-permute-done((bf16[32,5120]{1,0:T(8,128)(2,1)S(1)}, bf16[32,5120]{1,0:T(8,128)(2,1)S(1)}, u32[]{:S(2)}, u32[]{:S(2)}) %collective-permute-start.3) | collective-permute-done | bytes 327712 | tf_op jit(solution)/shard_map/ppermute | solution.py:681
  45.6 0.0 collective-permute-start.5
  45.6 0.0 copy-done.7
  45.6 6.3 %shard_map.138 = (f32[32,1536]{1,0:T(8,128)S(1)}, f32[32,128]{1,0:T(8,128)S(1)}, f32[8,5120]{1,0:T(8,128)S(1)}) custom-call(bf16[32,5120]{1,0:T(8,128)(2,1)S(1)} %shard_map.137.refs_0_, f32[1,8192]{1,0:T(1,128)S(1)} %bitcast.106, bf16[8192,1024]{1,0:T(8,128)(2,1)} %refs_2_.3, bf16[8192,256]{1,0:T(8,128)(2,1)} %refs_3_.5, bf16[8192,256]{1,0:T(8,128)(2,1)} %refs_4_.5), custom_call_target="tpu_custom_call" | custom-call | flops 4026531840 | bytes 327680 | tf_op jit(solution)/shard_map/pallas_call | solution.py:558
  51.9 0.0 all-to-all-done.7.got
  51.9 1.3 %shard_map.139.refs_6_.refs_0_ = bf16[32,3072]{1,0:T(8,128)(2,1)S(1)} custom-call(s32[8,128]{1,0:T(8,128)S(1)} %get-tuple-element.70.plan, bf16[40,2,3072]{2,1,0:T(2,128)(2,1)S(1)} %all-to-all-done.7.got, f32[32,128]{1,0:T(8,128)S(1)} %get-tuple-element.72.refs_0_.refs_6_, bf16[32,5120]{1,0:T(8,128)(2,1)S(1)} %collective-permute-done.3.refs_1_.refs_0_), custom_call_target="tpu_custom_call" | custom-call | tf_op jit(solution)/shard_map/pallas_call | solution.py:668
  53.2 1.6 %collective-permute-start.4 = (bf16[32,3072]{1,0:T(8,128)(2,1)S(1)}, bf16[32,3072]{1,0:T(8,128)(2,1)S(1)}, u32[]{:S(2)}, u32[]{:S(2)}) collective-permute-start(bf16[32,3072]{1,0:T(8,128)(2,1)S(1)} %shard_map.139.refs_6_.refs_0_), channel_id=1, source_target_pairs={{0,1},{1,2},{2,3},{3,0},{4,5},{5,6},{6,7},{7,4},{8,9},{9,10},{10,1... | collective-permute-start | bytes 589832 | tf_op jit(solution)/shard_map/ppermute | solution.py:681
  54.8 1.4 %collective-permute-done.5.refs_1_ = bf16[32,5120]{1,0:T(8,128)(2,1)S(1)} collective-permute-done((bf16[32,5120]{1,0:T(8,128)(2,1)S(1)}, bf16[32,5120]{1,0:T(8,128)(2,1)S(1)}, u32[]{:S(2)}, u32[]{:S(2)}) %collective-permute-start.5) | collective-permute-done | bytes 327712 | tf_op jit(solution)/shard_map/ppermute | solution.py:681
  56.1 0.2 collective-permute-start.8
  56.4 6.1 %shard_map.140 = (f32[64,1536]{1,0:T(8,128)S(1)}, f32[64,128]{1,0:T(8,128)S(1)}, bf16[5120,1024]{1,0:T(8,128)(2,1)S(1)}, bf16[5120,256]{1,0:T(8,128)(2,1)S(1)}, bf16[5120,256]{1,0:T(8,128)(2,1)S(1)}) custom-call(bf16[32,5120]{1,0:T(8,128)(2,1)S(1)} %collective-permute-done.3.refs_1_.refs_0_, bf16[32,5120]{1,0:T(8,128)(2,1)S(1)} %collective-permute-done.5.refs_1_, ...), custom_call_target="tpu_custom_call" | custom-call | flops 4026531840 | bytes 655360 | tf_op jit(solution)/shard_map/pallas_call | solution.py:558
  62.5 0.4 collective-permute-done.4.refs_7_.refs_0_
  62.9 1.5 %collective-permute-start.6 = (bf16[32,3072]{1,0:T(8,128)(2,1)S(1)}, bf16[32,3072]{1,0:T(8,128)(2,1)S(1)}, u32[]{:S(2)}, u32[]{:S(2)}) collective-permute-start(bf16[32,3072]{1,0:T(8,128)(2,1)S(1)} %collective-permute-done.4.refs_7_.refs_0_), channel_id=1, source_target_pairs={{0,1},{1,2},{2,3},{3,0},{4,5},{5,6},{6,7},{7,4},{8,9},{9,10},{10,1... | collective-permute-start | bytes 589832 | tf_op jit(solution)/shard_map/ppermute | solution.py:681
  64.4 4.4 %shard_map.141 = (f32[32,1536]{1,0:T(8,128)S(1)}, f32[32,128]{1,0:T(8,128)S(1)}, f32[8,3072]{1,0:T(8,128)S(1)}, bf16[3072,1024]{1,0:T(8,128)(2,1)S(1)}, bf16[307...) custom-call(bf16[32,3072]{1,0:T(8,128)(2,1)S(1)} %shard_map.139.refs_6_.refs_0_, f32[1,8192]{1,0:T(1,128)S(1)} %bitcast.108, ...), custom_call_target="tpu_custom_call" | custom-call | flops 2415919104 | bytes 196608 | tf_op jit(solution)/shard_map/pallas_call | solution.py:558
  68.8 3.4 %collective-permute-done.6.refs_1_ = bf16[32,3072]{1,0:T(8,128)(2,1)S(1)} collective-permute-done((bf16[32,3072]{1,0:T(8,128)(2,1)S(1)}, bf16[32,3072]{1,0:T(8,128)(2,1)S(1)}, u32[]{:S(2)}, u32[]{:S(2)}) %collective-permute-start.6) | collective-permute-done | bytes 196640 | tf_op jit(solution)/shard_map/ppermute | solution.py:681
  72.2 0.0 collective-permute-start.7
  72.2 2.6 %shard_map.142 = (f32[64,1536]{1,0:T(8,128)S(1)}, f32[64,128]{1,0:T(8,128)S(1)}) custom-call(bf16[32,3072]{1,0:T(8,128)(2,1)S(1)} %collective-permute-done.4.refs_7_.refs_0_, bf16[32,3072]{1,0:T(8,128)(2,1)S(1)} %collective-permute-done.6.refs_1_, f32[1,8192]{1,0:T(1,128)S(1)} %bitcast.109, bf16[3072,1024]{1,0:T(8,128)(2,1)S(1)} %get-tuple-element.76.refs_3_.wq, ...), custom_call_target="tpu_custom_call" | custom-call | bytes 393216 | tf_op jit(solution)/shard_map/pallas_call | solution.py:558
  74.8 0.0 collective-permute-done.8.refs_0_
  74.8 3.9 %shard_map.143 = (f32[32,1536]{1,0:T(8,128)S(1)}, f32[32,128]{1,0:T(8,128)S(1)}, bf16[512,8192]{1,0:T(8,128)(2,1)S(1)}) custom-call(bf16[32,5120]{1,0:T(8,128)(2,1)S(1)} %collective-permute-done.8.refs_0_, f32[1,8192]{1,0:T(1,128)S(1)} %bitcast.110, bf16[5120,1024]{1,0:T(8,128)(2,1)S(1)} %get-tuple-element.79.refs_2_, ...), custom_call_target="tpu_custom_call" | custom-call | flops 4026531840 | bytes 327680 | tf_op jit(solution)/shard_map/pallas_call | solution.py:558
  78.7 0.9 collective-permute-done.7.x_ref
  79.7 0.0 copy-start.3
  79.7 0.0 copy-start.8
  79.7 0.0 copy-start.9
  79.7 0.0 copy-start.10
  79.7 0.0 copy-start.11
  79.7 7.7 %shard_map.144 = (f32[8,2048]{1,0:T(8,128)S(1)}, bf16[8,2048]{1,0:T(8,128)(2,1)S(1)}, bf16[8,2048]{1,0:T(8,128)(2,1)S(1)}, bf16[8,2048]{1,0:T(8,128)(2,1)S(1)}) custom-call(s32[1]{0:T(128)} %bitcast.41.t_ref, bf16[32,3072]{1,0:T(8,128)(2,1)S(1)} %collective-permute-done.7.x_ref, f32[1,8192]{1,0:T(1,128)S(1)} %bitcast.111, ...), custom_call_target="tpu_custom_call" | custom-call | flops 2147483648 | bytes 524288 | tf_op jit(solution)/shard_map/pallas_call | solution.py:753
  87.5 1.5 %collective-permute-start.10 = (bf16[8,2048]{1,0:T(8,128)(2,1)S(1)}, bf16[8,2048]{1,0:T(8,128)(2,1)S(1)}, u32[]{:S(2)}, u32[]{:S(2)}) collective-permute-start(bf16[8,2048]{1,0:T(8,128)(2,1)S(1)} %get-tuple-element.94), channel_id=1, source_target_pairs={{0,2},{1,3},{2,0},{3,1},{4,6},{5,7},{6,4},{7,5},{8,10},{9,11},{10,... | collective-permute-start | bytes 98312 | tf_op jit(solution)/shard_map/ppermute | solution.py:777
  88.9 1.6 %collective-permute-start.11 = (bf16[8,2048]{1,0:T(8,128)(2,1)S(1)}, bf16[8,2048]{1,0:T(8,128)(2,1)S(1)}, u32[]{:S(2)}, u32[]{:S(2)}) collective-permute-start(bf16[8,2048]{1,0:T(8,128)(2,1)S(1)} %get-tuple-element.95), channel_id=1, source_target_pairs={{0,3},{1,2},{2,1},{3,0},{4,7},{5,6},{6,5},{7,4},{8,11},{9,10},{10,... | collective-permute-start | bytes 98312 | tf_op jit(solution)/shard_map/ppermute | solution.py:777
  90.5 0.5 collective-permute-start.9
  91.0 0.5 slice.9
  92.2 0.4 collective-permute-done.10
  92.6 2.2 %collective-permute-done.11 = bf16[8,2048]{1,0:T(8,128)(2,1)S(1)} collective-permute-done((bf16[8,2048]{1,0:T(8,128)(2,1)S(1)}, bf16[8,2048]{1,0:T(8,128)(2,1)S(1)}, u32[]{:S(2)}, u32[]{:S(2)}) %collective-permute-start.11) | collective-permute-done | bytes 32800 | tf_op jit(solution)/shard_map/ppermute | solution.py:777
  94.8 0.0 collective-permute-done.9
  94.8 9.4 %all_gather.3 = f32[64,2048]{1,0:T(8,128)S(1)} all-gather(f32[8,2048]{1,0:T(8,128)S(1)} %convert_add_fusion), channel_id=1, replica_groups=mesh['group'=8,'tensor'=4] {'group'}, dimensions={0}, use_global_device_ids=true | all-gather | bytes 589824 | tf_op jit(solution)/shard_map/all_gather | solution.py:778
  104.3 0.0 copy-done.3
  104.3 0.0 copy-done.8
  104.3 0.0 copy-done.9
  104.3 0.0 copy-done.10
  104.3 0.0 copy-done.11
  104.3 1.6 %conditional.1 = ((f32[64,2048]{1,0:T(8,128)}, f32[64,2048]{1,0:T(8,128)})) conditional(s32[]{:T(128)} %bitcast.40, (s32[8,128]{1,0:T(8,128)S(1)}, f32[64,2048]{1,0:T(8,128)S(1)}) %tuple.16, (s32[16,1]{0,1:T(1,128)S(1)}, s32[16]{0:T(128)S(1)}, s32[1]{0:T(128)}, bf16[64,2,8192]{2,1,0:T(2,128)(2,1)S(1)}, s32[16,1]{0,1:T(1,128)S(1)}, ...), branch_computations={%region_0.1_spmd, %region_1.13_spmd} | conditional | flops 10908256256 | bytes 262613120 | solution.py:811
  104.3 1.4 %branch_0_fun.1 = (f32[64,2048]{1,0:T(8,128)}, f32[64,2048]{1,0:T(8,128)}) custom-call(s32[8,128]{1,0:T(8,128)S(1)} %get-tuple-element.28.plan, f32[64,2048]{1,0:T(8,128)S(1)} %get-tuple-element.29.pooled), custom_call_target="tpu_custom_call" | custom-call | tf_op jit(solution)/shard_map/cond/branch_0_fun/pallas_call | solution.py:782
  (5 shorter events, 0.0 us)
Async XLA Ops:
  0.6 35.1 %copy-start.2 = (bf16[64,2,8192]{2,1,0:T(2,128)(2,1)S(1)}, bf16[64,2,8192]{2,1,0:T(2,128)(2,1)}, u32[]{:S(2)}) copy-start(bf16[64,2,8192]{2,1,0:T(2,128)(2,1)} %left.3) | copy-start | bytes 6291460
  2.2 33.5 %copy-start.4 = (bf16[64,2,8192]{2,1,0:T(2,128)(2,1)S(1)}, bf16[64,2,8192]{2,1,0:T(2,128)(2,1)}, u32[]{:S(2)}) copy-start(bf16[64,2,8192]{2,1,0:T(2,128)(2,1)} %right.3) | copy-start | bytes 6291460
  2.3 1.3 %collective-permute-start = (s32[1,128]{1,0:T(1,128)S(1)}, s32[1,128]{1,0:T(1,128)S(1)}, u32[]{:S(2)}, u32[]{:S(2)}) collective-permute-start(s32[1,128]{1,0:T(1,128)S(1)} %compare_select_fusion.7), channel_id=1, source_target_pairs={{0,4},{4,0},{8,12},{12,8},{16,20},{20,16},{24,28},{28,24},{1,5},{5... | collective-permute-start | bytes 1544 | tf_op jit(solution)/shard_map/ppermute | solution.py:626
  3.6 4.4 %collective-permute-start.1 = (s32[1,128]{1,0:T(1,128)S(1)}, s32[1,128]{1,0:T(1,128)S(1)}, u32[]{:S(2)}, u32[]{:S(2)}) collective-permute-start(s32[1,128]{1,0:T(1,128)S(1)} %fusion.53), channel_id=1, source_target_pairs={{0,8},{4,12},{8,0},{12,4},{16,24},{20,28},{24,16},{28,20},{1,9},{5... | collective-permute-start | bytes 1544 | tf_op jit(solution)/shard_map/ppermute | solution.py:626
  8.0 3.6 %collective-permute-start.2 = (s32[1,128]{1,0:T(1,128)S(1)}, s32[1,128]{1,0:T(1,128)S(1)}, u32[]{:S(2)}, u32[]{:S(2)}) collective-permute-start(s32[1,128]{1,0:T(1,128)S(1)} %add.112.mine), channel_id=1, source_target_pairs={{0,16},{4,20},{8,24},{12,28},{16,0},{20,4},{24,8},{28,12},{1,17},{... | collective-permute-start | bytes 1544 | tf_op jit(solution)/shard_map/ppermute | solution.py:626
  15.7 29.9 %copy-start.7 = (f32[8192]{0:T(1024)S(1)}, f32[8192]{0:T(1024)}, u32[]{:S(2)}) copy-start(f32[8192]{0:T(1024)} %param.21) | copy-start | bytes 98308
  34.1 11.5 %collective-permute-start.3 = (bf16[32,5120]{1,0:T(8,128)(2,1)S(1)}, bf16[32,5120]{1,0:T(8,128)(2,1)S(1)}, u32[]{:S(2)}, u32[]{:S(2)}) collective-permute-start(bf16[32,5120]{1,0:T(8,128)(2,1)S(1)} %shard_map.137.refs_0_), channel_id=1, source_target_pairs={{0,1},{1,2},{2,3},{3,0},{4,5},{5,6},{6,7},{7,4},{8,9},{9,10},{10,1... | collective-permute-start | bytes 983048 | tf_op jit(solution)/shard_map/ppermute | solution.py:681
  39.0 12.9 %all-to-all-start.7 = ((bf16[40,2,3072]{2,1,0:T(2,128)(2,1)}), bf16[40,2,3072]{2,1,0:T(2,128)(2,1)S(1)}, u32[]{:S(2)}, u32[]{:S(2)}) async-start(bf16[40,2,3072]{2,1,0:T(2,128)(2,1)} %shard_map.136), calls=%async_computation.7 | async-start | bytes 983040 | tf_op jit(solution)/shard_map/all_to_all | solution.py:664
  45.6 10.6 %collective-permute-start.5 = (bf16[32,5120]{1,0:T(8,128)(2,1)S(1)}, bf16[32,5120]{1,0:T(8,128)(2,1)S(1)}, u32[]{:S(2)}, u32[]{:S(2)}) collective-permute-start(bf16[32,5120]{1,0:T(8,128)(2,1)S(1)} %collective-permute-done.3.refs_1_.refs_0_), channel_id=1, source_target_pairs={{0,1},{1,2},{2,3},{3,0},{4,5},{5,6},{6,7},{7,4},{8,9},{9,10},{10,1... | collective-permute-start | bytes 983048 | tf_op jit(solution)/shard_map/ppermute | solution.py:681
  53.2 9.7 %collective-permute-start.4 = (bf16[32,3072]{1,0:T(8,128)(2,1)S(1)}, bf16[32,3072]{1,0:T(8,128)(2,1)S(1)}, u32[]{:S(2)}, u32[]{:S(2)}) collective-permute-start(bf16[32,3072]{1,0:T(8,128)(2,1)S(1)} %shard_map.139.refs_6_.refs_0_), channel_id=1, source_target_pairs={{0,1},{1,2},{2,3},{3,0},{4,5},{5,6},{6,7},{7,4},{8,9},{9,10},{10,1... | collective-permute-start | bytes 589832 | tf_op jit(solution)/shard_map/ppermute | solution.py:681
  56.1 18.7 %collective-permute-start.8 = (bf16[32,5120]{1,0:T(8,128)(2,1)S(1)}, bf16[32,5120]{1,0:T(8,128)(2,1)S(1)}, u32[]{:S(2)}, u32[]{:S(2)}) collective-permute-start(bf16[32,5120]{1,0:T(8,128)(2,1)S(1)} %collective-permute-done.5.refs_1_), channel_id=1, source_target_pairs={{0,1},{1,2},{2,3},{3,0},{4,5},{5,6},{6,7},{7,4},{8,9},{9,10},{10,1... | collective-permute-start | bytes 983048 | tf_op jit(solution)/shard_map/ppermute | solution.py:681
  62.9 9.3 %collective-permute-start.6 = (bf16[32,3072]{1,0:T(8,128)(2,1)S(1)}, bf16[32,3072]{1,0:T(8,128)(2,1)S(1)}, u32[]{:S(2)}, u32[]{:S(2)}) collective-permute-start(bf16[32,3072]{1,0:T(8,128)(2,1)S(1)} %collective-permute-done.4.refs_7_.refs_0_), channel_id=1, source_target_pairs={{0,1},{1,2},{2,3},{3,0},{4,5},{5,6},{6,7},{7,4},{8,9},{9,10},{10,1... | collective-permute-start | bytes 589832 | tf_op jit(solution)/shard_map/ppermute | solution.py:681
  72.2 7.5 %collective-permute-start.7 = (bf16[32,3072]{1,0:T(8,128)(2,1)S(1)}, bf16[32,3072]{1,0:T(8,128)(2,1)S(1)}, u32[]{:S(2)}, u32[]{:S(2)}) collective-permute-start(bf16[32,3072]{1,0:T(8,128)(2,1)S(1)} %collective-permute-done.6.refs_1_), channel_id=1, source_target_pairs={{0,1},{1,2},{2,3},{3,0},{4,5},{5,6},{6,7},{7,4},{8,9},{9,10},{10,1... | collective-permute-start | bytes 589832 | tf_op jit(solution)/shard_map/ppermute | solution.py:681
  79.7 24.6 %copy-start.3 = (bf16[64,2,8192]{2,1,0:T(2,128)(2,1)S(1)}, bf16[64,2,8192]{2,1,0:T(2,128)(2,1)}, u32[]{:S(2)}) copy-start(bf16[64,2,8192]{2,1,0:T(2,128)(2,1)} %left.3) | copy-start | bytes 6291460
  79.7 24.6 %copy-start.8 = (s32[16,1]{0,1:T(1,128)S(1)}, s32[16,1]{0,1:T(1,128)}, u32[]{:S(2)}) copy-start(s32[16,1]{0,1:T(1,128)} %param.18) | copy-start | bytes 196
  79.7 24.6 %copy-start.9 = (s32[16,1]{0,1:T(1,128)S(1)}, s32[16,1]{0,1:T(1,128)}, u32[]{:S(2)}) copy-start(s32[16,1]{0,1:T(1,128)} %param.16) | copy-start | bytes 196
  79.7 24.6 %copy-start.10 = (s32[16]{0:T(128)S(1)}, s32[16]{0:T(128)}, u32[]{:S(2)}) copy-start(s32[16]{0:T(128)} %param.19) | copy-start | bytes 196
  79.7 24.6 %copy-start.11 = (s32[16]{0:T(128)S(1)}, s32[16]{0:T(128)}, u32[]{:S(2)}) copy-start(s32[16]{0:T(128)} %param.17) | copy-start | bytes 196
  87.5 5.1 %collective-permute-start.10 = (bf16[8,2048]{1,0:T(8,128)(2,1)S(1)}, bf16[8,2048]{1,0:T(8,128)(2,1)S(1)}, u32[]{:S(2)}, u32[]{:S(2)}) collective-permute-start(bf16[8,2048]{1,0:T(8,128)(2,1)S(1)} %get-tuple-element.94), channel_id=1, source_target_pairs={{0,2},{1,3},{2,0},{3,1},{4,6},{5,7},{6,4},{7,5},{8,10},{9,11},{10,... | collective-permute-start | bytes 98312 | tf_op jit(solution)/shard_map/ppermute | solution.py:777
  88.9 5.8 %collective-permute-start.11 = (bf16[8,2048]{1,0:T(8,128)(2,1)S(1)}, bf16[8,2048]{1,0:T(8,128)(2,1)S(1)}, u32[]{:S(2)}, u32[]{:S(2)}) collective-permute-start(bf16[8,2048]{1,0:T(8,128)(2,1)S(1)} %get-tuple-element.95), channel_id=1, source_target_pairs={{0,3},{1,2},{2,1},{3,0},{4,7},{5,6},{6,5},{7,4},{8,11},{9,10},{10,... | collective-permute-start | bytes 98312 | tf_op jit(solution)/shard_map/ppermute | solution.py:777
  90.5 4.3 %collective-permute-start.9 = (bf16[8,2048]{1,0:T(8,128)(2,1)S(1)}, bf16[8,2048]{1,0:T(8,128)(2,1)S(1)}, u32[]{:S(2)}, u32[]{:S(2)}) collective-permute-start(bf16[8,2048]{1,0:T(8,128)(2,1)S(1)} %get-tuple-element.93), channel_id=1, source_target_pairs={{0,1},{1,0},{2,3},{3,2},{4,5},{5,4},{6,7},{7,6},{8,9},{9,8},{10,11... | collective-permute-start | bytes 98312 | tf_op jit(solution)/shard_map/ppermute | solution.py:777
